TPU v7x, 128 devices: a whole 4x4x4 slice. The times are simulated.
128 devices in a mesh: gx: 8 (over y, core), gy: 16 (over z, x).
Axes of the slice: x: 4, y: 4, z: 4, core: 2. Of those that a mesh axis runs over, the one named last changes fastest.
Arguments:
- embeddings: bfloat16 [1024, 128, 1024], P(('gx', 'gy')), may hold values from -120 to 120
- block_cluster: int32 [1024], P(('gx', 'gy')), may hold values from 0 to 1023, as said below
- block_rows: int32 [1024], P(('gx', 'gy')), may hold values from 1 to 128
Outputs:
- best: float32 [1024, 128], P(('gx', 'gy'))
Inputs may be any that keep to these rules, and one draw needn't show every extreme that they name: `block_cluster`: ids never fall along the blocks, so the blocks of one cluster are consecutive; one cluster holds at most 57 blocks, and some cluster holds exactly 57.
All inputs are finite; a program needn't handle non-finite values.
Results may differ from a plain program's by a relative error of at most 0.00055.
Values may be sent and summed in bfloat16 or wider, within the bound.
No kernel may reach another device: no remote copies, remote signals or barrier semaphores. Data moves between devices by JAX's collectives and lax.ppermute only.
A program may use at most 128 MiB of HBM per device.

v0:
```python
import jax
import jax.numpy as jnp
from jax import lax
from jax.sharding import PartitionSpec as P

REACH = 8


epsilon = 1e-06


def passed_along(array, axis, by):
    count = lax.axis_size(axis)
    pairs = [(i, i + by) for i in range(count) if 0 <= i + by < count]
    return lax.ppermute(array, axis, pairs)


def normalize(embeddings):
    values = embeddings.astype(jnp.float32)
    factor = lax.rsqrt(jnp.sum(values * values, axis=-1, keepdims=True) + epsilon)
    return (values * factor).astype(jnp.bfloat16)


def flat_tags(cluster, row_live, row_count):
    position = lax.broadcasted_iota(jnp.int32, (cluster.shape[0], row_count), 1)
    tagged = jnp.broadcast_to(cluster[:, None], (cluster.shape[0], row_count)).reshape(-1)
    usable = (position < row_live[:, None]).reshape(-1)
    return (tagged, usable)


def compare(own_units, own_info, other_units, other_info, itself):
    row_count = own_units.shape[1]
    own_flat = own_units.reshape(-1, own_units.shape[2])
    other_flat = other_units.reshape(-1, other_units.shape[2])
    similar = lax.dot_general(
        own_flat, other_flat, (((1,), (1,)), ((), ())), preferred_element_type=jnp.float32
    )
    own_tagged, own_usable = flat_tags(own_info[0], own_info[1], row_count)
    other_tagged, other_usable = flat_tags(other_info[0], other_info[1], row_count)
    allowed = (
        (own_tagged[:, None] == other_tagged[None, :]) & own_usable[:, None] & other_usable[None, :]
    )
    if itself:
        allowed = allowed & (
            lax.broadcasted_iota(jnp.int32, similar.shape, 0)
            != lax.broadcasted_iota(jnp.int32, similar.shape, 1)
        )
    levels = jnp.where(allowed, similar + 1.0, 0.0)
    rows_best = jnp.max(levels, axis=1).reshape(own_units.shape[0], row_count)
    columns_best = jnp.max(levels, axis=0).reshape(other_units.shape[0], row_count)
    return (rows_best, columns_best)


def tile_pass(own_units, own_info, other_units, other_info, itself):
    return compare(own_units, own_info, other_units, other_info, itself)


def body(embeddings, block_cluster, block_rows):
    units = normalize(embeddings)
    own_blocks = units.shape[0]
    own_info = (block_cluster, block_rows)
    row_best, unused = tile_pass(units, own_info, units, own_info, True)
    for offset in range(1, REACH):
        incoming, other_cluster, other_rows = passed_along(
            (units, block_cluster, block_rows), ("gx", "gy"), -offset
        )
        rows_part, columns_part = tile_pass(
            units, own_info, incoming, (other_cluster, other_rows), False
        )
        returned = passed_along(columns_part, ("gx", "gy"), offset)
        row_best = jnp.maximum(row_best, jnp.maximum(rows_part, returned))
    position = lax.broadcasted_iota(jnp.int32, (own_blocks, units.shape[1]), 1)
    usable = position < block_rows[:, None]
    return jnp.where(usable, row_best - 1.0, 0.0)


def solution(mesh):
    placed = (P(("gx", "gy"), None, None), P(("gx", "gy")), P(("gx", "gy")))
    return jax.shard_map(
        body, mesh=mesh, in_specs=placed, out_specs=P(("gx", "gy"), None), check_vma=False
    )
```

profile of v0, /device:TPU:11, one launch (start us, length us, event | category | flops | bytes accessed | tf_op | source)
XLA Modules:
  0.0 483.7 jit_solution(6338161833339647005)
XLA Ops:
  0.0 2.2 fusion
  2.7 7.8 %collective-permute-start.6 = (bf16[8,128,1024]{2,1,0:T(8,128)(2,1)S(1)}, bf16[8,128,1024]{2,1,0:T(8,128)(2,1)S(1)}, u32[]{:S(2)}, u32[]{:S(2)}) collective-permute-start(bf16[8,128,1024]{2,1,0:T(8,128)(2,1)S(1)} %fusion.1), channel_id=1, source_target_pairs={{2,0},{3,1},{4,2},{5,3},{6,4},{7,5},{8,6},{9,7},{10,8},{11,9},{12,... | collective-permute-start | bytes 6291464 | tf_op jit(solution)/shard_map/ppermute | solution.py:15
  10.5 1.9 collective-permute-start.10
  12.4 2.3 collective-permute-start.14
  14.7 3.0 collective-permute-start.18
  17.8 8.0 %collective-permute-start.16 = (s32[8]{0:T(128)S(1)}, s32[8]{0:T(128)S(1)}, u32[]{:S(2)}, u32[]{:S(2)}) collective-permute-start(s32[8]{0:T(128)S(1)} %copy-done.2), channel_id=1, source_target_pairs={{5,0},{6,1},{7,2},{8,3},{9,4},{10,5},{11,6},{12,7},{13,8},{14,9},{... | collective-permute-start | bytes 104 | tf_op jit(solution)/shard_map/ppermute | solution.py:15
  25.9 117.4 %collective-permute-done.16 = s32[8]{0:T(128)S(1)} collective-permute-done((s32[8]{0:T(128)S(1)}, s32[8]{0:T(128)S(1)}, u32[]{:S(2)}, u32[]{:S(2)}) %collective-permute-start.16) | collective-permute-done | bytes 64 | tf_op jit(solution)/shard_map/ppermute | solution.py:15
  143.3 1.9 collective-permute-start.1
  145.2 2.6 collective-permute-done.1
  147.8 16.3 %collective-permute-start.5 = (s32[8]{0:T(128)S(1)}, s32[8]{0:T(128)S(1)}, u32[]{:S(2)}, u32[]{:S(2)}) collective-permute-start(s32[8]{0:T(128)S(1)} %copy-done.1), channel_id=1, source_target_pairs={{2,0},{3,1},{4,2},{5,3},{6,4},{7,5},{8,6},{9,7},{10,8},{11,9},{12,... | collective-permute-start | bytes 104 | tf_op jit(solution)/shard_map/ppermute | solution.py:15
  164.9 8.6 %collective-permute-start.9 = (s32[8]{0:T(128)S(1)}, s32[8]{0:T(128)S(1)}, u32[]{:S(2)}, u32[]{:S(2)}) collective-permute-start(s32[8]{0:T(128)S(1)} %copy-done.1), channel_id=1, source_target_pairs={{3,0},{4,1},{5,2},{6,3},{7,4},{8,5},{9,6},{10,7},{11,8},{12,9},{13... | collective-permute-start | bytes 104 | tf_op jit(solution)/shard_map/ppermute | solution.py:15
  174.2 3.2 collective-permute-start.13
  177.5 1.0 collective-permute-done.13
  178.4 5.0 %collective-permute-start.12 = (s32[8]{0:T(128)S(1)}, s32[8]{0:T(128)S(1)}, u32[]{:S(2)}, u32[]{:S(2)}) collective-permute-start(s32[8]{0:T(128)S(1)} %copy-done.2), channel_id=1, source_target_pairs={{4,0},{5,1},{6,2},{7,3},{8,4},{9,5},{10,6},{11,7},{12,8},{13,9},{1... | collective-permute-start | bytes 104 | tf_op jit(solution)/shard_map/ppermute | solution.py:15
  184.1 20.6 %collective-permute-start.8 = (s32[8]{0:T(128)S(1)}, s32[8]{0:T(128)S(1)}, u32[]{:S(2)}, u32[]{:S(2)}) collective-permute-start(s32[8]{0:T(128)S(1)} %copy-done.2), channel_id=1, source_target_pairs={{3,0},{4,1},{5,2},{6,3},{7,4},{8,5},{9,6},{10,7},{11,8},{12,9},{13... | collective-permute-start | bytes 104 | tf_op jit(solution)/shard_map/ppermute | solution.py:15
  204.8 0.6 collective-permute-done.8
  205.4 4.5 collective-permute-start.17
  210.0 0.6 collective-permute-done.17
  210.6 10.1 %collective-permute-start.4 = (s32[8]{0:T(128)S(1)}, s32[8]{0:T(128)S(1)}, u32[]{:S(2)}, u32[]{:S(2)}) collective-permute-start(s32[8]{0:T(128)S(1)} %copy-done.2), channel_id=1, source_target_pairs={{2,0},{3,1},{4,2},{5,3},{6,4},{7,5},{8,6},{9,7},{10,8},{11,9},{12,... | collective-permute-start | bytes 104 | tf_op jit(solution)/shard_map/ppermute | solution.py:15
  221.5 5.3 %collective-permute-start.21 = (s32[8]{0:T(128)S(1)}, s32[8]{0:T(128)S(1)}, u32[]{:S(2)}, u32[]{:S(2)}) collective-permute-start(s32[8]{0:T(128)S(1)} %copy-done.1), channel_id=1, source_target_pairs={{6,0},{7,1},{8,2},{9,3},{10,4},{11,5},{12,6},{13,7},{14,8},{15,9},... | collective-permute-start | bytes 104 | tf_op jit(solution)/shard_map/ppermute | solution.py:15
  226.8 1.3 collective-permute-done.21
  228.2 1.9 collective-permute-start
  230.1 2.3 collective-permute-done
  232.4 7.1 %collective-permute-start.24 = (s32[8]{0:T(128)S(1)}, s32[8]{0:T(128)S(1)}, u32[]{:S(2)}, u32[]{:S(2)}) collective-permute-start(s32[8]{0:T(128)S(1)} %copy-done.2), channel_id=1, source_target_pairs={{7,0},{8,1},{9,2},{10,3},{11,4},{12,5},{13,6},{14,7},{15,8},{16,9}... | collective-permute-start | bytes 104 | tf_op jit(solution)/shard_map/ppermute | solution.py:15
  240.2 6.5 %collective-permute-start.25 = (s32[8]{0:T(128)S(1)}, s32[8]{0:T(128)S(1)}, u32[]{:S(2)}, u32[]{:S(2)}) collective-permute-start(s32[8]{0:T(128)S(1)} %copy-done.1), channel_id=1, source_target_pairs={{7,0},{8,1},{9,2},{10,3},{11,4},{12,5},{13,6},{14,7},{15,8},{16,9}... | collective-permute-start | bytes 104 | tf_op jit(solution)/shard_map/ppermute | solution.py:15
  246.8 5.5 %collective-permute-done.25 = s32[8]{0:T(128)S(1)} collective-permute-done((s32[8]{0:T(128)S(1)}, s32[8]{0:T(128)S(1)}, u32[]{:S(2)}, u32[]{:S(2)}) %collective-permute-start.25) | collective-permute-done | bytes 64 | tf_op jit(solution)/shard_map/ppermute | solution.py:15
  252.4 5.2 %collective-permute-start.20 = (s32[8]{0:T(128)S(1)}, s32[8]{0:T(128)S(1)}, u32[]{:S(2)}, u32[]{:S(2)}) collective-permute-start(s32[8]{0:T(128)S(1)} %copy-done.2), channel_id=1, source_target_pairs={{6,0},{7,1},{8,2},{9,3},{10,4},{11,5},{12,6},{13,7},{14,8},{15,9},... | collective-permute-start | bytes 104 | tf_op jit(solution)/shard_map/ppermute | solution.py:15
  257.6 1.4 collective-permute-done.20
  259.0 2.1 collective-permute-start.2
  261.3 7.7 %collective-permute-start.26 = (bf16[8,128,1024]{2,1,0:T(8,128)(2,1)S(1)}, bf16[8,128,1024]{2,1,0:T(8,128)(2,1)S(1)}, u32[]{:S(2)}, u32[]{:S(2)}) collective-permute-start(bf16[8,128,1024]{2,1,0:T(8,128)(2,1)S(1)} %fusion.1), channel_id=1, source_target_pairs={{7,0},{8,1},{9,2},{10,3},{11,4},{12,5},{13,6},{14,7},{15,8},{16,9}... | collective-permute-start | bytes 6291464 | tf_op jit(solution)/shard_map/ppermute | solution.py:15
  269.0 2.4 fusion.34
  271.4 4.8 collective-permute-start.22
  276.2 2.4 fusion.35
  278.5 2.4 fusion.36
  281.0 2.4 fusion.37
  283.4 24.7 %collective-permute-done.2 = bf16[8,128,1024]{2,1,0:T(8,128)(2,1)S(1)} collective-permute-done((bf16[8,128,1024]{2,1,0:T(8,128)(2,1)S(1)}, bf16[8,128,1024]{2,1,0:T(8,128)(2,1)S(1)}, u32[]{:S(2)}, u32[]{:S(2)}) %collective-permute-start.2) | collective-permute-done | bytes 2097184 | tf_op jit(solution)/shard_map/ppermute | solution.py:15
  308.1 8.5 %fusion.4 = (f32[1024]{0:T(1024)S(1)}, f32[1024]{0:T(1024)S(1)}, f32[1024]{0:T(1024)S(1)}, f32[1024]{0:T(1024)S(1)}, f32[1024]{0:T(1024)S(1)}, /*index=5*/f32[10...) fusion(s32[1024]{0:T(1024)S(1)} %broadcast_bitcast_fusion.7, ...), kind=kOutput, calls=%fused_computation.15 | convolution fusion | flops 2184173568 | bytes 21043200 | tf_op jit(solution)/shard_map/dot_general | solution.py:35
  316.7 105.5 %collective-permute-start.11 = (f32[8,128]{1,0:T(8,128)S(1)}, f32[8,128]{1,0:T(8,128)S(1)}, u32[]{:S(2)}, u32[]{:S(2)}) collective-permute-start(f32[8,128]{1,0:T(8,128)S(1)} %bitcast.128), channel_id=1, source_target_pairs={{0,3},{1,4},{2,5},{3,6},{4,7},{5,8},{6,9},{7,10},{8,11},{9,12},{10... | collective-permute-start | bytes 12296 | tf_op jit(solution)/shard_map/ppermute | solution.py:15
  422.1 1.9 collective-permute-start.15
  424.1 1.9 collective-permute-start.19
  426.0 8.5 %collective-permute-start.3 = (f32[8,128]{1,0:T(8,128)S(1)}, f32[8,128]{1,0:T(8,128)S(1)}, u32[]{:S(2)}, u32[]{:S(2)}) collective-permute-start(f32[8,128]{1,0:T(8,128)S(1)} %bitcast.125), channel_id=1, source_target_pairs={{0,1},{1,2},{2,3},{3,4},{4,5},{5,6},{6,7},{7,8},{8,9},{9,10},{10,1... | collective-permute-start | bytes 12296 | tf_op jit(solution)/shard_map/ppermute | solution.py:15
  434.5 2.4 fusion.38
  436.9 4.6 collective-permute-start.7
  441.5 4.9 %fusion.14 = (f32[1024]{0:T(1024)S(1)}, f32[1024]{0:T(1024)S(1)}, f32[1024]{0:T(1024)S(1)}, f32[1024]{0:T(1024)S(1)}) fusion(s32[1024]{0:T(1024)S(1)} %broadcast_bitcast_fusion.7, s32[1024]{0:T(1024)S(1)} %broadcast_bitcast_fusion.1, pred[1024]{0:T(1024)(128)(4,1)S(1)} %fusion.32, pred[1024]{0:T(1024)(128)(4,1)S(1)} %fusion.26, ...), kind=kOutput, calls=%fused_computation.25 | convolution fusion | flops 2162159616 | bytes 8420352 | tf_op jit(solution)/shard_map/dot_general | solution.py:35
  446.4 9.0 %collective-permute-start.23 = (f32[8,128]{1,0:T(8,128)S(1)}, f32[8,128]{1,0:T(8,128)S(1)}, u32[]{:S(2)}, u32[]{:S(2)}) collective-permute-start(f32[8,128]{1,0:T(8,128)S(1)} %bitcast.130), channel_id=1, source_target_pairs={{0,6},{1,7},{2,8},{3,9},{4,10},{5,11},{6,12},{7,13},{8,14},{9,15},... | collective-permute-start | bytes 12296 | tf_op jit(solution)/shard_map/ppermute | solution.py:15
  455.4 23.9 %collective-permute-start.27 = (f32[8,128]{1,0:T(8,128)S(1)}, f32[8,128]{1,0:T(8,128)S(1)}, u32[]{:S(2)}, u32[]{:S(2)}) collective-permute-start(f32[8,128]{1,0:T(8,128)S(1)} %bitcast.129), channel_id=1, source_target_pairs={{0,7},{1,8},{2,9},{3,10},{4,11},{5,12},{6,13},{7,14},{8,15},{9,16}... | collective-permute-start | bytes 12296 | tf_op jit(solution)/shard_map/ppermute | solution.py:15
  479.3 3.7 select_reduce_fusion
  483.1 0.7 fusion.19
  (42 shorter events, 4.7 us)
Async XLA Ops:
  0.0 2.2 copy-start
  2.2 15.5 %copy-start.2 = (s32[8]{0:T(128)S(1)}, s32[8]{0:T(128)}, u32[]{:S(2)}) copy-start(s32[8]{0:T(128)} %param.4) | copy-start | bytes 100
  2.3 23.5 %copy-start.1 = (s32[8]{0:T(128)S(1)}, s32[8]{0:T(128)}, u32[]{:S(2)}) copy-start(s32[8]{0:T(128)} %param.5) | copy-start | bytes 100
  2.7 258.6 %collective-permute-start.6 = (bf16[8,128,1024]{2,1,0:T(8,128)(2,1)S(1)}, bf16[8,128,1024]{2,1,0:T(8,128)(2,1)S(1)}, u32[]{:S(2)}, u32[]{:S(2)}) collective-permute-start(bf16[8,128,1024]{2,1,0:T(8,128)(2,1)S(1)} %fusion.1), channel_id=1, source_target_pairs={{2,0},{3,1},{4,2},{5,3},{6,4},{7,5},{8,6},{9,7},{10,8},{11,9},{12,... | collective-permute-start | bytes 6291464 | tf_op jit(solution)/shard_map/ppermute | solution.py:15
  10.5 260.9 %collective-permute-start.10 = (bf16[8,128,1024]{2,1,0:T(8,128)(2,1)S(1)}, bf16[8,128,1024]{2,1,0:T(8,128)(2,1)S(1)}, u32[]{:S(2)}, u32[]{:S(2)}) collective-permute-start(bf16[8,128,1024]{2,1,0:T(8,128)(2,1)S(1)} %fusion.1), channel_id=1, source_target_pairs={{3,0},{4,1},{5,2},{6,3},{7,4},{8,5},{9,6},{10,7},{11,8},{12,9},{13... | collective-permute-start | bytes 6291464 | tf_op jit(solution)/shard_map/ppermute | solution.py:15
  12.4 266.1 %collective-permute-start.14 = (bf16[8,128,1024]{2,1,0:T(8,128)(2,1)S(1)}, bf16[8,128,1024]{2,1,0:T(8,128)(2,1)S(1)}, u32[]{:S(2)}, u32[]{:S(2)}) collective-permute-start(bf16[8,128,1024]{2,1,0:T(8,128)(2,1)S(1)} %fusion.1), channel_id=1, source_target_pairs={{4,0},{5,1},{6,2},{7,3},{8,4},{9,5},{10,6},{11,7},{12,8},{13,9},{1... | collective-permute-start | bytes 6291464 | tf_op jit(solution)/shard_map/ppermute | solution.py:15
  14.7 266.3 %collective-permute-start.18 = (bf16[8,128,1024]{2,1,0:T(8,128)(2,1)S(1)}, bf16[8,128,1024]{2,1,0:T(8,128)(2,1)S(1)}, u32[]{:S(2)}, u32[]{:S(2)}) collective-permute-start(bf16[8,128,1024]{2,1,0:T(8,128)(2,1)S(1)} %fusion.1), channel_id=1, source_target_pairs={{5,0},{6,1},{7,2},{8,3},{9,4},{10,5},{11,6},{12,7},{13,8},{14,9},{... | collective-permute-start | bytes 6291464 | tf_op jit(solution)/shard_map/ppermute | solution.py:15
  17.8 125.5 %collective-permute-start.16 = (s32[8]{0:T(128)S(1)}, s32[8]{0:T(128)S(1)}, u32[]{:S(2)}, u32[]{:S(2)}) collective-permute-start(s32[8]{0:T(128)S(1)} %copy-done.2), channel_id=1, source_target_pairs={{5,0},{6,1},{7,2},{8,3},{9,4},{10,5},{11,6},{12,7},{13,8},{14,9},{... | collective-permute-start | bytes 104 | tf_op jit(solution)/shard_map/ppermute | solution.py:15
  143.3 4.6 collective-permute-start.1
  147.8 17.0 %collective-permute-start.5 = (s32[8]{0:T(128)S(1)}, s32[8]{0:T(128)S(1)}, u32[]{:S(2)}, u32[]{:S(2)}) collective-permute-start(s32[8]{0:T(128)S(1)} %copy-done.1), channel_id=1, source_target_pairs={{2,0},{3,1},{4,2},{5,3},{6,4},{7,5},{8,6},{9,7},{10,8},{11,9},{12,... | collective-permute-start | bytes 104 | tf_op jit(solution)/shard_map/ppermute | solution.py:15
  164.9 9.3 %collective-permute-start.9 = (s32[8]{0:T(128)S(1)}, s32[8]{0:T(128)S(1)}, u32[]{:S(2)}, u32[]{:S(2)}) collective-permute-start(s32[8]{0:T(128)S(1)} %copy-done.1), channel_id=1, source_target_pairs={{3,0},{4,1},{5,2},{6,3},{7,4},{8,5},{9,6},{10,7},{11,8},{12,9},{13... | collective-permute-start | bytes 104 | tf_op jit(solution)/shard_map/ppermute | solution.py:15
  174.2 4.3 collective-permute-start.13
  178.4 5.7 %collective-permute-start.12 = (s32[8]{0:T(128)S(1)}, s32[8]{0:T(128)S(1)}, u32[]{:S(2)}, u32[]{:S(2)}) collective-permute-start(s32[8]{0:T(128)S(1)} %copy-done.2), channel_id=1, source_target_pairs={{4,0},{5,1},{6,2},{7,3},{8,4},{9,5},{10,6},{11,7},{12,8},{13,9},{1... | collective-permute-start | bytes 104 | tf_op jit(solution)/shard_map/ppermute | solution.py:15
  184.1 21.3 %collective-permute-start.8 = (s32[8]{0:T(128)S(1)}, s32[8]{0:T(128)S(1)}, u32[]{:S(2)}, u32[]{:S(2)}) collective-permute-start(s32[8]{0:T(128)S(1)} %copy-done.2), channel_id=1, source_target_pairs={{3,0},{4,1},{5,2},{6,3},{7,4},{8,5},{9,6},{10,7},{11,8},{12,9},{13... | collective-permute-start | bytes 104 | tf_op jit(solution)/shard_map/ppermute | solution.py:15
  205.4 5.2 %collective-permute-start.17 = (s32[8]{0:T(128)S(1)}, s32[8]{0:T(128)S(1)}, u32[]{:S(2)}, u32[]{:S(2)}) collective-permute-start(s32[8]{0:T(128)S(1)} %copy-done.1), channel_id=1, source_target_pairs={{5,0},{6,1},{7,2},{8,3},{9,4},{10,5},{11,6},{12,7},{13,8},{14,9},{... | collective-permute-start | bytes 104 | tf_op jit(solution)/shard_map/ppermute | solution.py:15
  210.6 10.8 %collective-permute-start.4 = (s32[8]{0:T(128)S(1)}, s32[8]{0:T(128)S(1)}, u32[]{:S(2)}, u32[]{:S(2)}) collective-permute-start(s32[8]{0:T(128)S(1)} %copy-done.2), channel_id=1, source_target_pairs={{2,0},{3,1},{4,2},{5,3},{6,4},{7,5},{8,6},{9,7},{10,8},{11,9},{12,... | collective-permute-start | bytes 104 | tf_op jit(solution)/shard_map/ppermute | solution.py:15
  221.5 6.7 %collective-permute-start.21 = (s32[8]{0:T(128)S(1)}, s32[8]{0:T(128)S(1)}, u32[]{:S(2)}, u32[]{:S(2)}) collective-permute-start(s32[8]{0:T(128)S(1)} %copy-done.1), channel_id=1, source_target_pairs={{6,0},{7,1},{8,2},{9,3},{10,4},{11,5},{12,6},{13,7},{14,8},{15,9},... | collective-permute-start | bytes 104 | tf_op jit(solution)/shard_map/ppermute | solution.py:15
  228.2 4.3 collective-permute-start
  232.4 7.8 %collective-permute-start.24 = (s32[8]{0:T(128)S(1)}, s32[8]{0:T(128)S(1)}, u32[]{:S(2)}, u32[]{:S(2)}) collective-permute-start(s32[8]{0:T(128)S(1)} %copy-done.2), channel_id=1, source_target_pairs={{7,0},{8,1},{9,2},{10,3},{11,4},{12,5},{13,6},{14,7},{15,8},{16,9}... | collective-permute-start | bytes 104 | tf_op jit(solution)/shard_map/ppermute | solution.py:15
  240.2 12.2 %collective-permute-start.25 = (s32[8]{0:T(128)S(1)}, s32[8]{0:T(128)S(1)}, u32[]{:S(2)}, u32[]{:S(2)}) collective-permute-start(s32[8]{0:T(128)S(1)} %copy-done.1), channel_id=1, source_target_pairs={{7,0},{8,1},{9,2},{10,3},{11,4},{12,5},{13,6},{14,7},{15,8},{16,9}... | collective-permute-start | bytes 104 | tf_op jit(solution)/shard_map/ppermute | solution.py:15
  252.4 6.7 %collective-permute-start.20 = (s32[8]{0:T(128)S(1)}, s32[8]{0:T(128)S(1)}, u32[]{:S(2)}, u32[]{:S(2)}) collective-permute-start(s32[8]{0:T(128)S(1)} %copy-done.2), channel_id=1, source_target_pairs={{6,0},{7,1},{8,2},{9,3},{10,4},{11,5},{12,6},{13,7},{14,8},{15,9},... | collective-permute-start | bytes 104 | tf_op jit(solution)/shard_map/ppermute | solution.py:15
  259.0 49.1 %collective-permute-start.2 = (bf16[8,128,1024]{2,1,0:T(8,128)(2,1)S(1)}, bf16[8,128,1024]{2,1,0:T(8,128)(2,1)S(1)}, u32[]{:S(2)}, u32[]{:S(2)}) collective-permute-start(bf16[8,128,1024]{2,1,0:T(8,128)(2,1)S(1)} %fusion.1), channel_id=1, source_target_pairs={{1,0},{2,1},{3,2},{4,3},{5,4},{6,5},{7,6},{8,7},{9,8},{10,9},{11,1... | collective-permute-start | bytes 6291464 | tf_op jit(solution)/shard_map/ppermute | solution.py:15
  261.3 164.7 %collective-permute-start.26 = (bf16[8,128,1024]{2,1,0:T(8,128)(2,1)S(1)}, bf16[8,128,1024]{2,1,0:T(8,128)(2,1)S(1)}, u32[]{:S(2)}, u32[]{:S(2)}) collective-permute-start(bf16[8,128,1024]{2,1,0:T(8,128)(2,1)S(1)} %fusion.1), channel_id=1, source_target_pairs={{7,0},{8,1},{9,2},{10,3},{11,4},{12,5},{13,6},{14,7},{15,8},{16,9}... | collective-permute-start | bytes 6291464 | tf_op jit(solution)/shard_map/ppermute | solution.py:15
  271.4 165.5 %collective-permute-start.22 = (bf16[8,128,1024]{2,1,0:T(8,128)(2,1)S(1)}, bf16[8,128,1024]{2,1,0:T(8,128)(2,1)S(1)}, u32[]{:S(2)}, u32[]{:S(2)}) collective-permute-start(bf16[8,128,1024]{2,1,0:T(8,128)(2,1)S(1)} %fusion.1), channel_id=1, source_target_pairs={{6,0},{7,1},{8,2},{9,3},{10,4},{11,5},{12,6},{13,7},{14,8},{15,9},... | collective-permute-start | bytes 6291464 | tf_op jit(solution)/shard_map/ppermute | solution.py:15
  316.7 129.7 %collective-permute-start.11 = (f32[8,128]{1,0:T(8,128)S(1)}, f32[8,128]{1,0:T(8,128)S(1)}, u32[]{:S(2)}, u32[]{:S(2)}) collective-permute-start(f32[8,128]{1,0:T(8,128)S(1)} %bitcast.128), channel_id=1, source_target_pairs={{0,3},{1,4},{2,5},{3,6},{4,7},{5,8},{6,9},{7,10},{8,11},{9,12},{10... | collective-permute-start | bytes 12296 | tf_op jit(solution)/shard_map/ppermute | solution.py:15
  422.1 33.3 %collective-permute-start.15 = (f32[8,128]{1,0:T(8,128)S(1)}, f32[8,128]{1,0:T(8,128)S(1)}, u32[]{:S(2)}, u32[]{:S(2)}) collective-permute-start(f32[8,128]{1,0:T(8,128)S(1)} %bitcast.127), channel_id=1, source_target_pairs={{0,4},{1,5},{2,6},{3,7},{4,8},{5,9},{6,10},{7,11},{8,12},{9,13},{1... | collective-permute-start | bytes 12296 | tf_op jit(solution)/shard_map/ppermute | solution.py:15
  424.1 58.9 %collective-permute-start.19 = (f32[8,128]{1,0:T(8,128)S(1)}, f32[8,128]{1,0:T(8,128)S(1)}, u32[]{:S(2)}, u32[]{:S(2)}) collective-permute-start(f32[8,128]{1,0:T(8,128)S(1)} %bitcast.126), channel_id=1, source_target_pairs={{0,5},{1,6},{2,7},{3,8},{4,9},{5,10},{6,11},{7,12},{8,13},{9,14},{... | collective-permute-start | bytes 12296 | tf_op jit(solution)/shard_map/ppermute | solution.py:15
  426.0 57.0 %collective-permute-start.3 = (f32[8,128]{1,0:T(8,128)S(1)}, f32[8,128]{1,0:T(8,128)S(1)}, u32[]{:S(2)}, u32[]{:S(2)}) collective-permute-start(f32[8,128]{1,0:T(8,128)S(1)} %bitcast.125), channel_id=1, source_target_pairs={{0,1},{1,2},{2,3},{3,4},{4,5},{5,6},{6,7},{7,8},{8,9},{9,10},{10,1... | collective-permute-start | bytes 12296 | tf_op jit(solution)/shard_map/ppermute | solution.py:15
  436.9 46.1 %collective-permute-start.7 = (f32[8,128]{1,0:T(8,128)S(1)}, f32[8,128]{1,0:T(8,128)S(1)}, u32[]{:S(2)}, u32[]{:S(2)}) collective-permute-start(f32[8,128]{1,0:T(8,128)S(1)} %bitcast.124), channel_id=1, source_target_pairs={{0,2},{1,3},{2,4},{3,5},{4,6},{5,7},{6,8},{7,9},{8,10},{9,11},{10,... | collective-permute-start | bytes 12296 | tf_op jit(solution)/shard_map/ppermute | solution.py:15
  446.4 36.6 %collective-permute-start.23 = (f32[8,128]{1,0:T(8,128)S(1)}, f32[8,128]{1,0:T(8,128)S(1)}, u32[]{:S(2)}, u32[]{:S(2)}) collective-permute-start(f32[8,128]{1,0:T(8,128)S(1)} %bitcast.130), channel_id=1, source_target_pairs={{0,6},{1,7},{2,8},{3,9},{4,10},{5,11},{6,12},{7,13},{8,14},{9,15},... | collective-permute-start | bytes 12296 | tf_op jit(solution)/shard_map/ppermute | solution.py:15
  455.4 27.6 %collective-permute-start.27 = (f32[8,128]{1,0:T(8,128)S(1)}, f32[8,128]{1,0:T(8,128)S(1)}, u32[]{:S(2)}, u32[]{:S(2)}) collective-permute-start(f32[8,128]{1,0:T(8,128)S(1)} %bitcast.129), channel_id=1, source_target_pairs={{0,7},{1,8},{2,9},{3,10},{4,11},{5,12},{6,13},{7,14},{8,15},{9,16}... | collective-permute-start | bytes 12296 | tf_op jit(solution)/shard_map/ppermute | solution.py:15
where the time goes:
time: 485 us; the launch traced here: 484 us
  starting transfers between devices  289 us (60%)
  waiting for transfers between devices  161 us (33%)
  matrix products  29.1 us (6%)
    ppermute x28, starting transfers between devices, passed_along(): return lax.ppermute(array, axis, pairs)  289 us
    ppermute x28, waiting for transfers between devices, passed_along(): return lax.ppermute(array, axis, pairs)  161 us
    dot_general x8, matrix products, compare(): lax.dot_general(own_flat, other_flat, (((1,), (1,)), ((), ())), preferred...  29.1 us
  transfers between devices with their start and end apart: 28, of which 15 were waited for; matrix products, arithmetic and copies ran while one was open for 6% of the time, Pallas kernels for 0%

commit v1 on v0

v1 whole, which is shorter than its diff:
```python
import functools

import jax
import jax.numpy as jnp
from jax import lax
from jax.experimental import pallas as pl
from jax.experimental.pallas import tpu as pltpu
from jax.sharding import PartitionSpec as P

AXES = ("gx", "gy")
ROW = 4
LOW = -4.0
EPSILON = 1e-06
VMEM = 40 * 1024 * 1024

OWN, NEXT, PREV, UP, DOWN, UP_NEXT, DOWN_PREV = range(0, 56, 8)
ONE, LEFT_HALF, EVEN, ODD, EVEN_FIRST, ODD_LAST = range(56, 62)


def shifted(array, pairs):
    return lax.ppermute(array, AXES, pairs)


def smem():
    return pl.BlockSpec(memory_space=pltpu.SMEM)


def vmem():
    return pl.BlockSpec(memory_space=pltpu.VMEM)


def unit_kernel(live, embeddings, units):
    blocks, count, _ = embeddings.shape
    position = lax.broadcasted_iota(jnp.int32, (count, 1), 0)

    def normalize(b, carry):
        values = embeddings[b].astype(jnp.float32)
        factor = lax.rsqrt(jnp.sum(values * values, axis=-1, keepdims=True) + EPSILON)
        unit = values * factor
        units[b] = jnp.where(position < live[b], unit, unit[0:1]).astype(jnp.bfloat16)
        return carry

    lax.fori_loop(0, blocks, normalize, 0)


def normalize(embeddings, live):
    return pl.pallas_call(
        unit_kernel,
        out_shape=jax.ShapeDtypeStruct(embeddings.shape, jnp.bfloat16),
        in_specs=[smem(), vmem()],
        out_specs=vmem(),
        compiler_params=pltpu.CompilerParams(vmem_limit_bytes=VMEM),
        cost_estimate=pl.CostEstimate(flops=4 * embeddings.size, bytes_accessed=4 * embeddings.size, transcendentals=0),
    )(live, embeddings)


def own_kernel(cluster, live, units, best):
    blocks, count, width = units.shape
    rows = lax.broadcasted_iota(jnp.int32, (count, count), 0)
    columns = lax.broadcasted_iota(jnp.int32, (count, count), 1)
    other = units[...].reshape(blocks * count, width)

    def chunk(i, carry):
        similar = lax.dot_general(
            units[pl.ds(2 * i, 2)].reshape(2 * count, width), other,
            (((1,), (1,)), ((), ())), preferred_element_type=jnp.float32,
        )
        for k in range(2):
            a = 2 * i + k
            top = None
            for j in range(blocks):
                part = similar[k * count:(k + 1) * count, j * count:(j + 1) * count]
                part = part + jnp.where(cluster[a] == cluster[j], 0.0, LOW)
                hidden = (a == j) & ((rows == columns) | (columns >= live[j]))
                part = jnp.where(hidden, LOW, part)
                top = part if top is None else jnp.maximum(top, part)
            best[pl.ds(a, 1)] = jnp.max(top.T, axis=0, keepdims=True)
        return carry

    lax.fori_loop(0, blocks // 2, chunk, 0)


def own_tile(units, cluster, live):
    blocks, count, width = units.shape
    return pl.pallas_call(
        own_kernel,
        out_shape=jax.ShapeDtypeStruct((blocks, count), jnp.float32),
        in_specs=[smem(), smem(), vmem()],
        out_specs=vmem(),
        compiler_params=pltpu.CompilerParams(vmem_limit_bytes=VMEM),
        cost_estimate=pl.CostEstimate(
            flops=2 * (blocks * count) ** 2 * width, bytes_accessed=2 * blocks * count * width, transcendentals=0
        ),
    )(cluster, live, units)


def pairs_kernel(parts, jobs, items, ids, *refs):
    arrays, outs = refs[:len(parts)], refs[len(parts):]
    for out in outs:
        out[...] = jnp.full(out.shape, LOW, jnp.float32)
    for first, second, flag in jobs:
        a, b = arrays[first], arrays[second]
        a_item, a_base, a_offset = parts[first]
        b_item, b_base, b_offset = parts[second]
        a_out, b_out = outs[items.index(a_item)], outs[items.index(b_item)]
        count, width = a.shape[1], a.shape[2]
        b_blocks = b.shape[0]

        @pl.when(ids[flag] > 0)
        def _(a=a, b=b, a_out=a_out, b_out=b_out, a_base=a_base, b_base=b_base,
              a_offset=a_offset, b_offset=b_offset, b_blocks=b_blocks):
            a0 = a_base + a_offset
            b0 = b_base + b_offset
            least, most = ids[b0], ids[b0 + b_blocks - 1]

            def chunk(i, carry):
                meets = (ids[a0 + 2 * i + 1] >= least) & (ids[a0 + 2 * i] <= most)

                @pl.when(meets)
                def _():
                    similar = lax.dot_general(
                        a[pl.ds(2 * i, 2)].reshape(2 * count, width),
                        b[...].reshape(b_blocks * count, width),
                        (((1,), (1,)), ((), ())), preferred_element_type=jnp.float32,
                    )
                    tops = [None, None]
                    for j in range(b_blocks):
                        column = None
                        for k in range(2):
                            part = similar[k * count:(k + 1) * count, j * count:(j + 1) * count]
                            part = part + jnp.where(ids[a0 + 2 * i + k] == ids[b0 + j], 0.0, LOW)
                            tops[k] = part if tops[k] is None else jnp.maximum(tops[k], part)
                            column = part if column is None else jnp.maximum(column, part)
                        here = pl.ds(b_offset + j, 1)
                        b_out[here] = jnp.maximum(b_out[here], jnp.max(column, axis=0, keepdims=True))
                    for k in range(2):
                        here = pl.ds(a_offset + 2 * i + k, 1)
                        a_out[here] = jnp.maximum(a_out[here], jnp.max(tops[k].T, axis=0, keepdims=True))

                return carry

            lax.fori_loop(0, a.shape[0] // 2, chunk, 0)


def compare(ids, parts, jobs):
    items = []
    for _, item, _, _ in parts:
        if item not in items:
            items.append(item)
    arrays = [part[0] for part in parts]
    blocks = 8
    count, width = arrays[0].shape[1], arrays[0].shape[2]
    flops = sum(2 * arrays[f].shape[0] * arrays[s].shape[0] * count * count * width for f, s, _ in jobs)
    found = pl.pallas_call(
        functools.partial(pairs_kernel, [part[1:] for part in parts], jobs, items),
        out_shape=[jax.ShapeDtypeStruct((blocks, count), jnp.float32) for _ in items],
        in_specs=[smem()] + [vmem() for _ in arrays],
        out_specs=[vmem() for _ in items],
        compiler_params=pltpu.CompilerParams(vmem_limit_bytes=VMEM),
        cost_estimate=pl.CostEstimate(
            flops=flops, bytes_accessed=sum(2 * a.size for a in arrays), transcendentals=0
        ),
    )(ids, *arrays)
    return dict(zip(items, found))


def merged(*results):
    total = {}
    for result in results:
        for item, value in result.items():
            total[item] = jnp.maximum(total[item], value) if item in total else value
    return total


def ring(devices, by, rows=None):
    return [
        (row * ROW + x, row * ROW + (x + by) % ROW)
        for row in range(devices // ROW) if rows is None or rows(row) for x in range(ROW)
    ]


def column(devices, by, rows=None):
    return [
        (i, i + by * ROW) for i in range(devices)
        if 0 <= i + by * ROW < devices and (rows is None or rows((i + by * ROW) // ROW))
    ]


def body(embeddings, block_cluster, block_rows):
    minor = lax.axis_size(AXES[1])
    devices = lax.axis_size(AXES[0]) * minor
    blocks, count, _ = embeddings.shape
    major = lax.axis_index(AXES[0])
    me = lax.axis_index(AXES).astype(jnp.int32)
    x, row = me % ROW, me // ROW
    last_row = devices // ROW - 1
    even_site = major % 2 == 0

    def even(r):
        return (r * ROW // minor) % 2 == 0

    def odd(r):
        return not even(r)

    right, left = ring(devices, 1), ring(devices, -1)
    below, above = column(devices, 1), column(devices, -1)

    line = jnp.stack([
        block_cluster, shifted(block_cluster, left), shifted(block_cluster, ring(devices, 2)), shifted(block_cluster, right)
    ])
    line_up = jnp.where(row > 0, shifted(line, below), -1)
    line_down = jnp.where(row < last_row, shifted(line, above), -2)
    down_prev = jnp.where(even_site & (x == 0), line_up[3], jnp.where(~even_site & (x == ROW - 1), line_down[1], line_down[3]))
    flags = jnp.stack([
        x >= 0, x < 2, even_site, ~even_site, even_site & (x == 0), ~even_site & (x == ROW - 1), x < 0, x < 0
    ]).astype(jnp.int32)
    ids = jnp.concatenate([line[0], line[1], line[3], line_up[0], line_down[0], line_up[1], down_prev, flags])

    units = normalize(embeddings, block_rows)
    to_down, to_up = shifted(units, below), shifted(units, above)
    nxt, prv = shifted(units, left), shifted(units, right)
    up, down = to_down, to_up
    up_next_even = shifted(up, ring(devices, -1, even))
    down_prev_even = shifted(jnp.where(x == ROW - 1, up, down), ring(devices, 1, even))
    up_next_odd = shifted(nxt, column(devices, 1, odd))
    down_prev_odd = shifted(jnp.where(x == ROW - 1, nxt, prv), column(devices, -1, odd))

    best = own_tile(units, block_cluster, block_rows)
    first = compare(
        ids, [(units, "own", OWN, 0), (nxt, "next", NEXT, 0), (prv, "prev", PREV, 0), (up, "up", UP, 0)],
        [(0, 1, ONE), (1, 2, LEFT_HALF), (0, 3, ONE), (1, 3, ONE), (2, 3, ONE)],
    )
    second = compare(
        ids,
        [
            (prv, "prev", PREV, 0), (up, "up", UP, 0), (down, "down", DOWN, 0),
            (up_next_even, "up_next", UP_NEXT, 0), (down_prev_even, "down_prev", DOWN_PREV, 0),
            (up_next_odd, "up_next", UP_NEXT, 0), (down_prev_odd, "down_prev", DOWN_PREV, 0),
        ],
        [
            (0, 3, EVEN), (2, 3, EVEN), (3, 4, EVEN), (2, 4, EVEN_FIRST),
            (0, 5, ODD), (2, 5, ODD), (5, 6, ODD), (1, 6, ODD_LAST),
        ],
    )
    found = merged(first, second)
    none = jnp.full((blocks, count), LOW, jnp.float32)
    early, late = even_site & (x == 0), ~even_site & (x == ROW - 1)
    from_prev = shifted(
        jnp.stack([found["next"], found["up_next"], jnp.where(late, found["down_prev"], none)]), right
    )
    from_next = shifted(
        jnp.stack([
            found["prev"], jnp.where(early, found["down_prev"], none),
            jnp.where(early | late, none, found["down_prev"]),
        ]), left
    )
    around = jnp.maximum(from_prev, from_next)
    from_down = shifted(jnp.maximum(found["up"], around[1]), above)
    from_up = shifted(jnp.maximum(found["down"], around[2]), below)
    best = jnp.maximum(jnp.maximum(best, found["own"]), around[0])
    best = jnp.maximum(best, jnp.where(row < last_row, from_down, LOW))
    best = jnp.maximum(best, jnp.where(row > 0, from_up, LOW))
    position = lax.broadcasted_iota(jnp.int32, (blocks, count), 1)
    return jnp.where(position < block_rows[:, None], jnp.maximum(1.0 + best, 0.0) - 1.0, 0.0)


def solution(mesh):
    placed = (P(AXES, None, None), P(AXES), P(AXES))
    return jax.shard_map(body, mesh=mesh, in_specs=placed, out_specs=P(AXES, None), check_vma=False)
```

time: 485 us -> 157 us (0.32)
  the two profiles are of different devices: /device:TPU:11 before, /device:TPU:32 now
where the time goes in v1:
time: 157 us
  waiting for transfers between devices  68.7 us (44%)
  starting transfers between devices  40.4 us (26%)
  Pallas kernels  39.8 us (25%)
  other arithmetic  5.42 us (3%)
  local copies, waits for them, and re-layouts  2.45 us (2%)
    ppermute x17, waiting for transfers between devices, shifted(): return lax.ppermute(array, AXES, pairs)  68.7 us
    ppermute x17, starting transfers between devices, shifted(): return lax.ppermute(array, AXES, pairs)  40.4 us
    pallas_call x2, Pallas kernels, compare(): pl.pallas_call(functools.partial(pairs_kernel, [part[1:] for part in part...  31.5 us
    pallas_call x1, Pallas kernels, own_tile(): pl.pallas_call(own_kernel, out_shape=jax.ShapeDtypeStruct((blocks, count)...  5.27 us
  transfers between devices with their start and end apart: 17, of which 8 were waited for; matrix products, arithmetic and copies ran while one was open for 3% of the time, Pallas kernels for 16%

profile of v1, /device:TPU:32, one launch (start us, length us, event | category | flops | bytes accessed | tf_op | source)
XLA Modules:
  0.0 157.0 jit_solution(5439430611197549013)
XLA Ops:
  0.0 1.6 %copy-done = bf16[8,128,1024]{2,1,0:T(8,128)(2,1)S(1)} copy-done((bf16[8,128,1024]{2,1,0:T(8,128)(2,1)S(1)}, bf16[8,128,1024]{2,1,0:T(8,128)(2,1)}, u32[]{:S(2)}) %copy-start) | copy-done | bytes 2097176
  1.6 0.7 copy-done.1
  2.2 3.1 %shard_map.37.units.refs_0_ = bf16[8,128,1024]{2,1,0:T(8,128)(2,1)} custom-call(s32[8]{0:T(128)S(1)} %copy-done.1, bf16[8,128,1024]{2,1,0:T(8,128)(2,1)S(1)} %copy-done), custom_call_target="tpu_custom_call" | custom-call | flops 4194304 | bytes 4194304 | tf_op jit(solution)/shard_map/pallas_call | solution.py:47
  5.3 1.9 %collective-permute-start.8 = (bf16[8,128,1024]{2,1,0:T(8,128)(2,1)}, bf16[8,128,1024]{2,1,0:T(8,128)(2,1)S(1)}, u32[]{:S(2)}, u32[]{:S(2)}) collective-permute-start(bf16[8,128,1024]{2,1,0:T(8,128)(2,1)} %shard_map.37.units.refs_0_), channel_id=1, source_target_pairs={{4,0},{5,1},{6,2},{7,3},{8,4},{9,5},{10,6},{11,7},{12,8},{13,9},{1... | collective-permute-start | bytes 6291464 | tf_op jit(solution)/shard_map/ppermute | solution.py:21
  7.2 3.9 %collective-permute-start.7 = (bf16[8,128,1024]{2,1,0:T(8,128)(2,1)}, bf16[8,128,1024]{2,1,0:T(8,128)(2,1)}, u32[]{:S(2)}, u32[]{:S(2)}) collective-permute-start(bf16[8,128,1024]{2,1,0:T(8,128)(2,1)} %shard_map.37.units.refs_0_), channel_id=1, source_target_pairs={{0,4},{1,5},{2,6},{3,7},{4,8},{5,9},{6,10},{7,11},{8,12},{9,13},{1... | collective-permute-start | bytes 6291464 | tf_op jit(solution)/shard_map/ppermute | solution.py:21
  11.2 1.6 collective-permute-start.6
  12.7 1.7 %collective-permute-start.5 = (bf16[8,128,1024]{2,1,0:T(8,128)(2,1)}, bf16[8,128,1024]{2,1,0:T(8,128)(2,1)}, u32[]{:S(2)}, u32[]{:S(2)}) collective-permute-start(bf16[8,128,1024]{2,1,0:T(8,128)(2,1)} %shard_map.37.units.refs_0_), channel_id=1, source_target_pairs={{0,3},{1,0},{2,1},{3,2},{4,7},{5,4},{6,5},{7,6},{8,11},{9,8},{10,9... | collective-permute-start | bytes 6291464 | tf_op jit(solution)/shard_map/ppermute | solution.py:21
  14.5 40.5 %collective-permute-done.8.refs_2_ = bf16[8,128,1024]{2,1,0:T(8,128)(2,1)S(1)} collective-permute-done((bf16[8,128,1024]{2,1,0:T(8,128)(2,1)}, bf16[8,128,1024]{2,1,0:T(8,128)(2,1)S(1)}, u32[]{:S(2)}, u32[]{:S(2)}) %collective-permute-start.8) | collective-permute-done | bytes 2097184 | tf_op jit(solution)/shard_map/ppermute | solution.py:21
  55.0 1.4 collective-permute-done.7.refs_3_.refs_1_
  56.4 1.6 broadcast_select_fusion.1
  57.9 3.7 %collective-permute-start.10 = (bf16[8,128,1024]{2,1,0:T(8,128)(2,1)}, bf16[8,128,1024]{2,1,0:T(8,128)(2,1)}, u32[]{:S(2)}, u32[]{:S(2)}) collective-permute-start(bf16[8,128,1024]{2,1,0:T(8,128)(2,1)} %broadcast_select_fusion.1), channel_id=1, source_target_pairs={{0,1},{1,2},{2,3},{3,0},{4,5},{5,6},{6,7},{7,4},{8,9},{9,10},{10,1... | collective-permute-start | bytes 6291464 | tf_op jit(solution)/shard_map/ppermute | solution.py:21
  61.6 4.8 %collective-permute-start.9 = (bf16[8,128,1024]{2,1,0:T(8,128)(2,1)}, bf16[8,128,1024]{2,1,0:T(8,128)(2,1)}, u32[]{:S(2)}, u32[]{:S(2)}) collective-permute-start(bf16[8,128,1024]{2,1,0:T(8,128)(2,1)} %collective-permute-done.7.refs_3_.refs_1_), channel_id=1, source_target_pairs={{0,3},{1,0},{2,1},{3,2},{4,7},{5,4},{6,5},{7,6},{8,11},{9,8},{10,9... | collective-permute-start | bytes 6291464 | tf_op jit(solution)/shard_map/ppermute | solution.py:21
  66.4 0.0 collective-permute-done.6.refs_2_.refs_0_
  66.4 0.0 collective-permute-done.5.refs_1_
  66.4 3.1 %broadcast_select_fusion = bf16[8,128,1024]{2,1,0:T(8,128)(2,1)} fusion(bf16[8,128,1024]{2,1,0:T(8,128)(2,1)} %collective-permute-done.5.refs_1_, bf16[8,128,1024]{2,1,0:T(8,128)(2,1)} %collective-permute-done.6.refs_2_.refs_0_, pred[]{:T(512)S(6)} %eq.20), kind=kLoop, calls=%fused_computation | loop fusion | flops 1048576 | bytes 6291457 | tf_op jit(solution)/shard_map/jit(_where)/select_n | solution.py:226
  69.5 2.0 %collective-permute-start.12 = (bf16[8,128,1024]{2,1,0:T(8,128)(2,1)}, bf16[8,128,1024]{2,1,0:T(8,128)(2,1)}, u32[]{:S(2)}, u32[]{:S(2)}) collective-permute-start(bf16[8,128,1024]{2,1,0:T(8,128)(2,1)} %broadcast_select_fusion), channel_id=1, source_target_pairs={{20,16},{21,17},{22,18},{23,19},{24,20},{25,21},{26,22},{27,23},{2... | collective-permute-start | bytes 6291464 | tf_op jit(solution)/shard_map/ppermute | solution.py:21
  71.5 2.0 %collective-permute-start.11 = (bf16[8,128,1024]{2,1,0:T(8,128)(2,1)}, bf16[8,128,1024]{2,1,0:T(8,128)(2,1)}, u32[]{:S(2)}, u32[]{:S(2)}) collective-permute-start(bf16[8,128,1024]{2,1,0:T(8,128)(2,1)} %collective-permute-done.5.refs_1_), channel_id=1, source_target_pairs={{12,16},{13,17},{14,18},{15,19},{16,20},{17,21},{18,22},{19,23},{2... | collective-permute-start | bytes 6291464 | tf_op jit(solution)/shard_map/ppermute | solution.py:21
  73.5 0.0 copy-done.3
  73.5 0.0 collective-permute-start.1
  73.5 15.3 %collective-permute-done.1 = s32[8]{0:T(128)S(1)} collective-permute-done((s32[8]{0:T(128)S(1)}, s32[8]{0:T(128)S(1)}, u32[]{:S(2)}, u32[]{:S(2)}) %collective-permute-start.1) | collective-permute-done | bytes 64 | tf_op jit(solution)/shard_map/ppermute | solution.py:21
  88.8 2.0 %collective-permute-start = (s32[8]{0:T(128)S(1)}, s32[8]{0:T(128)S(1)}, u32[]{:S(2)}, u32[]{:S(2)}) collective-permute-start(s32[8]{0:T(128)S(1)} %copy-done.3), channel_id=1, source_target_pairs={{0,3},{1,0},{2,1},{3,2},{4,7},{5,4},{6,5},{7,6},{8,11},{9,8},{10,9... | collective-permute-start | bytes 104 | tf_op jit(solution)/shard_map/ppermute | solution.py:21
  90.8 1.5 collective-permute-done
  92.3 1.9 %collective-permute-start.2 = (s32[8]{0:T(128)S(1)}, s32[8]{0:T(128)S(1)}, u32[]{:S(2)}, u32[]{:S(2)}) collective-permute-start(s32[8]{0:T(128)S(1)} %copy-done.3), channel_id=1, source_target_pairs={{0,2},{1,3},{2,0},{3,1},{4,6},{5,7},{6,4},{7,5},{8,10},{9,11},{10,... | collective-permute-start | bytes 104 | tf_op jit(solution)/shard_map/ppermute | solution.py:21
  94.2 3.2 %collective-permute-done.2 = s32[8]{0:T(128)S(1)} collective-permute-done((s32[8]{0:T(128)S(1)}, s32[8]{0:T(128)S(1)}, u32[]{:S(2)}, u32[]{:S(2)}) %collective-permute-start.2) | collective-permute-done | bytes 64 | tf_op jit(solution)/shard_map/ppermute | solution.py:21
  97.4 1.9 %collective-permute-start.4 = (s32[4,8]{1,0:T(4,128)S(1)}, s32[4,8]{1,0:T(4,128)S(1)}, u32[]{:S(2)}, u32[]{:S(2)}) collective-permute-start(s32[4,8]{1,0:T(4,128)S(1)} %pad_add_fusion), channel_id=1, source_target_pairs={{4,0},{5,1},{6,2},{7,3},{8,4},{9,5},{10,6},{11,7},{12,8},{13,9},{1... | collective-permute-start | bytes 392 | tf_op jit(solution)/shard_map/ppermute | solution.py:21
  99.3 0.1 stack.76
  99.4 3.6 %collective-permute-done.4 = s32[4,8]{1,0:T(4,128)S(1)} collective-permute-done((s32[4,8]{1,0:T(4,128)S(1)}, s32[4,8]{1,0:T(4,128)S(1)}, u32[]{:S(2)}, u32[]{:S(2)}) %collective-permute-start.4) | collective-permute-done | bytes 160 | tf_op jit(solution)/shard_map/ppermute | solution.py:21
  103.1 3.9 %collective-permute-start.3 = (s32[4,8]{1,0:T(4,128)S(1)}, s32[4,8]{1,0:T(4,128)S(1)}, u32[]{:S(2)}, u32[]{:S(2)}) collective-permute-start(s32[4,8]{1,0:T(4,128)S(1)} %pad_add_fusion), channel_id=1, source_target_pairs={{0,4},{1,5},{2,6},{3,7},{4,8},{5,9},{6,10},{7,11},{8,12},{9,13},{1... | collective-permute-start | bytes 392 | tf_op jit(solution)/shard_map/ppermute | solution.py:21
  107.0 1.5 collective-permute-done.3
  108.5 0.1 concatenate.3.ids
  108.6 20.0 %shard_map.39 = (f32[8,128]{1,0:T(8,128)S(1)}, f32[8,128]{1,0:T(8,128)S(1)}, f32[8,128]{1,0:T(8,128)S(1)}, f32[8,128]{1,0:T(8,128)S(1)}) custom-call(s32[64]{0:T(128)S(1)} %concatenate.3.ids, bf16[8,128,1024]{2,1,0:T(8,128)(2,1)} %shard_map.37.units.refs_0_, bf16[8,128,1024]{2,1,0:T(8,128)(2,1)} %collective-permute-done.5.refs_1_, ...), custom_call_target="tpu_custom_call" | custom-call | flops 10737418240 | bytes 8388608 | tf_op jit(solution)/shard_map/pallas_call | solution.py:154
  128.6 0.0 copy-start.2
  128.7 0.0 collective-permute-done.10.refs_4_
  128.7 0.0 collective-permute-done.9.refs_3_
  128.7 0.0 collective-permute-done.12.refs_6_
  128.7 0.0 collective-permute-done.11.refs_5_
  128.7 11.4 %shard_map.40 = (f32[8,128]{1,0:T(8,128)S(1)}, f32[8,128]{1,0:T(8,128)S(1)}, f32[8,128]{1,0:T(8,128)S(1)}, f32[8,128]{1,0:T(8,128)S(1)}, f32[8,128]{1,0:T(8,128)S(1)}) custom-call(s32[64]{0:T(128)S(1)} %concatenate.3.ids, bf16[8,128,1024]{2,1,0:T(8,128)(2,1)} %collective-permute-done.6.refs_2_.refs_0_, ...), custom_call_target="tpu_custom_call" | custom-call | flops 17179869184 | bytes 14680064 | tf_op jit(solution)/shard_map/pallas_call | solution.py:154
  140.2 0.1 collective-permute-start.13
  140.3 3.2 %collective-permute-start.14 = (f32[3,8,128]{2,1,0:T(8,128)S(1)}, f32[3,8,128]{2,1,0:T(8,128)S(1)}, u32[]{:S(2)}, u32[]{:S(2)}) collective-permute-start(f32[3,8,128]{2,1,0:T(8,128)S(1)} %pad_maximum_fusion.1), channel_id=1, source_target_pairs={{0,3},{1,0},{2,1},{3,2},{4,7},{5,4},{6,5},{7,6},{8,11},{9,8},{10,9... | collective-permute-start | bytes 36872 | tf_op jit(solution)/shard_map/ppermute | solution.py:21
  143.5 1.7 %collective-permute-done.13 = f32[3,8,128]{2,1,0:T(8,128)S(1)} collective-permute-done((f32[3,8,128]{2,1,0:T(8,128)S(1)}, f32[3,8,128]{2,1,0:T(8,128)S(1)}, u32[]{:S(2)}, u32[]{:S(2)}) %collective-permute-start.13) | collective-permute-done | bytes 12320 | tf_op jit(solution)/shard_map/ppermute | solution.py:21
  145.2 0.0 collective-permute-done.14
  145.2 1.9 %collective-permute-start.15 = (f32[8,128]{1,0:T(8,128)S(1)}, f32[8,128]{1,0:T(8,128)S(1)}, u32[]{:S(2)}, u32[]{:S(2)}) collective-permute-start(f32[8,128]{1,0:T(8,128)S(1)} %get-tuple-element.23), channel_id=1, source_target_pairs={{4,0},{5,1},{6,2},{7,3},{8,4},{9,5},{10,6},{11,7},{12,8},{13,9},{1... | collective-permute-start | bytes 12296 | tf_op jit(solution)/shard_map/ppermute | solution.py:21
  147.1 3.9 %collective-permute-start.16 = (f32[8,128]{1,0:T(8,128)S(1)}, f32[8,128]{1,0:T(8,128)S(1)}, u32[]{:S(2)}, u32[]{:S(2)}) collective-permute-start(f32[8,128]{1,0:T(8,128)S(1)} %get-tuple-element.24), channel_id=1, source_target_pairs={{0,4},{1,5},{2,6},{3,7},{4,8},{5,9},{6,10},{7,11},{8,12},{9,13},{1... | collective-permute-start | bytes 12296 | tf_op jit(solution)/shard_map/ppermute | solution.py:21
  151.0 0.0 copy-done.2
  151.0 5.3 %shard_map.38 = f32[8,128]{1,0:T(8,128)S(1)} custom-call(s32[8]{0:T(128)S(1)} %copy-done.3, s32[8]{0:T(128)S(1)} %copy-done.2, bf16[8,128,1024]{2,1,0:T(8,128)(2,1)} %shard_map.37.units.refs_0_), custom_call_target="tpu_custom_call" | custom-call | flops 2147483648 | bytes 2097152 | tf_op jit(solution)/shard_map/pallas_call | solution.py:85
  156.3 0.0 collective-permute-done.15
  156.3 0.0 collective-permute-done.16
  156.3 0.7 fusion.8
  (14 shorter events, 0.1 us)
Async XLA Ops:
  0.0 1.6 %copy-start = (bf16[8,128,1024]{2,1,0:T(8,128)(2,1)S(1)}, bf16[8,128,1024]{2,1,0:T(8,128)(2,1)}, u32[]{:S(2)}) copy-start(bf16[8,128,1024]{2,1,0:T(8,128)(2,1)} %embeddings.1) | copy-start | bytes 6291460
  1.6 0.7 copy-start.1
  5.3 49.6 %collective-permute-start.8 = (bf16[8,128,1024]{2,1,0:T(8,128)(2,1)}, bf16[8,128,1024]{2,1,0:T(8,128)(2,1)S(1)}, u32[]{:S(2)}, u32[]{:S(2)}) collective-permute-start(bf16[8,128,1024]{2,1,0:T(8,128)(2,1)} %shard_map.37.units.refs_0_), channel_id=1, source_target_pairs={{4,0},{5,1},{6,2},{7,3},{8,4},{9,5},{10,6},{11,7},{12,8},{13,9},{1... | collective-permute-start | bytes 6291464 | tf_op jit(solution)/shard_map/ppermute | solution.py:21
  7.2 49.1 %collective-permute-start.7 = (bf16[8,128,1024]{2,1,0:T(8,128)(2,1)}, bf16[8,128,1024]{2,1,0:T(8,128)(2,1)}, u32[]{:S(2)}, u32[]{:S(2)}) collective-permute-start(bf16[8,128,1024]{2,1,0:T(8,128)(2,1)} %shard_map.37.units.refs_0_), channel_id=1, source_target_pairs={{0,4},{1,5},{2,6},{3,7},{4,8},{5,9},{6,10},{7,11},{8,12},{9,13},{1... | collective-permute-start | bytes 6291464 | tf_op jit(solution)/shard_map/ppermute | solution.py:21
  11.2 55.2 %collective-permute-start.6 = (bf16[8,128,1024]{2,1,0:T(8,128)(2,1)}, bf16[8,128,1024]{2,1,0:T(8,128)(2,1)}, u32[]{:S(2)}, u32[]{:S(2)}) collective-permute-start(bf16[8,128,1024]{2,1,0:T(8,128)(2,1)} %shard_map.37.units.refs_0_), channel_id=1, source_target_pairs={{0,1},{1,2},{2,3},{3,0},{4,5},{5,6},{6,7},{7,4},{8,9},{9,10},{10,1... | collective-permute-start | bytes 6291464 | tf_op jit(solution)/shard_map/ppermute | solution.py:21
  12.7 53.7 %collective-permute-start.5 = (bf16[8,128,1024]{2,1,0:T(8,128)(2,1)}, bf16[8,128,1024]{2,1,0:T(8,128)(2,1)}, u32[]{:S(2)}, u32[]{:S(2)}) collective-permute-start(bf16[8,128,1024]{2,1,0:T(8,128)(2,1)} %shard_map.37.units.refs_0_), channel_id=1, source_target_pairs={{0,3},{1,0},{2,1},{3,2},{4,7},{5,4},{6,5},{7,6},{8,11},{9,8},{10,9... | collective-permute-start | bytes 6291464 | tf_op jit(solution)/shard_map/ppermute | solution.py:21
  57.9 15.6 %copy-start.3 = (s32[8]{0:T(128)S(1)}, s32[8]{0:T(128)}, u32[]{:S(2)}) copy-start(s32[8]{0:T(128)} %cluster.1) | copy-start | bytes 100
  57.9 70.7 %collective-permute-start.10 = (bf16[8,128,1024]{2,1,0:T(8,128)(2,1)}, bf16[8,128,1024]{2,1,0:T(8,128)(2,1)}, u32[]{:S(2)}, u32[]{:S(2)}) collective-permute-start(bf16[8,128,1024]{2,1,0:T(8,128)(2,1)} %broadcast_select_fusion.1), channel_id=1, source_target_pairs={{0,1},{1,2},{2,3},{3,0},{4,5},{5,6},{6,7},{7,4},{8,9},{9,10},{10,1... | collective-permute-start | bytes 6291464 | tf_op jit(solution)/shard_map/ppermute | solution.py:21
  61.6 67.1 %collective-permute-start.9 = (bf16[8,128,1024]{2,1,0:T(8,128)(2,1)}, bf16[8,128,1024]{2,1,0:T(8,128)(2,1)}, u32[]{:S(2)}, u32[]{:S(2)}) collective-permute-start(bf16[8,128,1024]{2,1,0:T(8,128)(2,1)} %collective-permute-done.7.refs_3_.refs_1_), channel_id=1, source_target_pairs={{0,3},{1,0},{2,1},{3,2},{4,7},{5,4},{6,5},{7,6},{8,11},{9,8},{10,9... | collective-permute-start | bytes 6291464 | tf_op jit(solution)/shard_map/ppermute | solution.py:21
  69.5 59.1 %collective-permute-start.12 = (bf16[8,128,1024]{2,1,0:T(8,128)(2,1)}, bf16[8,128,1024]{2,1,0:T(8,128)(2,1)}, u32[]{:S(2)}, u32[]{:S(2)}) collective-permute-start(bf16[8,128,1024]{2,1,0:T(8,128)(2,1)} %broadcast_select_fusion), channel_id=1, source_target_pairs={{20,16},{21,17},{22,18},{23,19},{24,20},{25,21},{26,22},{27,23},{2... | collective-permute-start | bytes 6291464 | tf_op jit(solution)/shard_map/ppermute | solution.py:21
  71.5 57.2 %collective-permute-start.11 = (bf16[8,128,1024]{2,1,0:T(8,128)(2,1)}, bf16[8,128,1024]{2,1,0:T(8,128)(2,1)}, u32[]{:S(2)}, u32[]{:S(2)}) collective-permute-start(bf16[8,128,1024]{2,1,0:T(8,128)(2,1)} %collective-permute-done.5.refs_1_), channel_id=1, source_target_pairs={{12,16},{13,17},{14,18},{15,19},{16,20},{17,21},{18,22},{19,23},{2... | collective-permute-start | bytes 6291464 | tf_op jit(solution)/shard_map/ppermute | solution.py:21
  73.5 15.3 %collective-permute-start.1 = (s32[8]{0:T(128)S(1)}, s32[8]{0:T(128)S(1)}, u32[]{:S(2)}, u32[]{:S(2)}) collective-permute-start(s32[8]{0:T(128)S(1)} %copy-done.3), channel_id=1, source_target_pairs={{0,1},{1,2},{2,3},{3,0},{4,5},{5,6},{6,7},{7,4},{8,9},{9,10},{10,1... | collective-permute-start | bytes 104 | tf_op jit(solution)/shard_map/ppermute | solution.py:21
  88.8 3.5 %collective-permute-start = (s32[8]{0:T(128)S(1)}, s32[8]{0:T(128)S(1)}, u32[]{:S(2)}, u32[]{:S(2)}) collective-permute-start(s32[8]{0:T(128)S(1)} %copy-done.3), channel_id=1, source_target_pairs={{0,3},{1,0},{2,1},{3,2},{4,7},{5,4},{6,5},{7,6},{8,11},{9,8},{10,9... | collective-permute-start | bytes 104 | tf_op jit(solution)/shard_map/ppermute | solution.py:21
  92.3 5.0 %collective-permute-start.2 = (s32[8]{0:T(128)S(1)}, s32[8]{0:T(128)S(1)}, u32[]{:S(2)}, u32[]{:S(2)}) collective-permute-start(s32[8]{0:T(128)S(1)} %copy-done.3), channel_id=1, source_target_pairs={{0,2},{1,3},{2,0},{3,1},{4,6},{5,7},{6,4},{7,5},{8,10},{9,11},{10,... | collective-permute-start | bytes 104 | tf_op jit(solution)/shard_map/ppermute | solution.py:21
  97.4 5.7 %collective-permute-start.4 = (s32[4,8]{1,0:T(4,128)S(1)}, s32[4,8]{1,0:T(4,128)S(1)}, u32[]{:S(2)}, u32[]{:S(2)}) collective-permute-start(s32[4,8]{1,0:T(4,128)S(1)} %pad_add_fusion), channel_id=1, source_target_pairs={{4,0},{5,1},{6,2},{7,3},{8,4},{9,5},{10,6},{11,7},{12,8},{13,9},{1... | collective-permute-start | bytes 392 | tf_op jit(solution)/shard_map/ppermute | solution.py:21
  103.1 5.5 %collective-permute-start.3 = (s32[4,8]{1,0:T(4,128)S(1)}, s32[4,8]{1,0:T(4,128)S(1)}, u32[]{:S(2)}, u32[]{:S(2)}) collective-permute-start(s32[4,8]{1,0:T(4,128)S(1)} %pad_add_fusion), channel_id=1, source_target_pairs={{0,4},{1,5},{2,6},{3,7},{4,8},{5,9},{6,10},{7,11},{8,12},{9,13},{1... | collective-permute-start | bytes 392 | tf_op jit(solution)/shard_map/ppermute | solution.py:21
  128.6 22.4 %copy-start.2 = (s32[8]{0:T(128)S(1)}, s32[8]{0:T(128)}, u32[]{:S(2)}) copy-start(s32[8]{0:T(128)} %live.3) | copy-start | bytes 100
  140.2 5.0 %collective-permute-start.13 = (f32[3,8,128]{2,1,0:T(8,128)S(1)}, f32[3,8,128]{2,1,0:T(8,128)S(1)}, u32[]{:S(2)}, u32[]{:S(2)}) collective-permute-start(f32[3,8,128]{2,1,0:T(8,128)S(1)} %pad_maximum_fusion), channel_id=1, source_target_pairs={{0,1},{1,2},{2,3},{3,0},{4,5},{5,6},{6,7},{7,4},{8,9},{9,10},{10,1... | collective-permute-start | bytes 36872 | tf_op jit(solution)/shard_map/ppermute | solution.py:21
  140.3 4.9 %collective-permute-start.14 = (f32[3,8,128]{2,1,0:T(8,128)S(1)}, f32[3,8,128]{2,1,0:T(8,128)S(1)}, u32[]{:S(2)}, u32[]{:S(2)}) collective-permute-start(f32[3,8,128]{2,1,0:T(8,128)S(1)} %pad_maximum_fusion.1), channel_id=1, source_target_pairs={{0,3},{1,0},{2,1},{3,2},{4,7},{5,4},{6,5},{7,6},{8,11},{9,8},{10,9... | collective-permute-start | bytes 36872 | tf_op jit(solution)/shard_map/ppermute | solution.py:21
  145.2 11.1 %collective-permute-start.15 = (f32[8,128]{1,0:T(8,128)S(1)}, f32[8,128]{1,0:T(8,128)S(1)}, u32[]{:S(2)}, u32[]{:S(2)}) collective-permute-start(f32[8,128]{1,0:T(8,128)S(1)} %get-tuple-element.23), channel_id=1, source_target_pairs={{4,0},{5,1},{6,2},{7,3},{8,4},{9,5},{10,6},{11,7},{12,8},{13,9},{1... | collective-permute-start | bytes 12296 | tf_op jit(solution)/shard_map/ppermute | solution.py:21
  147.1 9.2 %collective-permute-start.16 = (f32[8,128]{1,0:T(8,128)S(1)}, f32[8,128]{1,0:T(8,128)S(1)}, u32[]{:S(2)}, u32[]{:S(2)}) collective-permute-start(f32[8,128]{1,0:T(8,128)S(1)} %get-tuple-element.24), channel_id=1, source_target_pairs={{0,4},{1,5},{2,6},{3,7},{4,8},{5,9},{6,10},{7,11},{8,12},{9,13},{1... | collective-permute-start | bytes 12296 | tf_op jit(solution)/shard_map/ppermute | solution.py:21

commit v2 on v1

--- a/solution.py
+++ b/solution.py
@@ -11,10 +11,13 @@
 ROW = 4
 LOW = -4.0
 EPSILON = 1e-06
-VMEM = 40 * 1024 * 1024
+VMEM = 20 * 1024 * 1024
+TAIL = 16
+DIGIT = 32
+BLOCKS, COUNT = 8, 128
 
 OWN, NEXT, PREV, UP, DOWN, UP_NEXT, DOWN_PREV = range(0, 56, 8)
-ONE, LEFT_HALF, EVEN, ODD, EVEN_FIRST, ODD_LAST = range(56, 62)
+ONE, LEFT_HALF, EVEN, ODD, EVEN_FIRST, ODD_LAST, EVEN_BETWEEN, ODD_BETWEEN = range(56, 64)
 
 
 def shifted(array, pairs):
@@ -29,40 +32,57 @@
     return pl.BlockSpec(memory_space=pltpu.VMEM)
 
 
-def unit_kernel(live, embeddings, units):
-    blocks, count, _ = embeddings.shape
+def unit_kernel(cluster, live, embeddings, units):
+    blocks, count, width = embeddings.shape
     position = lax.broadcasted_iota(jnp.int32, (count, 1), 0)
 
     def normalize(b, carry):
         values = embeddings[b].astype(jnp.float32)
         factor = lax.rsqrt(jnp.sum(values * values, axis=-1, keepdims=True) + EPSILON)
         unit = values * factor
-        units[b] = jnp.where(position < live[b], unit, unit[0:1]).astype(jnp.bfloat16)
+        units[pl.ds(pl.multiple_of(b * count, count), count)] = jnp.where(
+            position < live[b], unit, unit[0:1]
+        ).astype(jnp.bfloat16)
         return carry
 
     lax.fori_loop(0, blocks, normalize, 0)
-
-
-def normalize(embeddings, live):
+    rows = lax.broadcasted_iota(jnp.int32, (TAIL, width), 0)
+    columns = lax.broadcasted_iota(jnp.int32, (TAIL, width), 1)
+    digits = jnp.zeros((TAIL, width), jnp.float32)
+    for j in range(blocks):
+        high = lax.div(cluster[j] + 1, DIGIT)
+        low = cluster[j] + 1 - high * DIGIT
+        digit = jnp.where(rows == 0, high, jnp.where(rows == 1, low, 0)).astype(jnp.float32)
+        digits = jnp.where(columns == j, digit, digits)
+    units[blocks * count:blocks * count + TAIL] = digits.astype(jnp.bfloat16)
+
+
+def normalize(embeddings, cluster, live):
+    blocks, count, width = embeddings.shape
     return pl.pallas_call(
         unit_kernel,
-        out_shape=jax.ShapeDtypeStruct(embeddings.shape, jnp.bfloat16),
-        in_specs=[smem(), vmem()],
+        out_shape=jax.ShapeDtypeStruct((blocks * count + TAIL, width), jnp.bfloat16),
+        in_specs=[smem(), smem(), vmem()],
         out_specs=vmem(),
         compiler_params=pltpu.CompilerParams(vmem_limit_bytes=VMEM),
         cost_estimate=pl.CostEstimate(flops=4 * embeddings.size, bytes_accessed=4 * embeddings.size, transcendentals=0),
-    )(live, embeddings)
+    )(cluster, live, embeddings)
+
+
+def ids_of(units, blocks):
+    digits = units[-TAIL:-TAIL + 2, :blocks].astype(jnp.float32)
+    return (digits[0] * DIGIT + digits[1]).astype(jnp.int32)
 
 
 def own_kernel(cluster, live, units, best):
-    blocks, count, width = units.shape
+    blocks, count = best.shape
     rows = lax.broadcasted_iota(jnp.int32, (count, count), 0)
     columns = lax.broadcasted_iota(jnp.int32, (count, count), 1)
-    other = units[...].reshape(blocks * count, width)
+    other = units[:blocks * count]
 
     def chunk(i, carry):
         similar = lax.dot_general(
-            units[pl.ds(2 * i, 2)].reshape(2 * count, width), other,
+            units[pl.ds(pl.multiple_of(2 * i * count, 2 * count), 2 * count)], other,
             (((1,), (1,)), ((), ())), preferred_element_type=jnp.float32,
         )
         for k in range(2):
@@ -81,7 +101,7 @@
 
 
 def own_tile(units, cluster, live):
-    blocks, count, width = units.shape
+    blocks, count, width = BLOCKS, COUNT, units.shape[1]
     return pl.pallas_call(
         own_kernel,
         out_shape=jax.ShapeDtypeStruct((blocks, count), jnp.float32),
@@ -103,8 +123,7 @@
         a_item, a_base, a_offset = parts[first]
         b_item, b_base, b_offset = parts[second]
         a_out, b_out = outs[items.index(a_item)], outs[items.index(b_item)]
-        count, width = a.shape[1], a.shape[2]
-        b_blocks = b.shape[0]
+        count, b_blocks = COUNT, BLOCKS
 
         @pl.when(ids[flag] > 0)
         def _(a=a, b=b, a_out=a_out, b_out=b_out, a_base=a_base, b_base=b_base,
@@ -119,8 +138,7 @@
                 @pl.when(meets)
                 def _():
                     similar = lax.dot_general(
-                        a[pl.ds(2 * i, 2)].reshape(2 * count, width),
-                        b[...].reshape(b_blocks * count, width),
+                        a[pl.ds(pl.multiple_of(2 * i * count, 2 * count), 2 * count)], b[:b_blocks * count],
                         (((1,), (1,)), ((), ())), preferred_element_type=jnp.float32,
                     )
                     tops = [None, None]
@@ -139,7 +157,7 @@
 
                 return carry
 
-            lax.fori_loop(0, a.shape[0] // 2, chunk, 0)
+            lax.fori_loop(0, BLOCKS // 2, chunk, 0)
 
 
 def compare(ids, parts, jobs):
@@ -148,9 +166,8 @@
         if item not in items:
             items.append(item)
     arrays = [part[0] for part in parts]
-    blocks = 8
-    count, width = arrays[0].shape[1], arrays[0].shape[2]
-    flops = sum(2 * arrays[f].shape[0] * arrays[s].shape[0] * count * count * width for f, s, _ in jobs)
+    blocks, count = BLOCKS, COUNT
+    flops = len(jobs) * 2 * (blocks * count) ** 2 * arrays[0].shape[1]
     found = pl.pallas_call(
         functools.partial(pairs_kernel, [part[1:] for part in parts], jobs, items),
         out_shape=[jax.ShapeDtypeStruct((blocks, count), jnp.float32) for _ in items],
@@ -205,29 +222,31 @@
     right, left = ring(devices, 1), ring(devices, -1)
     below, above = column(devices, 1), column(devices, -1)
 
-    line = jnp.stack([
-        block_cluster, shifted(block_cluster, left), shifted(block_cluster, ring(devices, 2)), shifted(block_cluster, right)
-    ])
-    line_up = jnp.where(row > 0, shifted(line, below), -1)
-    line_down = jnp.where(row < last_row, shifted(line, above), -2)
-    down_prev = jnp.where(even_site & (x == 0), line_up[3], jnp.where(~even_site & (x == ROW - 1), line_down[1], line_down[3]))
+    early, late = even_site & (x == 0), ~even_site & (x == ROW - 1)
+    between = (x == 1) | (x == 2)
     flags = jnp.stack([
-        x >= 0, x < 2, even_site, ~even_site, even_site & (x == 0), ~even_site & (x == ROW - 1), x < 0, x < 0
+        x >= 0, x < 2, even_site, ~even_site, early, late, even_site & between, ~even_site & between
     ]).astype(jnp.int32)
-    ids = jnp.concatenate([line[0], line[1], line[3], line_up[0], line_down[0], line_up[1], down_prev, flags])
-
-    units = normalize(embeddings, block_rows)
-    to_down, to_up = shifted(units, below), shifted(units, above)
+
+    units = normalize(embeddings, block_cluster, block_rows)
+    up, down = shifted(units, below), shifted(units, above)
     nxt, prv = shifted(units, left), shifted(units, right)
-    up, down = to_down, to_up
+    best = own_tile(units, block_cluster, block_rows)
+    up, down, nxt, prv, best = lax.optimization_barrier((up, down, nxt, prv, best))
     up_next_even = shifted(up, ring(devices, -1, even))
+    up_next_odd = shifted(nxt, column(devices, 1, odd))
     down_prev_even = shifted(jnp.where(x == ROW - 1, up, down), ring(devices, 1, even))
-    up_next_odd = shifted(nxt, column(devices, 1, odd))
     down_prev_odd = shifted(jnp.where(x == ROW - 1, nxt, prv), column(devices, -1, odd))
-
-    best = own_tile(units, block_cluster, block_rows)
+    near = [ids_of(units, blocks), ids_of(nxt, blocks), ids_of(prv, blocks), ids_of(up, blocks), ids_of(down, blocks)]
+    far = [
+        jnp.where(even_site, ids_of(up_next_even, blocks), ids_of(up_next_odd, blocks)),
+        jnp.where(even_site, ids_of(down_prev_even, blocks), ids_of(down_prev_odd, blocks)),
+    ]
+    near_ids = jnp.concatenate(near + [jnp.zeros((2 * blocks,), jnp.int32), flags])
+    ids = jnp.concatenate(near + far + [flags])
+
     first = compare(
-        ids, [(units, "own", OWN, 0), (nxt, "next", NEXT, 0), (prv, "prev", PREV, 0), (up, "up", UP, 0)],
+        near_ids, [(units, "own", OWN, 0), (nxt, "next", NEXT, 0), (prv, "prev", PREV, 0), (up, "up", UP, 0)],
         [(0, 1, ONE), (1, 2, LEFT_HALF), (0, 3, ONE), (1, 3, ONE), (2, 3, ONE)],
     )
     second = compare(
@@ -238,13 +257,12 @@
             (up_next_odd, "up_next", UP_NEXT, 0), (down_prev_odd, "down_prev", DOWN_PREV, 0),
         ],
         [
-            (0, 3, EVEN), (2, 3, EVEN), (3, 4, EVEN), (2, 4, EVEN_FIRST),
-            (0, 5, ODD), (2, 5, ODD), (5, 6, ODD), (1, 6, ODD_LAST),
+            (0, 3, EVEN), (2, 3, EVEN), (3, 4, EVEN_BETWEEN), (2, 4, EVEN_FIRST),
+            (0, 5, ODD), (2, 5, ODD), (5, 6, ODD_BETWEEN), (1, 6, ODD_LAST),
         ],
     )
     found = merged(first, second)
     none = jnp.full((blocks, count), LOW, jnp.float32)
-    early, late = even_site & (x == 0), ~even_site & (x == ROW - 1)
     from_prev = shifted(
         jnp.stack([found["next"], found["up_next"], jnp.where(late, found["down_prev"], none)]), right
     )

time: 157 us -> 137 us (0.87)
  starting transfers between devices: 40.4 us -> 29.4 us
  waiting for transfers between devices: 68.7 us -> 59.7 us
  Pallas kernels: 39.8 us -> 32.8 us
  other arithmetic: 5.42 us -> 10.2 us
    ppermute x17 -> x12, starting transfers between devices: 40.4 us -> 29.4 us  [shifted(): return lax.ppermute(array, AXES, pairs)]
    ppermute x17 -> x12, waiting for transfers between devices: 68.7 us -> 59.7 us  [shifted(): return lax.ppermute(array, AXES, pairs)]
    pallas_call x2, Pallas kernels: 31.5 us -> 24.4 us  [compare(): pl.pallas_call(functools.partial(pairs_kernel, [part[1:] for part in part...]
    convert_element_type x1 -> x13, other arithmetic: 0.01 us -> 4.68 us  [the longest x7 4.64 us: ids_of(): digits = units[-TAIL:-TAIL + 2, :blocks].astype(jnp.float32)]
    select_n x1, other arithmetic: 1.55 us -> 3.16 us  [body(): jnp.where(x == ROW - 1, up, down)]
  transfers between devices with their start and end apart: 17 -> 12, of which waited for: 8 -> 7; matrix products, arithmetic and copies ran while one was open for 3% -> 5% of each run, Pallas kernels for 16% -> 11%
where the time goes in v2:
time: 137 us; the launch traced here: 136 us
  waiting for transfers between devices  59.7 us (44%)
  Pallas kernels  32.8 us (24%)
  starting transfers between devices  29.4 us (21%)
  other arithmetic  10.2 us (7%)
  local copies, waits for them, and re-layouts  3.18 us (2%)
    ppermute x12, waiting for transfers between devices, shifted(): return lax.ppermute(array, AXES, pairs)  59.7 us
    ppermute x12, starting transfers between devices, shifted(): return lax.ppermute(array, AXES, pairs)  29.4 us
    pallas_call x2, Pallas kernels, compare(): pl.pallas_call(functools.partial(pairs_kernel, [part[1:] for part in part...  24.4 us
    pallas_call x1, Pallas kernels, own_tile(): pl.pallas_call(own_kernel, out_shape=jax.ShapeDtypeStruct((blocks, count)...  5.28 us
    convert_element_type x7, other arithmetic, ids_of(): digits = units[-TAIL:-TAIL + 2, :blocks].astype(jnp.float32)  4.64 us
    select_n x1, other arithmetic, body(): jnp.where(x == ROW - 1, up, down)  3.16 us
    pallas_call x1, Pallas kernels, normalize(): pl.pallas_call(unit_kernel, out_shape=jax.ShapeDtypeStruct((blocks * coun...  3.16 us
    unnamed x10, local copies, waits for them, and re-layouts  2.91 us
  transfers between devices with their start and end apart: 12, of which 7 were waited for; matrix products, arithmetic and copies ran while one was open for 5% of the time, Pallas kernels for 11%

profile of v2, /device:TPU:32, one launch (start us, length us, event | category | flops | bytes accessed | tf_op | source)
XLA Modules:
  0.0 135.5 jit_solution(6737923383609811092)
XLA Ops:
  0.0 0.0 copy-start
  0.0 1.6 %copy-done = bf16[8,128,1024]{2,1,0:T(8,128)(2,1)S(1)} copy-done((bf16[8,128,1024]{2,1,0:T(8,128)(2,1)S(1)}, bf16[8,128,1024]{2,1,0:T(8,128)(2,1)}, u32[]{:S(2)}) %copy-start) | copy-done | bytes 2097176
  1.6 0.0 copy-start.1
  1.6 0.7 copy-done.1
  2.2 0.7 copy-done.3
  2.9 3.2 %shard_map.37.units.refs_0_ = bf16[1040,1024]{1,0:T(8,128)(2,1)} custom-call(s32[8]{0:T(128)S(1)} %copy-done.3, s32[8]{0:T(128)S(1)} %copy-done.1, bf16[8,128,1024]{2,1,0:T(8,128)(2,1)S(1)} %copy-done), custom_call_target="tpu_custom_call" | custom-call | flops 4194304 | bytes 4194304 | tf_op jit(solution)/shard_map/pallas_call | solution.py:62
  6.1 1.5 %collective-permute-start.3 = (bf16[1040,1024]{1,0:T(8,128)(2,1)}, bf16[1040,1024]{1,0:T(8,128)(2,1)S(1)}, u32[]{:S(2)}, u32[]{:S(2)}) collective-permute-start(bf16[1040,1024]{1,0:T(8,128)(2,1)} %shard_map.37.units.refs_0_), channel_id=1, source_target_pairs={{0,1},{1,2},{2,3},{3,0},{4,5},{5,6},{6,7},{7,4},{8,9},{9,10},{10,1... | collective-permute-start | bytes 6389768 | tf_op jit(solution)/shard_map/ppermute | solution.py:24
  7.6 1.7 %collective-permute-start.2 = (bf16[1040,1024]{1,0:T(8,128)(2,1)}, bf16[1040,1024]{1,0:T(8,128)(2,1)}, u32[]{:S(2)}, u32[]{:S(2)}) collective-permute-start(bf16[1040,1024]{1,0:T(8,128)(2,1)} %shard_map.37.units.refs_0_), channel_id=1, source_target_pairs={{0,3},{1,0},{2,1},{3,2},{4,7},{5,4},{6,5},{7,6},{8,11},{9,8},{10,9... | collective-permute-start | bytes 6389768 | tf_op jit(solution)/shard_map/ppermute | solution.py:24
  9.3 1.9 %collective-permute-start.1 = (bf16[1040,1024]{1,0:T(8,128)(2,1)}, bf16[1040,1024]{1,0:T(8,128)(2,1)}, u32[]{:S(2)}, u32[]{:S(2)}) collective-permute-start(bf16[1040,1024]{1,0:T(8,128)(2,1)} %shard_map.37.units.refs_0_), channel_id=1, source_target_pairs={{4,0},{5,1},{6,2},{7,3},{8,4},{9,5},{10,6},{11,7},{12,8},{13,9},{1... | collective-permute-start | bytes 6389768 | tf_op jit(solution)/shard_map/ppermute | solution.py:24
  11.2 3.9 %collective-permute-start = (bf16[1040,1024]{1,0:T(8,128)(2,1)}, bf16[1040,1024]{1,0:T(8,128)(2,1)}, u32[]{:S(2)}, u32[]{:S(2)}) collective-permute-start(bf16[1040,1024]{1,0:T(8,128)(2,1)} %shard_map.37.units.refs_0_), channel_id=1, source_target_pairs={{0,4},{1,5},{2,6},{3,7},{4,8},{5,9},{6,10},{7,11},{8,12},{9,13},{1... | collective-permute-start | bytes 6389768 | tf_op jit(solution)/shard_map/ppermute | solution.py:24
  15.2 0.1 stack.59
  15.3 0.0 copy-done.2
  15.3 0.0 copy-done.4
  15.3 5.3 %shard_map.38 = f32[8,128]{1,0:T(8,128)S(1)} custom-call(s32[8]{0:T(128)S(1)} %copy-done.4, s32[8]{0:T(128)S(1)} %copy-done.2, bf16[1040,1024]{1,0:T(8,128)(2,1)} %shard_map.37.units.refs_0_), custom_call_target="tpu_custom_call" | custom-call | flops 2147483648 | bytes 2097152 | tf_op jit(solution)/shard_map/pallas_call | solution.py:105
  20.6 0.7 slice_convert_fusion.4
  21.3 34.3 %collective-permute-done.3.refs_2_.refs_0_ = bf16[1040,1024]{1,0:T(8,128)(2,1)S(1)} collective-permute-done((bf16[1040,1024]{1,0:T(8,128)(2,1)}, bf16[1040,1024]{1,0:T(8,128)(2,1)S(1)}, u32[]{:S(2)}, u32[]{:S(2)}) %collective-permute-start.3) | collective-permute-done | bytes 2129952 | tf_op jit(solution)/shard_map/ppermute | solution.py:24
  55.6 0.1 collective-permute-done.2.refs_1_
  55.7 3.5 %collective-permute-done.1.refs_2_ = bf16[1040,1024]{1,0:T(8,128)(2,1)} collective-permute-done((bf16[1040,1024]{1,0:T(8,128)(2,1)}, bf16[1040,1024]{1,0:T(8,128)(2,1)}, u32[]{:S(2)}, u32[]{:S(2)}) %collective-permute-start.1) | collective-permute-done | bytes 2129952 | tf_op jit(solution)/shard_map/ppermute | solution.py:24
  59.2 1.9 %collective-permute-done.refs_3_.refs_1_ = bf16[1040,1024]{1,0:T(8,128)(2,1)} collective-permute-done((bf16[1040,1024]{1,0:T(8,128)(2,1)}, bf16[1040,1024]{1,0:T(8,128)(2,1)}, u32[]{:S(2)}, u32[]{:S(2)}) %collective-permute-start) | collective-permute-done | bytes 2129952 | tf_op jit(solution)/shard_map/ppermute | solution.py:24
  61.1 1.6 %broadcast_select_fusion = bf16[1040,1024]{1,0:T(8,128)(2,1)} fusion(bf16[1040,1024]{1,0:T(8,128)(2,1)} %collective-permute-done.2.refs_1_, bf16[1040,1024]{1,0:T(8,128)(2,1)S(1)} %collective-permute-done.3.refs_2_.refs_0_, pred[]{:T(512)S(6)} %eq.22), kind=kLoop, calls=%fused_computation | loop fusion | flops 1064960 | bytes 6389761 | tf_op jit(solution)/shard_map/jit(_where)/select_n | solution.py:239
  62.6 2.0 %collective-permute-start.7 = (bf16[1040,1024]{1,0:T(8,128)(2,1)}, bf16[1040,1024]{1,0:T(8,128)(2,1)}, u32[]{:S(2)}, u32[]{:S(2)}) collective-permute-start(bf16[1040,1024]{1,0:T(8,128)(2,1)} %broadcast_select_fusion), channel_id=1, source_target_pairs={{20,16},{21,17},{22,18},{23,19},{24,20},{25,21},{26,22},{27,23},{2... | collective-permute-start | bytes 6389768 | tf_op jit(solution)/shard_map/ppermute | solution.py:24
  64.7 3.2 %broadcast_select_fusion.1 = bf16[1040,1024]{1,0:T(8,128)(2,1)} fusion(bf16[1040,1024]{1,0:T(8,128)(2,1)} %collective-permute-done.refs_3_.refs_1_, bf16[1040,1024]{1,0:T(8,128)(2,1)} %collective-permute-done.1.refs_2_, pred[]{:T(512)S(6)} %eq.22), kind=kLoop, calls=%fused_computation.1 | loop fusion | flops 1064960 | bytes 6389761 | tf_op jit(solution)/shard_map/jit(_where)/select_n | solution.py:238
  67.8 0.7 slice_convert_fusion.5
  68.5 2.0 %collective-permute-start.5 = (bf16[1040,1024]{1,0:T(8,128)(2,1)}, bf16[1040,1024]{1,0:T(8,128)(2,1)}, u32[]{:S(2)}, u32[]{:S(2)}) collective-permute-start(bf16[1040,1024]{1,0:T(8,128)(2,1)} %collective-permute-done.2.refs_1_), channel_id=1, source_target_pairs={{12,16},{13,17},{14,18},{15,19},{16,20},{17,21},{18,22},{19,23},{2... | collective-permute-start | bytes 6389768 | tf_op jit(solution)/shard_map/ppermute | solution.py:24
  70.5 5.2 %collective-permute-start.4 = (bf16[1040,1024]{1,0:T(8,128)(2,1)}, bf16[1040,1024]{1,0:T(8,128)(2,1)}, u32[]{:S(2)}, u32[]{:S(2)}) collective-permute-start(bf16[1040,1024]{1,0:T(8,128)(2,1)} %collective-permute-done.refs_3_.refs_1_), channel_id=1, source_target_pairs={{0,3},{1,0},{2,1},{3,2},{4,7},{5,4},{6,5},{7,6},{8,11},{9,8},{10,9... | collective-permute-start | bytes 6389768 | tf_op jit(solution)/shard_map/ppermute | solution.py:24
  75.8 1.9 %collective-permute-start.6 = (bf16[1040,1024]{1,0:T(8,128)(2,1)}, bf16[1040,1024]{1,0:T(8,128)(2,1)}, u32[]{:S(2)}, u32[]{:S(2)}) collective-permute-start(bf16[1040,1024]{1,0:T(8,128)(2,1)} %broadcast_select_fusion.1), channel_id=1, source_target_pairs={{0,1},{1,2},{2,3},{3,0},{4,5},{5,6},{6,7},{7,4},{8,9},{9,10},{10,1... | collective-permute-start | bytes 6389768 | tf_op jit(solution)/shard_map/ppermute | solution.py:24
  77.7 0.7 slice_convert_fusion.7
  78.4 0.1 concatenate.6.ids
  78.5 9.7 %shard_map.39 = (f32[8,128]{1,0:T(8,128)S(1)}, f32[8,128]{1,0:T(8,128)S(1)}, f32[8,128]{1,0:T(8,128)S(1)}, f32[8,128]{1,0:T(8,128)S(1)}) custom-call(s32[64]{0:T(128)S(1)} %concatenate.6.ids, bf16[1040,1024]{1,0:T(8,128)(2,1)} %shard_map.37.units.refs_0_, bf16[1040,1024]{1,0:T(8,128)(2,1)} %collective-permute-done.2.refs_1_, ...), custom_call_target="tpu_custom_call" | custom-call | flops 10737418240 | bytes 8519680 | tf_op jit(solution)/shard_map/pallas_call | solution.py:171
  88.2 0.0 collective-permute-done.7.refs_6_
  88.2 0.6 slice_convert_fusion
  88.8 16.7 %collective-permute-done.6.refs_4_ = bf16[1040,1024]{1,0:T(8,128)(2,1)} collective-permute-done((bf16[1040,1024]{1,0:T(8,128)(2,1)}, bf16[1040,1024]{1,0:T(8,128)(2,1)}, u32[]{:S(2)}, u32[]{:S(2)}) %collective-permute-start.6) | collective-permute-done | bytes 2129952 | tf_op jit(solution)/shard_map/ppermute | solution.py:24
  105.6 0.7 slice_convert_fusion.1
  106.3 0.0 collective-permute-done.5.refs_5_
  106.3 0.7 slice_convert_fusion.2
  107.0 0.0 collective-permute-done.4.refs_3_
  107.0 0.6 slice_convert_fusion.3
  107.6 0.1 concatenate.7.ids
  107.7 14.7 %shard_map.40 = (f32[8,128]{1,0:T(8,128)S(1)}, f32[8,128]{1,0:T(8,128)S(1)}, f32[8,128]{1,0:T(8,128)S(1)}, f32[8,128]{1,0:T(8,128)S(1)}, f32[8,128]{1,0:T(8,128)S(1)}) custom-call(s32[64]{0:T(128)S(1)} %concatenate.7.ids, bf16[1040,1024]{1,0:T(8,128)(2,1)S(1)} %collective-permute-done.3.refs_2_.refs_0_, ...), custom_call_target="tpu_custom_call" | custom-call | flops 17179869184 | bytes 14909440 | tf_op jit(solution)/shard_map/pallas_call | solution.py:171
  122.4 0.1 collective-permute-start.8
  122.5 3.2 %collective-permute-start.9 = (f32[3,8,128]{2,1,0:T(8,128)S(1)}, f32[3,8,128]{2,1,0:T(8,128)S(1)}, u32[]{:S(2)}, u32[]{:S(2)}) collective-permute-start(f32[3,8,128]{2,1,0:T(8,128)S(1)} %pad_maximum_fusion.1), channel_id=1, source_target_pairs={{0,3},{1,0},{2,1},{3,2},{4,7},{5,4},{6,5},{7,6},{8,11},{9,8},{10,9... | collective-permute-start | bytes 36872 | tf_op jit(solution)/shard_map/ppermute | solution.py:24
  125.7 1.7 %collective-permute-done.8 = f32[3,8,128]{2,1,0:T(8,128)S(1)} collective-permute-done((f32[3,8,128]{2,1,0:T(8,128)S(1)}, f32[3,8,128]{2,1,0:T(8,128)S(1)}, u32[]{:S(2)}, u32[]{:S(2)}) %collective-permute-start.8) | collective-permute-done | bytes 12320 | tf_op jit(solution)/shard_map/ppermute | solution.py:24
  127.4 0.0 collective-permute-done.9
  127.4 1.9 %collective-permute-start.10 = (f32[8,128]{1,0:T(8,128)S(1)}, f32[8,128]{1,0:T(8,128)S(1)}, u32[]{:S(2)}, u32[]{:S(2)}) collective-permute-start(f32[8,128]{1,0:T(8,128)S(1)} %get-tuple-element.33), channel_id=1, source_target_pairs={{4,0},{5,1},{6,2},{7,3},{8,4},{9,5},{10,6},{11,7},{12,8},{13,9},{1... | collective-permute-start | bytes 12296 | tf_op jit(solution)/shard_map/ppermute | solution.py:24
  129.3 3.9 %collective-permute-start.11 = (f32[8,128]{1,0:T(8,128)S(1)}, f32[8,128]{1,0:T(8,128)S(1)}, u32[]{:S(2)}, u32[]{:S(2)}) collective-permute-start(f32[8,128]{1,0:T(8,128)S(1)} %get-tuple-element.34), channel_id=1, source_target_pairs={{0,4},{1,5},{2,6},{3,7},{4,8},{5,9},{6,10},{7,11},{8,12},{9,13},{1... | collective-permute-start | bytes 12296 | tf_op jit(solution)/shard_map/ppermute | solution.py:24
  133.3 0.0 collective-permute-done.10
  133.3 1.5 %collective-permute-done.11 = f32[8,128]{1,0:T(8,128)S(1)} collective-permute-done((f32[8,128]{1,0:T(8,128)S(1)}, f32[8,128]{1,0:T(8,128)S(1)}, u32[]{:S(2)}, u32[]{:S(2)}) %collective-permute-start.11) | collective-permute-done | bytes 4128 | tf_op jit(solution)/shard_map/ppermute | solution.py:24
  134.8 0.7 fusion.8
  (18 shorter events, 0.1 us)
Async XLA Ops:
  0.0 1.6 %copy-start = (bf16[8,128,1024]{2,1,0:T(8,128)(2,1)S(1)}, bf16[8,128,1024]{2,1,0:T(8,128)(2,1)}, u32[]{:S(2)}) copy-start(bf16[8,128,1024]{2,1,0:T(8,128)(2,1)} %embeddings.1) | copy-start | bytes 6291460
  1.6 0.7 copy-start.1
  2.2 0.7 copy-start.3
  2.9 12.4 %copy-start.2 = (s32[8]{0:T(128)S(1)}, s32[8]{0:T(128)}, u32[]{:S(2)}) copy-start(s32[8]{0:T(128)} %live.3) | copy-start | bytes 100
  2.9 12.4 %copy-start.4 = (s32[8]{0:T(128)S(1)}, s32[8]{0:T(128)}, u32[]{:S(2)}) copy-start(s32[8]{0:T(128)} %cluster.3) | copy-start | bytes 100
  6.1 49.5 %collective-permute-start.3 = (bf16[1040,1024]{1,0:T(8,128)(2,1)}, bf16[1040,1024]{1,0:T(8,128)(2,1)S(1)}, u32[]{:S(2)}, u32[]{:S(2)}) collective-permute-start(bf16[1040,1024]{1,0:T(8,128)(2,1)} %shard_map.37.units.refs_0_), channel_id=1, source_target_pairs={{0,1},{1,2},{2,3},{3,0},{4,5},{5,6},{6,7},{7,4},{8,9},{9,10},{10,1... | collective-permute-start | bytes 6389768 | tf_op jit(solution)/shard_map/ppermute | solution.py:24
  7.6 48.1 %collective-permute-start.2 = (bf16[1040,1024]{1,0:T(8,128)(2,1)}, bf16[1040,1024]{1,0:T(8,128)(2,1)}, u32[]{:S(2)}, u32[]{:S(2)}) collective-permute-start(bf16[1040,1024]{1,0:T(8,128)(2,1)} %shard_map.37.units.refs_0_), channel_id=1, source_target_pairs={{0,3},{1,0},{2,1},{3,2},{4,7},{5,4},{6,5},{7,6},{8,11},{9,8},{10,9... | collective-permute-start | bytes 6389768 | tf_op jit(solution)/shard_map/ppermute | solution.py:24
  9.3 49.9 %collective-permute-start.1 = (bf16[1040,1024]{1,0:T(8,128)(2,1)}, bf16[1040,1024]{1,0:T(8,128)(2,1)}, u32[]{:S(2)}, u32[]{:S(2)}) collective-permute-start(bf16[1040,1024]{1,0:T(8,128)(2,1)} %shard_map.37.units.refs_0_), channel_id=1, source_target_pairs={{4,0},{5,1},{6,2},{7,3},{8,4},{9,5},{10,6},{11,7},{12,8},{13,9},{1... | collective-permute-start | bytes 6389768 | tf_op jit(solution)/shard_map/ppermute | solution.py:24
  11.2 49.8 %collective-permute-start = (bf16[1040,1024]{1,0:T(8,128)(2,1)}, bf16[1040,1024]{1,0:T(8,128)(2,1)}, u32[]{:S(2)}, u32[]{:S(2)}) collective-permute-start(bf16[1040,1024]{1,0:T(8,128)(2,1)} %shard_map.37.units.refs_0_), channel_id=1, source_target_pairs={{0,4},{1,5},{2,6},{3,7},{4,8},{5,9},{6,10},{7,11},{8,12},{9,13},{1... | collective-permute-start | bytes 6389768 | tf_op jit(solution)/shard_map/ppermute | solution.py:24
  62.6 25.6 %collective-permute-start.7 = (bf16[1040,1024]{1,0:T(8,128)(2,1)}, bf16[1040,1024]{1,0:T(8,128)(2,1)}, u32[]{:S(2)}, u32[]{:S(2)}) collective-permute-start(bf16[1040,1024]{1,0:T(8,128)(2,1)} %broadcast_select_fusion), channel_id=1, source_target_pairs={{20,16},{21,17},{22,18},{23,19},{24,20},{25,21},{26,22},{27,23},{2... | collective-permute-start | bytes 6389768 | tf_op jit(solution)/shard_map/ppermute | solution.py:24
  68.5 37.8 %collective-permute-start.5 = (bf16[1040,1024]{1,0:T(8,128)(2,1)}, bf16[1040,1024]{1,0:T(8,128)(2,1)}, u32[]{:S(2)}, u32[]{:S(2)}) collective-permute-start(bf16[1040,1024]{1,0:T(8,128)(2,1)} %collective-permute-done.2.refs_1_), channel_id=1, source_target_pairs={{12,16},{13,17},{14,18},{15,19},{16,20},{17,21},{18,22},{19,23},{2... | collective-permute-start | bytes 6389768 | tf_op jit(solution)/shard_map/ppermute | solution.py:24
  70.5 36.4 %collective-permute-start.4 = (bf16[1040,1024]{1,0:T(8,128)(2,1)}, bf16[1040,1024]{1,0:T(8,128)(2,1)}, u32[]{:S(2)}, u32[]{:S(2)}) collective-permute-start(bf16[1040,1024]{1,0:T(8,128)(2,1)} %collective-permute-done.refs_3_.refs_1_), channel_id=1, source_target_pairs={{0,3},{1,0},{2,1},{3,2},{4,7},{5,4},{6,5},{7,6},{8,11},{9,8},{10,9... | collective-permute-start | bytes 6389768 | tf_op jit(solution)/shard_map/ppermute | solution.py:24
  75.8 29.8 %collective-permute-start.6 = (bf16[1040,1024]{1,0:T(8,128)(2,1)}, bf16[1040,1024]{1,0:T(8,128)(2,1)}, u32[]{:S(2)}, u32[]{:S(2)}) collective-permute-start(bf16[1040,1024]{1,0:T(8,128)(2,1)} %broadcast_select_fusion.1), channel_id=1, source_target_pairs={{0,1},{1,2},{2,3},{3,0},{4,5},{5,6},{6,7},{7,4},{8,9},{9,10},{10,1... | collective-permute-start | bytes 6389768 | tf_op jit(solution)/shard_map/ppermute | solution.py:24
  122.4 5.0 %collective-permute-start.8 = (f32[3,8,128]{2,1,0:T(8,128)S(1)}, f32[3,8,128]{2,1,0:T(8,128)S(1)}, u32[]{:S(2)}, u32[]{:S(2)}) collective-permute-start(f32[3,8,128]{2,1,0:T(8,128)S(1)} %pad_maximum_fusion), channel_id=1, source_target_pairs={{0,1},{1,2},{2,3},{3,0},{4,5},{5,6},{6,7},{7,4},{8,9},{9,10},{10,1... | collective-permute-start | bytes 36872 | tf_op jit(solution)/shard_map/ppermute | solution.py:24
  122.5 4.9 %collective-permute-start.9 = (f32[3,8,128]{2,1,0:T(8,128)S(1)}, f32[3,8,128]{2,1,0:T(8,128)S(1)}, u32[]{:S(2)}, u32[]{:S(2)}) collective-permute-start(f32[3,8,128]{2,1,0:T(8,128)S(1)} %pad_maximum_fusion.1), channel_id=1, source_target_pairs={{0,3},{1,0},{2,1},{3,2},{4,7},{5,4},{6,5},{7,6},{8,11},{9,8},{10,9... | collective-permute-start | bytes 36872 | tf_op jit(solution)/shard_map/ppermute | solution.py:24
  127.4 5.9 %collective-permute-start.10 = (f32[8,128]{1,0:T(8,128)S(1)}, f32[8,128]{1,0:T(8,128)S(1)}, u32[]{:S(2)}, u32[]{:S(2)}) collective-permute-start(f32[8,128]{1,0:T(8,128)S(1)} %get-tuple-element.33), channel_id=1, source_target_pairs={{4,0},{5,1},{6,2},{7,3},{8,4},{9,5},{10,6},{11,7},{12,8},{13,9},{1... | collective-permute-start | bytes 12296 | tf_op jit(solution)/shard_map/ppermute | solution.py:24
  129.3 5.5 %collective-permute-start.11 = (f32[8,128]{1,0:T(8,128)S(1)}, f32[8,128]{1,0:T(8,128)S(1)}, u32[]{:S(2)}, u32[]{:S(2)}) collective-permute-start(f32[8,128]{1,0:T(8,128)S(1)} %get-tuple-element.34), channel_id=1, source_target_pairs={{0,4},{1,5},{2,6},{3,7},{4,8},{5,9},{6,10},{7,11},{8,12},{9,13},{1... | collective-permute-start | bytes 12296 | tf_op jit(solution)/shard_map/ppermute | solution.py:24

commit v3 on v2

v3 whole, which is shorter than its diff:
```python
import functools

import jax
import jax.numpy as jnp
from jax import lax
from jax.experimental import pallas as pl
from jax.experimental.pallas import tpu as pltpu
from jax.sharding import PartitionSpec as P

AXES = ("gx", "gy")
ROW = 4
LOW = -4.0
EPSILON = 1e-06
VMEM = 60 * 1024 * 1024
TAIL = 16
DIGIT = 32
BLOCKS, COUNT = 8, 128

ONE, LEFT_HALF, EVEN, ODD, EVEN_FIRST, ODD_LAST, EVEN_BETWEEN, ODD_BETWEEN, EVEN_LEFT, ODD_LEFT = range(10)


def shifted(array, pairs):
    return lax.ppermute(array, AXES, pairs)


def smem():
    return pl.BlockSpec(memory_space=pltpu.SMEM)


def anywhere():
    return pl.BlockSpec(memory_space=pl.ANY)


def vmem():
    return pl.BlockSpec(memory_space=pltpu.VMEM)


def unit_kernel(cluster_in, live_in, embeddings, out, given, units, cluster, live, small, arrive, leave):
    blocks, count, width = given.shape
    scalars = [
        pltpu.make_async_copy(cluster_in, cluster, small.at[0]), pltpu.make_async_copy(live_in, live, small.at[1])
    ]
    reads = [pltpu.make_async_copy(embeddings.at[b], given.at[b], arrive.at[b]) for b in range(blocks)]
    spans = [pl.ds(b * count, count) for b in range(blocks)] + [pl.ds(blocks * count, TAIL)]
    writes = [pltpu.make_async_copy(units.at[span], out.at[span], leave.at[b]) for b, span in enumerate(spans)]
    for copy in scalars + reads:
        copy.start()
    for copy in scalars:
        copy.wait()
    rows = lax.broadcasted_iota(jnp.int32, (TAIL, width), 0)
    columns = lax.broadcasted_iota(jnp.int32, (TAIL, width), 1)
    digits = jnp.zeros((TAIL, width), jnp.float32)
    for j in range(blocks):
        high = lax.div(cluster[j] + 1, DIGIT)
        low = cluster[j] + 1 - high * DIGIT
        digit = jnp.where(rows == 0, high, jnp.where(rows == 1, low, 0)).astype(jnp.float32)
        digits = jnp.where(columns == j, digit, digits)
    units[spans[blocks]] = digits.astype(jnp.bfloat16)
    writes[blocks].start()
    position = lax.broadcasted_iota(jnp.int32, (count, 1), 0)
    for b in range(blocks):
        reads[b].wait()
        values = given[b].astype(jnp.float32)
        factor = lax.rsqrt(jnp.sum(values * values, axis=-1, keepdims=True) + EPSILON)
        unit = values * factor
        units[spans[b]] = jnp.where(position < live[b], unit, unit[0:1]).astype(jnp.bfloat16)
        writes[b].start()
    for copy in writes:
        copy.wait()


def normalize(embeddings, cluster, live):
    blocks, count, width = embeddings.shape
    return pl.pallas_call(
        unit_kernel,
        out_shape=jax.ShapeDtypeStruct((blocks * count + TAIL, width), jnp.bfloat16),
        in_specs=[anywhere()] * 3,
        out_specs=anywhere(),
        scratch_shapes=[
            pltpu.VMEM(embeddings.shape, jnp.bfloat16),
            pltpu.VMEM((blocks * count + TAIL, width), jnp.bfloat16),
            pltpu.SMEM((blocks,), jnp.int32),
            pltpu.SMEM((blocks,), jnp.int32),
            pltpu.SemaphoreType.DMA((2,)),
            pltpu.SemaphoreType.DMA((blocks,)),
            pltpu.SemaphoreType.DMA((blocks + 1,)),
        ],
        compiler_params=pltpu.CompilerParams(vmem_limit_bytes=VMEM),
        cost_estimate=pl.CostEstimate(flops=4 * embeddings.size, bytes_accessed=4 * embeddings.size, transcendentals=0),
    )(cluster, live, embeddings)


def own_kernel(cluster, live, units, best):
    blocks, count = best.shape
    rows = lax.broadcasted_iota(jnp.int32, (count, count), 0)
    columns = lax.broadcasted_iota(jnp.int32, (count, count), 1)
    other = units[:blocks * count]

    def chunk(i, carry):
        similar = lax.dot_general(
            units[pl.ds(pl.multiple_of(2 * i * count, 2 * count), 2 * count)], other,
            (((1,), (1,)), ((), ())), preferred_element_type=jnp.float32,
        )
        for k in range(2):
            a = 2 * i + k
            top = None
            for j in range(blocks):
                part = similar[k * count:(k + 1) * count, j * count:(j + 1) * count]
                part = part + jnp.where(cluster[a] == cluster[j], 0.0, LOW)
                hidden = (a == j) & ((rows == columns) | (columns >= live[j]))
                part = jnp.where(hidden, LOW, part)
                top = part if top is None else jnp.maximum(top, part)
            best[pl.ds(a, 1)] = jnp.max(top.T, axis=0, keepdims=True)
        return carry

    lax.fori_loop(0, blocks // 2, chunk, 0)


def own_tile(units, cluster, live):
    blocks, count, width = BLOCKS, COUNT, units.shape[1]
    return pl.pallas_call(
        own_kernel,
        out_shape=jax.ShapeDtypeStruct((blocks, count), jnp.float32),
        in_specs=[smem(), smem(), vmem()],
        out_specs=vmem(),
        compiler_params=pltpu.CompilerParams(vmem_limit_bytes=VMEM),
        cost_estimate=pl.CostEstimate(
            flops=2 * (blocks * count) ** 2 * width, bytes_accessed=2 * blocks * count * width, transcendentals=0
        ),
    )(cluster, live, units)


def pairs_kernel(parts, jobs, items, begun, flags, *refs):
    many = len(parts)
    arrays, refs = refs[:many], refs[many:]
    starts, refs = refs[:len(begun)], refs[len(begun):]
    outs, refs = refs[:len(items)], refs[len(items):]
    held, refs = refs[:many], refs[many:]
    tails, listed, ids, arrived, came, moved, seen, rows_best = refs
    count = COUNT
    ends = [
        pltpu.make_async_copy(arrays[i].at[pl.ds(BLOCKS * count, TAIL), pl.ds(0, 128)], tails.at[i], came.at[i])
        for i in range(many)
    ]
    copies = [
        pltpu.make_async_copy(arrays[i].at[pl.ds(0, BLOCKS * count)], held[i], arrived.at[i]) for i in range(many)
    ]
    for end in ends:
        end.start()
    for item, out in zip(items, outs):
        if item in begun:
            out[...] = starts[begun.index(item)][...]
        else:
            out[...] = jnp.full(out.shape, LOW, jnp.float32)
    for i, end in enumerate(ends):
        end.wait()
        digits = tails[i].astype(jnp.float32)
        listed[i:i + 1] = (digits[0:1] * DIGIT + digits[1:2]).astype(jnp.int32)
    move = pltpu.make_async_copy(listed, ids, moved.at[0])
    move.start()
    move.wait()
    wanted, needed = [], [jnp.bool_(False)] * many
    for first, second, flag in jobs:
        want = (flags[flag] > 0) & (ids[first, BLOCKS - 1] >= ids[second, 0])
        want = want & (ids[first, 0] <= ids[second, BLOCKS - 1])
        wanted.append(want)
        for i in (first, second):
            needed[i] = needed[i] | want
    for i in range(many):
        seen[i] = 0
        pl.when(needed[i])(copies[i].start)
    for (first, second, _), want in zip(jobs, wanted):

        @pl.when(want)
        def _(first=first, second=second):
            for i in (first, second):

                @pl.when(seen[i] == 0)
                def _(i=i):
                    copies[i].wait()
                    seen[i] = 1

            a, b = held[first], held[second]
            a_out, b_out = outs[items.index(parts[first])], outs[items.index(parts[second])]
            tops = rows_best
            tops[...] = jnp.full(tops.shape, LOW, jnp.float32)

            def chunk(i, carry):
                low, high = ids[second, 2 * i], ids[second, 2 * i + 1]
                meets = (high >= ids[first, 0]) & (low <= ids[first, BLOCKS - 1])
                same = (low == high) & (ids[first, 0] == low) & (ids[first, BLOCKS - 1] == low)

                def work(hide):
                    similar = lax.dot_general(
                        a[...], b[pl.ds(pl.multiple_of(2 * i * count, 2 * count), 2 * count)],
                        (((1,), (1,)), ((), ())), preferred_element_type=jnp.float32,
                    )
                    columns = [None, None]
                    for j in range(BLOCKS):
                        here = slice(j * count, (j + 1) * count)
                        top = tops[here]
                        for k in range(2):
                            part = similar[here, k * count:(k + 1) * count]
                            if hide:
                                part = part + jnp.where(ids[first, j] == ids[second, 2 * i + k], 0.0, LOW)
                            top = jnp.maximum(top, part)
                            part = jnp.max(part.reshape(count // 8, 8, count), axis=0)
                            columns[k] = part if columns[k] is None else jnp.maximum(columns[k], part)
                        tops[here] = top
                    for k in range(2):
                        here = pl.ds(2 * i + k, 1)
                        b_out[here] = jnp.maximum(b_out[here], jnp.max(columns[k], axis=0, keepdims=True))

                pl.when(same)(lambda: work(False))
                pl.when(meets & jnp.logical_not(same))(lambda: work(True))
                return carry

            lax.fori_loop(0, BLOCKS // 2, chunk, 0)
            for j in range(BLOCKS):
                top = jnp.max(tops[j * count:(j + 1) * count].T, axis=0, keepdims=True)
                a_out[j:j + 1] = jnp.maximum(a_out[j:j + 1], top)


def compare(flags, parts, jobs, begun):
    items = []
    for _, item in parts:
        if item not in items:
            items.append(item)
    known = [item for item in items if item in begun]
    arrays = [part[0] for part in parts]
    many, width = len(arrays), arrays[0].shape[1]
    found = pl.pallas_call(
        functools.partial(pairs_kernel, [part[1] for part in parts], jobs, items, known),
        out_shape=[jax.ShapeDtypeStruct((BLOCKS, COUNT), jnp.float32) for _ in items],
        in_specs=[smem()] + [anywhere() for _ in arrays] + [vmem() for _ in known],
        out_specs=[vmem() for _ in items],
        scratch_shapes=[pltpu.VMEM((BLOCKS * COUNT, width), jnp.bfloat16) for _ in arrays]
        + [
            pltpu.VMEM((many, TAIL, 128), jnp.bfloat16),
            pltpu.VMEM((8, 128), jnp.int32),
            pltpu.SMEM((8, 128), jnp.int32),
            pltpu.SemaphoreType.DMA((many,)),
            pltpu.SemaphoreType.DMA((many,)),
            pltpu.SemaphoreType.DMA((1,)),
            pltpu.SMEM((many,), jnp.int32),
            pltpu.VMEM((BLOCKS * COUNT, COUNT), jnp.float32),
        ],
        compiler_params=pltpu.CompilerParams(vmem_limit_bytes=VMEM),
        cost_estimate=pl.CostEstimate(
            flops=len(jobs) * 2 * (BLOCKS * COUNT) ** 2 * width,
            bytes_accessed=sum(2 * a.size for a in arrays), transcendentals=0,
        ),
    )(flags, *arrays, *[begun[item] for item in known])
    return {**begun, **dict(zip(items, found))}


def corner_kernel(flags, down, up, out, held, arrive, leave):
    spans = [pl.ds(b * COUNT, COUNT) for b in range(BLOCKS)] + [pl.ds(BLOCKS * COUNT, TAIL)]
    reads = [pltpu.make_async_copy(up.at[span], held.at[span], arrive.at[i]) for i, span in enumerate(spans)]
    writes = [pltpu.make_async_copy(held.at[span], out.at[span], leave.at[i]) for i, span in enumerate(spans)]

    @pl.when(flags[0] > 0)
    def _():
        for read in reads:
            read.start()
        for read, write in zip(reads, writes):
            read.wait()
            write.start()
        for write in writes:
            write.wait()


def with_corner(last, down, up):
    return pl.pallas_call(
        corner_kernel,
        out_shape=jax.ShapeDtypeStruct(down.shape, down.dtype),
        in_specs=[smem(), anywhere(), anywhere()],
        out_specs=anywhere(),
        scratch_shapes=[
            pltpu.VMEM(down.shape, down.dtype),
            pltpu.SemaphoreType.DMA((BLOCKS + 1,)),
            pltpu.SemaphoreType.DMA((BLOCKS + 1,)),
        ],
        input_output_aliases={1: 0},
        compiler_params=pltpu.CompilerParams(vmem_limit_bytes=VMEM),
        cost_estimate=pl.CostEstimate(flops=0, bytes_accessed=4 * down.size, transcendentals=0),
    )(last, down, up)


def ring(devices, by, rows=None):
    return [
        (row * ROW + x, row * ROW + (x + by) % ROW)
        for row in range(devices // ROW) if rows is None or rows(row) for x in range(ROW)
    ]


def column(devices, by, rows=None):
    return [
        (i, i + by * ROW) for i in range(devices)
        if 0 <= i + by * ROW < devices and (rows is None or rows((i + by * ROW) // ROW))
    ]


def body(embeddings, block_cluster, block_rows):
    minor = lax.axis_size(AXES[1])
    devices = lax.axis_size(AXES[0]) * minor
    blocks, count, _ = embeddings.shape
    major = lax.axis_index(AXES[0])
    me = lax.axis_index(AXES).astype(jnp.int32)
    x, row = me % ROW, me // ROW
    last_row = devices // ROW - 1
    even_site = major % 2 == 0

    def even(r):
        return (r * ROW // minor) % 2 == 0

    def odd(r):
        return not even(r)

    right, left = ring(devices, 1), ring(devices, -1)
    below, above = column(devices, 1), column(devices, -1)

    early, late = even_site & (x == 0), ~even_site & (x == ROW - 1)
    between = (x == 1) | (x == 2)
    flags = jnp.stack([
        x >= 0, x < 2, even_site, ~even_site, early, late, even_site & between, ~even_site & between,
        even_site & (x < ROW - 1), ~even_site & (x < ROW - 1),
    ]).astype(jnp.int32)

    units = normalize(embeddings, block_cluster, block_rows)
    up, nxt = shifted(units, below), shifted(units, left)
    down, prv = shifted(units, above), shifted(units, right)
    best = own_tile(units, block_cluster, block_rows)
    up, nxt, best = lax.optimization_barrier((up, nxt, best))
    up_next_even = shifted(up, ring(devices, -1, even))
    up_next_odd = shifted(nxt, column(devices, 1, odd))
    down = with_corner((x == ROW - 1).astype(jnp.int32)[None], down, up)
    down_prev_even = shifted(down, [(i, j) for i, j in ring(devices, 1, even) if j % ROW != ROW - 1])
    down_prev_odd = shifted(prv, [(i, j) for i, j in column(devices, -1, odd) if j % ROW in (1, 2)])
    corner_odd = shifted(nxt, [(i, j) for i, j in column(devices, -1, odd) if j % ROW == ROW - 1])

    found = compare(
        flags, [(nxt, "next"), (units, "own"), (prv, "prev"), (up, "up")],
        [(0, 1, ONE), (0, 3, ONE), (0, 2, LEFT_HALF), (1, 3, ONE), (2, 3, ONE)], {},
    )
    from_prev = shifted(found["next"], right)
    found = compare(
        flags, [(prv, "prev"), (down, "down"), (up_next_even, "up_next"), (up_next_odd, "up_next")],
        [(2, 0, EVEN), (2, 1, EVEN_LEFT), (3, 0, ODD), (3, 1, ODD_LEFT)], found,
    )
    from_next = shifted(found["prev"], left)
    found = compare(
        flags,
        [
            (up, "up"), (down, "down"), (up_next_even, "up_next"), (down_prev_even, "down_prev"),
            (up_next_odd, "up_next"), (down_prev_odd, "down_prev"), (corner_odd, "down_prev"),
        ],
        [(2, 3, EVEN_BETWEEN), (1, 3, EVEN_FIRST), (4, 5, ODD_BETWEEN), (0, 6, ODD_LAST)], found,
    )
    from_below = shifted(found["up"], above)
    from_above = shifted(found["down"], below)
    rows = devices // ROW
    sites = [(r, c) for r in range(rows) for c in range(ROW)]
    from_below_prev = shifted(
        found["up_next"], [(r * ROW + c, (r - 1) * ROW + (c + 1) % ROW) for r, c in sites if r > 0]
    )
    from_corner = shifted(
        found["down_prev"],
        [(r * ROW + c, (r + 1) * ROW + c - 1) for r, c in sites if r + 1 < rows and c in (1, 2)]
        + [(r * ROW, r * ROW - 1) for r in range(1, rows) if even(r)],
    )
    from_last = shifted(
        found["down_prev"], [(r * ROW + ROW - 1, (r + 1) * ROW) for r in range(rows - 1) if odd(r)]
    )
    has_below, has_above = row < last_row, row > 0
    parity_below = ((row + 1) * ROW // minor) % 2
    parity_above = (jnp.maximum(row - 1, 0) * ROW // minor) % 2
    best = jnp.maximum(jnp.maximum(best, found["own"]), jnp.maximum(from_prev, from_next))
    for there, value in (
        (has_below, from_below),
        (has_above, from_above),
        (has_below, from_below_prev),
        ((has_above & (x < 2)) | (has_below & (x == ROW - 1) & (parity_below == 0)), from_corner),
        (has_above & (x == 0) & (parity_above == 1), from_last),
    ):
        best = jnp.maximum(best, jnp.where(there, value, LOW))
    position = lax.broadcasted_iota(jnp.int32, (blocks, count), 1)
    return jnp.where(position < block_rows[:, None], jnp.maximum(1.0 + best, 0.0) - 1.0, 0.0)


def solution(mesh):
    placed = (P(AXES, None, None), P(AXES), P(AXES))
    return jax.shard_map(body, mesh=mesh, in_specs=placed, out_specs=P(AXES, None), check_vma=False)
```

time: 137 us -> 126 us (0.920)
  the two profiles are of different devices: /device:TPU:32 before, /device:TPU:22 now
where the time goes in v3:
time: 126 us
  starting transfers between devices  49.5 us (39%)
  waiting for transfers between devices  49.3 us (39%)
  Pallas kernels  25.4 us (20%)
    ppermute x16, starting transfers between devices, shifted(): return lax.ppermute(array, AXES, pairs)  49.5 us
    ppermute x16, waiting for transfers between devices, shifted(): return lax.ppermute(array, AXES, pairs)  49.3 us
    pallas_call x3, Pallas kernels, compare(): pl.pallas_call(functools.partial(pairs_kernel, [part[1] for part in parts...  14.1 us
    pallas_call x1, Pallas kernels, own_tile(): pl.pallas_call(own_kernel, out_shape=jax.ShapeDtypeStruct((blocks, count)...  5.91 us
    pallas_call x1, Pallas kernels, normalize(): pl.pallas_call(unit_kernel, out_shape=jax.ShapeDtypeStruct((blocks * coun...  3.03 us
  transfers between devices with their start and end apart: 16, of which 6 were waited for; matrix products, arithmetic and copies ran while one was open for 1% of the time, Pallas kernels for 18%

profile of v3, /device:TPU:22, one launch (start us, length us, event | category | flops | bytes accessed | tf_op | source)
XLA Modules:
  0.0 125.9 jit_solution(452534811378729923)
XLA Ops:
  0.0 3.0 %shard_map.37.units.refs_1_ = bf16[1040,1024]{1,0:T(8,128)(2,1)} custom-call(s32[8]{0:T(128)} %cluster.1, s32[8]{0:T(128)} %live.1, bf16[8,128,1024]{2,1,0:T(8,128)(2,1)} %embeddings.1), custom_call_target="tpu_custom_call" | custom-call | flops 4194304 | bytes 4194304 | tf_op jit(solution)/shard_map/pallas_call | solution.py:74
  3.0 0.9 collective-permute-start.1
  3.9 3.8 %collective-permute-start = (bf16[1040,1024]{1,0:T(8,128)(2,1)}, bf16[1040,1024]{1,0:T(8,128)(2,1)S(1)}, u32[]{:S(2)}, u32[]{:S(2)}) collective-permute-start(bf16[1040,1024]{1,0:T(8,128)(2,1)} %shard_map.37.units.refs_1_), channel_id=1, source_target_pairs={{0,4},{1,5},{2,6},{3,7},{4,8},{5,9},{6,10},{7,11},{8,12},{9,13},{1... | collective-permute-start | bytes 6389768 | tf_op jit(solution)/shard_map/ppermute | solution.py:23
  7.8 2.5 %collective-permute-start.2 = (bf16[1040,1024]{1,0:T(8,128)(2,1)}, bf16[1040,1024]{1,0:T(8,128)(2,1)}, u32[]{:S(2)}, u32[]{:S(2)}) collective-permute-start(bf16[1040,1024]{1,0:T(8,128)(2,1)} %shard_map.37.units.refs_1_), channel_id=1, source_target_pairs={{0,1},{1,2},{2,3},{3,0},{4,5},{5,6},{6,7},{7,4},{8,9},{9,10},{10,1... | collective-permute-start | bytes 6389768 | tf_op jit(solution)/shard_map/ppermute | solution.py:23
  10.2 3.6 %collective-permute-start.4 = (bf16[1040,1024]{1,0:T(8,128)(2,1)}, bf16[1040,1024]{1,0:T(8,128)(2,1)}, u32[]{:S(2)}, u32[]{:S(2)}) collective-permute-start(bf16[1040,1024]{1,0:T(8,128)(2,1)} %shard_map.37.units.refs_1_), channel_id=1, source_target_pairs={{4,0},{5,1},{6,2},{7,3},{8,4},{9,5},{10,6},{11,7},{12,8},{13,9},{1... | collective-permute-start | bytes 6389768 | tf_op jit(solution)/shard_map/ppermute | solution.py:23
  13.8 5.9 %shard_map.38 = f32[8,128]{1,0:T(8,128)} custom-call(s32[8]{0:T(128)} %cluster.1, s32[8]{0:T(128)} %live.1, bf16[1040,1024]{1,0:T(8,128)(2,1)} %shard_map.37.units.refs_1_), custom_call_target="tpu_custom_call" | custom-call | flops 2147483648 | bytes 2097152 | tf_op jit(solution)/shard_map/pallas_call | solution.py:121
  19.7 33.0 %collective-permute-done.1.refs_0_ = bf16[1040,1024]{1,0:T(8,128)(2,1)} collective-permute-done((bf16[1040,1024]{1,0:T(8,128)(2,1)}, bf16[1040,1024]{1,0:T(8,128)(2,1)}, u32[]{:S(2)}, u32[]{:S(2)}) %collective-permute-start.1) | collective-permute-done | bytes 2129952 | tf_op jit(solution)/shard_map/ppermute | solution.py:23
  52.7 0.7 collective-permute-done.refs_3_.up.refs_0_
  53.4 0.0 copy-start
  53.4 2.0 %collective-permute-start.6 = (bf16[1040,1024]{1,0:T(8,128)(2,1)}, bf16[1040,1024]{1,0:T(8,128)(2,1)}, u32[]{:S(2)}, u32[]{:S(2)}) collective-permute-start(bf16[1040,1024]{1,0:T(8,128)(2,1)} %collective-permute-done.1.refs_0_), channel_id=1, source_target_pairs={{12,16},{13,17},{14,18},{15,19},{16,20},{17,21},{18,22},{19,23},{2... | collective-permute-start | bytes 6389768 | tf_op jit(solution)/shard_map/ppermute | solution.py:23
  55.4 2.4 %collective-permute-start.5 = (bf16[1040,1024]{1,0:T(8,128)(2,1)S(1)}, bf16[1040,1024]{1,0:T(8,128)(2,1)}, u32[]{:S(2)}, u32[]{:S(2)}) collective-permute-start(bf16[1040,1024]{1,0:T(8,128)(2,1)S(1)} %collective-permute-done.refs_3_.up.refs_0_), channel_id=1, source_target_pairs={{0,3},{1,0},{2,1},{3,2},{4,7},{5,4},{6,5},{7,6},{8,11},{9,8},{10,9... | collective-permute-start | bytes 6389768 | tf_op jit(solution)/shard_map/ppermute | solution.py:23
  57.9 4.8 %collective-permute-start.10 = (bf16[1040,1024]{1,0:T(8,128)(2,1)}, bf16[1040,1024]{1,0:T(8,128)(2,1)}, u32[]{:S(2)}, u32[]{:S(2)}) collective-permute-start(bf16[1040,1024]{1,0:T(8,128)(2,1)} %collective-permute-done.1.refs_0_), channel_id=1, source_target_pairs={{23,19},{27,23},{31,27},{35,31},{55,51},{59,55},{63,59},{67,63},{8... | collective-permute-start | bytes 6389768 | tf_op jit(solution)/shard_map/ppermute | solution.py:23
  62.6 0.0 collective-permute-done.2.refs_2_.refs_0_
  62.6 2.1 %collective-permute-start.9 = (bf16[1040,1024]{1,0:T(8,128)(2,1)}, bf16[1040,1024]{1,0:T(8,128)(2,1)}, u32[]{:S(2)}, u32[]{:S(2)}) collective-permute-start(bf16[1040,1024]{1,0:T(8,128)(2,1)} %collective-permute-done.2.refs_2_.refs_0_), channel_id=1, source_target_pairs={{21,17},{22,18},{25,21},{26,22},{29,25},{30,26},{33,29},{34,30},{5... | collective-permute-start | bytes 6389768 | tf_op jit(solution)/shard_map/ppermute | solution.py:23
  64.7 0.0 collective-permute-done.4.down
  64.7 0.0 copy-done
  64.7 2.4 %shard_map.40.refs_1_ = bf16[1040,1024]{1,0:T(8,128)(2,1)} custom-call(s32[1]{0:T(128)} %bitcast.10.flags, bf16[1040,1024]{1,0:T(8,128)(2,1)} %collective-permute-done.4.down, bf16[1040,1024]{1,0:T(8,128)(2,1)} %copy-done), custom_call_target="tpu_custom_call", output_to_operand_aliasing={{}: (1, {})} | custom-call | bytes 4259840 | tf_op jit(solution)/shard_map/pallas_call | solution.py:274
  67.2 2.7 %collective-permute-start.8 = (bf16[1040,1024]{1,0:T(8,128)(2,1)}, bf16[1040,1024]{1,0:T(8,128)(2,1)}, u32[]{:S(2)}, u32[]{:S(2)}) collective-permute-start(bf16[1040,1024]{1,0:T(8,128)(2,1)} %shard_map.40.refs_1_), channel_id=1, source_target_pairs={{0,1},{1,2},{3,0},{4,5},{5,6},{7,4},{8,9},{9,10},{11,8},{12,13},{1... | collective-permute-start | bytes 6389768 | tf_op jit(solution)/shard_map/ppermute | solution.py:23
  69.8 0.1 stack.43
  69.9 0.5 convert_element_type.4.flags
  70.5 8.2 %shard_map.39 = (f32[8,128]{1,0:T(8,128)}, f32[8,128]{1,0:T(8,128)}, f32[8,128]{1,0:T(8,128)}, f32[8,128]{1,0:T(8,128)}) custom-call(s32[10]{0:T(128)} %convert_element_type.4.flags, bf16[1040,1024]{1,0:T(8,128)(2,1)} %collective-permute-done.1.refs_0_, bf16[1040,1024]{1,0:T(8,128)(2,1)} %shard_map.37.units.refs_1_, ...), custom_call_target="tpu_custom_call" | custom-call | flops 10737418240 | bytes 8519680 | tf_op jit(solution)/shard_map/pallas_call | solution.py:232
  78.7 0.0 collective-permute-done.6.refs_3_.refs_4_
  78.7 0.1 collective-permute-start.3
  78.8 6.2 %collective-permute-done.5.refs_2_ = bf16[1040,1024]{1,0:T(8,128)(2,1)} collective-permute-done((bf16[1040,1024]{1,0:T(8,128)(2,1)S(1)}, bf16[1040,1024]{1,0:T(8,128)(2,1)}, u32[]{:S(2)}, u32[]{:S(2)}) %collective-permute-start.5) | collective-permute-done | bytes 2129952 | tf_op jit(solution)/shard_map/ppermute | solution.py:23
  85.0 2.9 %shard_map.41 = (f32[8,128]{1,0:T(8,128)}, f32[8,128]{1,0:T(8,128)}, f32[8,128]{1,0:T(8,128)}) custom-call(s32[10]{0:T(128)} %convert_element_type.4.flags, bf16[1040,1024]{1,0:T(8,128)(2,1)} %collective-permute-done.2.refs_2_.refs_0_, bf16[1040,1024]{1,0:T(8,128)(2,1)} %shard_map.40.refs_1_, bf16[1040,1024]{1,0:T(8,128)(2,1)} %collective-permute-done.5.refs_2_, ...), custom_call_target="tpu_custom_call" | custom-call | flops 8589934592 | bytes 8519680 | tf_op jit(solution)/shard_map/pallas_call | solution.py:232
  87.9 0.0 collective-permute-done.9.refs_5_
  87.9 0.0 collective-permute-done.10.refs_6_
  87.9 4.8 %collective-permute-done.8.refs_3_ = bf16[1040,1024]{1,0:T(8,128)(2,1)} collective-permute-done((bf16[1040,1024]{1,0:T(8,128)(2,1)}, bf16[1040,1024]{1,0:T(8,128)(2,1)}, u32[]{:S(2)}, u32[]{:S(2)}) %collective-permute-start.8) | collective-permute-done | bytes 2129952 | tf_op jit(solution)/shard_map/ppermute | solution.py:23
  92.7 0.0 copy-start.4
  92.7 2.9 %shard_map.42 = (f32[8,128]{1,0:T(8,128)}, f32[8,128]{1,0:T(8,128)}, f32[8,128]{1,0:T(8,128)}, f32[8,128]{1,0:T(8,128)}) custom-call(s32[10]{0:T(128)} %convert_element_type.4.flags, bf16[1040,1024]{1,0:T(8,128)(2,1)} %copy-done, bf16[1040,1024]{1,0:T(8,128)(2,1)} %shard_map.40.refs_1_, bf16[1040,1024]{1,0:T(8,128)(2,1)} %collective-permute-done.5.refs_2_, ...), custom_call_target="tpu_custom_call" | custom-call | flops 8589934592 | bytes 14909440 | tf_op jit(solution)/shard_map/pallas_call | solution.py:232
  95.6 6.7 %collective-permute-start.11 = (f32[8,128]{1,0:T(8,128)}, f32[8,128]{1,0:T(8,128)S(1)}, u32[]{:S(2)}, u32[]{:S(2)}) collective-permute-start(f32[8,128]{1,0:T(8,128)} %get-tuple-element.29), channel_id=1, source_target_pairs={{4,0},{5,1},{6,2},{7,3},{8,4},{9,5},{10,6},{11,7},{12,8},{13,9},{1... | collective-permute-start | bytes 12296 | tf_op jit(solution)/shard_map/ppermute | solution.py:23
  102.3 0.7 collective-permute-start.15
  103.0 1.3 %collective-permute-start.14 = (f32[8,128]{1,0:T(8,128)}, f32[8,128]{1,0:T(8,128)S(1)}, u32[]{:S(2)}, u32[]{:S(2)}) collective-permute-start(f32[8,128]{1,0:T(8,128)} %get-tuple-element.32), channel_id=1, source_target_pairs={{1,4},{2,5},{5,8},{6,9},{9,12},{10,13},{13,16},{14,17},{17,20},{18... | collective-permute-start | bytes 12296 | tf_op jit(solution)/shard_map/ppermute | solution.py:23
  104.3 1.9 %collective-permute-start.12 = (f32[8,128]{1,0:T(8,128)}, f32[8,128]{1,0:T(8,128)S(1)}, u32[]{:S(2)}, u32[]{:S(2)}) collective-permute-start(f32[8,128]{1,0:T(8,128)} %get-tuple-element.30), channel_id=1, source_target_pairs={{0,4},{1,5},{2,6},{3,7},{4,8},{5,9},{6,10},{7,11},{8,12},{9,13},{1... | collective-permute-start | bytes 12296 | tf_op jit(solution)/shard_map/ppermute | solution.py:23
  106.2 0.0 collective-permute-done.3
  106.2 14.1 %collective-permute-start.13 = (f32[8,128]{1,0:T(8,128)}, f32[8,128]{1,0:T(8,128)S(1)}, u32[]{:S(2)}, u32[]{:S(2)}) collective-permute-start(f32[8,128]{1,0:T(8,128)} %get-tuple-element.31), channel_id=1, source_target_pairs={{4,1},{5,2},{6,3},{7,0},{8,5},{9,6},{10,7},{11,4},{12,9},{13,10},{... | collective-permute-start | bytes 12296 | tf_op jit(solution)/shard_map/ppermute | solution.py:23
  120.3 0.0 collective-permute-done.11
  120.3 0.0 copy-done.4
  120.3 0.1 collective-permute-start.7
  120.5 0.0 collective-permute-done.12
  120.5 1.3 %collective-permute-done.13 = f32[8,128]{1,0:T(8,128)S(1)} collective-permute-done((f32[8,128]{1,0:T(8,128)}, f32[8,128]{1,0:T(8,128)S(1)}, u32[]{:S(2)}, u32[]{:S(2)}) %collective-permute-start.13) | collective-permute-done | bytes 4128 | tf_op jit(solution)/shard_map/ppermute | solution.py:23
  121.8 0.0 collective-permute-done.15
  121.8 0.0 collective-permute-done.14
  121.8 3.4 %collective-permute-done.7 = f32[8,128]{1,0:T(8,128)S(1)} collective-permute-done((f32[8,128]{1,0:T(8,128)S(1)}, f32[8,128]{1,0:T(8,128)S(1)}, u32[]{:S(2)}, u32[]{:S(2)}) %collective-permute-start.7) | collective-permute-done | bytes 4128 | tf_op jit(solution)/shard_map/ppermute | solution.py:23
  125.2 0.0 copy-done.1
  125.2 0.0 copy-done.2
  125.2 0.0 copy-done.3
  125.2 0.7 add_select_fusion
  (3 shorter events, 0.0 us)
Async XLA Ops:
  3.0 49.7 %collective-permute-start.1 = (bf16[1040,1024]{1,0:T(8,128)(2,1)}, bf16[1040,1024]{1,0:T(8,128)(2,1)}, u32[]{:S(2)}, u32[]{:S(2)}) collective-permute-start(bf16[1040,1024]{1,0:T(8,128)(2,1)} %shard_map.37.units.refs_1_), channel_id=1, source_target_pairs={{0,3},{1,0},{2,1},{3,2},{4,7},{5,4},{6,5},{7,6},{8,11},{9,8},{10,9... | collective-permute-start | bytes 6389768 | tf_op jit(solution)/shard_map/ppermute | solution.py:23
  3.9 49.4 %collective-permute-start = (bf16[1040,1024]{1,0:T(8,128)(2,1)}, bf16[1040,1024]{1,0:T(8,128)(2,1)S(1)}, u32[]{:S(2)}, u32[]{:S(2)}) collective-permute-start(bf16[1040,1024]{1,0:T(8,128)(2,1)} %shard_map.37.units.refs_1_), channel_id=1, source_target_pairs={{0,4},{1,5},{2,6},{3,7},{4,8},{5,9},{6,10},{7,11},{8,12},{9,13},{1... | collective-permute-start | bytes 6389768 | tf_op jit(solution)/shard_map/ppermute | solution.py:23
  7.8 54.9 %collective-permute-start.2 = (bf16[1040,1024]{1,0:T(8,128)(2,1)}, bf16[1040,1024]{1,0:T(8,128)(2,1)}, u32[]{:S(2)}, u32[]{:S(2)}) collective-permute-start(bf16[1040,1024]{1,0:T(8,128)(2,1)} %shard_map.37.units.refs_1_), channel_id=1, source_target_pairs={{0,1},{1,2},{2,3},{3,0},{4,5},{5,6},{6,7},{7,4},{8,9},{9,10},{10,1... | collective-permute-start | bytes 6389768 | tf_op jit(solution)/shard_map/ppermute | solution.py:23
  10.2 54.5 %collective-permute-start.4 = (bf16[1040,1024]{1,0:T(8,128)(2,1)}, bf16[1040,1024]{1,0:T(8,128)(2,1)}, u32[]{:S(2)}, u32[]{:S(2)}) collective-permute-start(bf16[1040,1024]{1,0:T(8,128)(2,1)} %shard_map.37.units.refs_1_), channel_id=1, source_target_pairs={{4,0},{5,1},{6,2},{7,3},{8,4},{9,5},{10,6},{11,7},{12,8},{13,9},{1... | collective-permute-start | bytes 6389768 | tf_op jit(solution)/shard_map/ppermute | solution.py:23
  53.4 11.3 %copy-start = (bf16[1040,1024]{1,0:T(8,128)(2,1)}, bf16[1040,1024]{1,0:T(8,128)(2,1)S(1)}, u32[]{:S(2)}) copy-start(bf16[1040,1024]{1,0:T(8,128)(2,1)S(1)} %collective-permute-done.refs_3_.up.refs_0_) | copy-start | bytes 6389764
  53.4 25.4 %collective-permute-start.6 = (bf16[1040,1024]{1,0:T(8,128)(2,1)}, bf16[1040,1024]{1,0:T(8,128)(2,1)}, u32[]{:S(2)}, u32[]{:S(2)}) collective-permute-start(bf16[1040,1024]{1,0:T(8,128)(2,1)} %collective-permute-done.1.refs_0_), channel_id=1, source_target_pairs={{12,16},{13,17},{14,18},{15,19},{16,20},{17,21},{18,22},{19,23},{2... | collective-permute-start | bytes 6389768 | tf_op jit(solution)/shard_map/ppermute | solution.py:23
  55.4 29.6 %collective-permute-start.5 = (bf16[1040,1024]{1,0:T(8,128)(2,1)S(1)}, bf16[1040,1024]{1,0:T(8,128)(2,1)}, u32[]{:S(2)}, u32[]{:S(2)}) collective-permute-start(bf16[1040,1024]{1,0:T(8,128)(2,1)S(1)} %collective-permute-done.refs_3_.up.refs_0_), channel_id=1, source_target_pairs={{0,3},{1,0},{2,1},{3,2},{4,7},{5,4},{6,5},{7,6},{8,11},{9,8},{10,9... | collective-permute-start | bytes 6389768 | tf_op jit(solution)/shard_map/ppermute | solution.py:23
  57.9 30.0 %collective-permute-start.10 = (bf16[1040,1024]{1,0:T(8,128)(2,1)}, bf16[1040,1024]{1,0:T(8,128)(2,1)}, u32[]{:S(2)}, u32[]{:S(2)}) collective-permute-start(bf16[1040,1024]{1,0:T(8,128)(2,1)} %collective-permute-done.1.refs_0_), channel_id=1, source_target_pairs={{23,19},{27,23},{31,27},{35,31},{55,51},{59,55},{63,59},{67,63},{8... | collective-permute-start | bytes 6389768 | tf_op jit(solution)/shard_map/ppermute | solution.py:23
  62.6 25.2 %collective-permute-start.9 = (bf16[1040,1024]{1,0:T(8,128)(2,1)}, bf16[1040,1024]{1,0:T(8,128)(2,1)}, u32[]{:S(2)}, u32[]{:S(2)}) collective-permute-start(bf16[1040,1024]{1,0:T(8,128)(2,1)} %collective-permute-done.2.refs_2_.refs_0_), channel_id=1, source_target_pairs={{21,17},{22,18},{25,21},{26,22},{29,25},{30,26},{33,29},{34,30},{5... | collective-permute-start | bytes 6389768 | tf_op jit(solution)/shard_map/ppermute | solution.py:23
  67.2 25.5 %collective-permute-start.8 = (bf16[1040,1024]{1,0:T(8,128)(2,1)}, bf16[1040,1024]{1,0:T(8,128)(2,1)}, u32[]{:S(2)}, u32[]{:S(2)}) collective-permute-start(bf16[1040,1024]{1,0:T(8,128)(2,1)} %shard_map.40.refs_1_), channel_id=1, source_target_pairs={{0,1},{1,2},{3,0},{4,5},{5,6},{7,4},{8,9},{9,10},{11,8},{12,13},{1... | collective-permute-start | bytes 6389768 | tf_op jit(solution)/shard_map/ppermute | solution.py:23
  78.7 27.5 %collective-permute-start.3 = (f32[8,128]{1,0:T(8,128)}, f32[8,128]{1,0:T(8,128)S(1)}, u32[]{:S(2)}, u32[]{:S(2)}) collective-permute-start(f32[8,128]{1,0:T(8,128)} %get-tuple-element.23), channel_id=1, source_target_pairs={{0,1},{1,2},{2,3},{3,0},{4,5},{5,6},{6,7},{7,4},{8,9},{9,10},{10,1... | collective-permute-start | bytes 12296 | tf_op jit(solution)/shard_map/ppermute | solution.py:23
  92.7 27.6 %copy-start.4 = (f32[8,128]{1,0:T(8,128)S(1)}, f32[8,128]{1,0:T(8,128)}, u32[]{:S(2)}) copy-start(f32[8,128]{1,0:T(8,128)} %get-tuple-element.25) | copy-start | bytes 12292
  92.7 32.5 %copy-start.1 = (f32[8,128]{1,0:T(8,128)S(1)}, f32[8,128]{1,0:T(8,128)}, u32[]{:S(2)}) copy-start(f32[8,128]{1,0:T(8,128)} %shard_map.38) | copy-start | bytes 12292
  92.7 32.5 %copy-start.2 = (f32[8,128]{1,0:T(8,128)S(1)}, f32[8,128]{1,0:T(8,128)}, u32[]{:S(2)}) copy-start(f32[8,128]{1,0:T(8,128)} %get-tuple-element.22) | copy-start | bytes 12292
  92.7 32.5 %copy-start.3 = (s32[8]{0:T(128)S(1)}, s32[8]{0:T(128)}, u32[]{:S(2)}) copy-start(s32[8]{0:T(128)} %live.1) | copy-start | bytes 100
  95.6 24.7 %collective-permute-start.11 = (f32[8,128]{1,0:T(8,128)}, f32[8,128]{1,0:T(8,128)S(1)}, u32[]{:S(2)}, u32[]{:S(2)}) collective-permute-start(f32[8,128]{1,0:T(8,128)} %get-tuple-element.29), channel_id=1, source_target_pairs={{4,0},{5,1},{6,2},{7,3},{8,4},{9,5},{10,6},{11,7},{12,8},{13,9},{1... | collective-permute-start | bytes 12296 | tf_op jit(solution)/shard_map/ppermute | solution.py:23
  102.3 19.5 %collective-permute-start.15 = (f32[8,128]{1,0:T(8,128)}, f32[8,128]{1,0:T(8,128)S(1)}, u32[]{:S(2)}, u32[]{:S(2)}) collective-permute-start(f32[8,128]{1,0:T(8,128)} %get-tuple-element.32), channel_id=1, source_target_pairs={{19,20},{23,24},{27,28},{31,32},{51,52},{55,56},{59,60},{63,64},{8... | collective-permute-start | bytes 12296 | tf_op jit(solution)/shard_map/ppermute | solution.py:23
  103.0 18.9 %collective-permute-start.14 = (f32[8,128]{1,0:T(8,128)}, f32[8,128]{1,0:T(8,128)S(1)}, u32[]{:S(2)}, u32[]{:S(2)}) collective-permute-start(f32[8,128]{1,0:T(8,128)} %get-tuple-element.32), channel_id=1, source_target_pairs={{1,4},{2,5},{5,8},{6,9},{9,12},{10,13},{13,16},{14,17},{17,20},{18... | collective-permute-start | bytes 12296 | tf_op jit(solution)/shard_map/ppermute | solution.py:23
  104.3 16.3 %collective-permute-start.12 = (f32[8,128]{1,0:T(8,128)}, f32[8,128]{1,0:T(8,128)S(1)}, u32[]{:S(2)}, u32[]{:S(2)}) collective-permute-start(f32[8,128]{1,0:T(8,128)} %get-tuple-element.30), channel_id=1, source_target_pairs={{0,4},{1,5},{2,6},{3,7},{4,8},{5,9},{6,10},{7,11},{8,12},{9,13},{1... | collective-permute-start | bytes 12296 | tf_op jit(solution)/shard_map/ppermute | solution.py:23
  106.2 15.6 %collective-permute-start.13 = (f32[8,128]{1,0:T(8,128)}, f32[8,128]{1,0:T(8,128)S(1)}, u32[]{:S(2)}, u32[]{:S(2)}) collective-permute-start(f32[8,128]{1,0:T(8,128)} %get-tuple-element.31), channel_id=1, source_target_pairs={{4,1},{5,2},{6,3},{7,0},{8,5},{9,6},{10,7},{11,4},{12,9},{13,10},{... | collective-permute-start | bytes 12296 | tf_op jit(solution)/shard_map/ppermute | solution.py:23
  120.3 4.9 %collective-permute-start.7 = (f32[8,128]{1,0:T(8,128)S(1)}, f32[8,128]{1,0:T(8,128)S(1)}, u32[]{:S(2)}, u32[]{:S(2)}) collective-permute-start(f32[8,128]{1,0:T(8,128)S(1)} %copy-done.4), channel_id=1, source_target_pairs={{0,3},{1,0},{2,1},{3,2},{4,7},{5,4},{6,5},{7,6},{8,11},{9,8},{10,9... | collective-permute-start | bytes 12296 | tf_op jit(solution)/shard_map/ppermute | solution.py:23

commit v4 on v3

--- a/solution.py
+++ b/solution.py
@@ -130,28 +130,23 @@
     )(cluster, live, units)
 
 
-def pairs_kernel(parts, jobs, items, begun, flags, *refs):
-    many = len(parts)
+def pairs_kernel(parts, count_jobs, items, begun, jobs, flags, *refs):
+    many, count = len(parts), COUNT
     arrays, refs = refs[:many], refs[many:]
     starts, refs = refs[:len(begun)], refs[len(begun):]
     outs, refs = refs[:len(items)], refs[len(items):]
-    held, refs = refs[:many], refs[many:]
-    tails, listed, ids, arrived, came, moved, seen, rows_best = refs
-    count = COUNT
+    held, best, tails, listed, ids, arrived, came, moved, state, rows_best = refs
     ends = [
         pltpu.make_async_copy(arrays[i].at[pl.ds(BLOCKS * count, TAIL), pl.ds(0, 128)], tails.at[i], came.at[i])
         for i in range(many)
     ]
-    copies = [
-        pltpu.make_async_copy(arrays[i].at[pl.ds(0, BLOCKS * count)], held[i], arrived.at[i]) for i in range(many)
-    ]
     for end in ends:
         end.start()
-    for item, out in zip(items, outs):
+    for k, item in enumerate(items):
         if item in begun:
-            out[...] = starts[begun.index(item)][...]
+            best[k] = starts[begun.index(item)][...]
         else:
-            out[...] = jnp.full(out.shape, LOW, jnp.float32)
+            best[k] = jnp.full(best.shape[1:], LOW, jnp.float32)
     for i, end in enumerate(ends):
         end.wait()
         digits = tails[i].astype(jnp.float32)
@@ -159,66 +154,111 @@
     move = pltpu.make_async_copy(listed, ids, moved.at[0])
     move.start()
     move.wait()
-    wanted, needed = [], [jnp.bool_(False)] * many
-    for first, second, flag in jobs:
-        want = (flags[flag] > 0) & (ids[first, BLOCKS - 1] >= ids[second, 0])
-        want = want & (ids[first, 0] <= ids[second, BLOCKS - 1])
-        wanted.append(want)
-        for i in (first, second):
-            needed[i] = needed[i] | want
     for i in range(many):
-        seen[i] = 0
-        pl.when(needed[i])(copies[i].start)
-    for (first, second, _), want in zip(jobs, wanted):
-
-        @pl.when(want)
-        def _(first=first, second=second):
-            for i in (first, second):
-
-                @pl.when(seen[i] == 0)
-                def _(i=i):
-                    copies[i].wait()
-                    seen[i] = 1
-
-            a, b = held[first], held[second]
-            a_out, b_out = outs[items.index(parts[first])], outs[items.index(parts[second])]
-            tops = rows_best
-            tops[...] = jnp.full(tops.shape, LOW, jnp.float32)
-
-            def chunk(i, carry):
-                low, high = ids[second, 2 * i], ids[second, 2 * i + 1]
-                meets = (high >= ids[first, 0]) & (low <= ids[first, BLOCKS - 1])
-                same = (low == high) & (ids[first, 0] == low) & (ids[first, BLOCKS - 1] == low)
-
-                def work(hide):
+        state[i] = 0
+
+    def wanted(j):
+        first, second = jobs[5 * j], jobs[5 * j + 1]
+        meet = (ids[first, BLOCKS - 1] >= ids[second, 0]) & (ids[first, 0] <= ids[second, BLOCKS - 1])
+        return meet & (flags[jobs[5 * j + 2]] > 0)
+
+    def mark(j, carry):
+        @pl.when(wanted(j))
+        def _():
+            state[jobs[5 * j]] = 1
+            state[jobs[5 * j + 1]] = 1
+
+        return carry
+
+    lax.fori_loop(0, count_jobs, mark, 0)
+    for i in range(many):
+        copy = pltpu.make_async_copy(arrays[i].at[pl.ds(0, BLOCKS * count)], held.at[i], arrived.at[i])
+        pl.when(state[i] > 0)(copy.start)
+
+    def fetched(i):
+        @pl.when(state[i] == 1)
+        def _():
+            pltpu.make_async_copy(arrays[0].at[pl.ds(0, BLOCKS * count)], held.at[i], arrived.at[i]).wait()
+            state[i] = 2
+
+    def tile(first, second, a_out, b_out):
+        a, b = held.at[first], held.at[second]
+        same = (ids[first, 0] == ids[first, BLOCKS - 1]) & (ids[second, 0] == ids[second, BLOCKS - 1])
+        same = same & (ids[first, 0] == ids[second, 0])
+
+        @pl.when(same)
+        def _():
+            columns = [None] * BLOCKS
+            for i in range(BLOCKS // 2):
+                similar = lax.dot_general(
+                    a[2 * i * count:2 * (i + 1) * count], b[...],
+                    (((1,), (1,)), ((), ())), preferred_element_type=jnp.float32,
+                )
+                for k in range(2):
+                    top = None
+                    for j in range(BLOCKS):
+                        part = similar[k * count:(k + 1) * count, j * count:(j + 1) * count]
+                        top = part if top is None else jnp.maximum(top, part)
+                        part = jnp.max(part.reshape(count // 8, 8, count), axis=0)
+                        columns[j] = part if columns[j] is None else jnp.maximum(columns[j], part)
+                    here = slice(2 * i + k, 2 * i + k + 1)
+                    top = jnp.max(top.T, axis=0, keepdims=True)
+                    best[a_out, here] = jnp.maximum(best[a_out, here], top)
+            for j in range(BLOCKS):
+                here = slice(j, j + 1)
+                top = jnp.max(columns[j], axis=0, keepdims=True)
+                best[b_out, here] = jnp.maximum(best[b_out, here], top)
+
+        @pl.when(jnp.logical_not(same))
+        def _():
+            rows_best[...] = jnp.full(rows_best.shape, LOW, jnp.float32)
+
+            def chunk(n, carry):
+                i, j = lax.div(n, BLOCKS // 2), lax.rem(n, BLOCKS // 2)
+                meet = ids[first, 2 * i + 1] >= ids[second, 2 * j]
+
+                @pl.when(meet & (ids[first, 2 * i] <= ids[second, 2 * j + 1]))
+                def _():
                     similar = lax.dot_general(
-                        a[...], b[pl.ds(pl.multiple_of(2 * i * count, 2 * count), 2 * count)],
+                        a[pl.ds(pl.multiple_of(2 * i * count, 2 * count), 2 * count)],
+                        b[pl.ds(pl.multiple_of(2 * j * count, 2 * count), 2 * count)],
                         (((1,), (1,)), ((), ())), preferred_element_type=jnp.float32,
                     )
                     columns = [None, None]
-                    for j in range(BLOCKS):
-                        here = slice(j * count, (j + 1) * count)
-                        top = tops[here]
-                        for k in range(2):
-                            part = similar[here, k * count:(k + 1) * count]
-                            if hide:
-                                part = part + jnp.where(ids[first, j] == ids[second, 2 * i + k], 0.0, LOW)
+                    for k in range(2):
+                        here = pl.ds(pl.multiple_of((2 * i + k) * count, count), count)
+                        top = rows_best[here]
+                        for m in range(2):
+                            part = similar[k * count:(k + 1) * count, m * count:(m + 1) * count]
+                            part = part + jnp.where(ids[first, 2 * i + k] == ids[second, 2 * j + m], 0.0, LOW)
                             top = jnp.maximum(top, part)
-                            part = jnp.max(part.reshape(count // 8, 8, count), axis=0)
-                            columns[k] = part if columns[k] is None else jnp.maximum(columns[k], part)
-                        tops[here] = top
-                    for k in range(2):
-                        here = pl.ds(2 * i + k, 1)
-                        b_out[here] = jnp.maximum(b_out[here], jnp.max(columns[k], axis=0, keepdims=True))
-
-                pl.when(same)(lambda: work(False))
-                pl.when(meets & jnp.logical_not(same))(lambda: work(True))
+                            columns[m] = part if columns[m] is None else jnp.maximum(columns[m], part)
+                        rows_best[here] = top
+                    for m in range(2):
+                        here = pl.ds(2 * j + m, 1)
+                        top = jnp.max(columns[m], axis=0, keepdims=True)
+                        best[b_out, here] = jnp.maximum(best[b_out, here], top)
+
                 return carry
 
-            lax.fori_loop(0, BLOCKS // 2, chunk, 0)
+            lax.fori_loop(0, (BLOCKS // 2) ** 2, chunk, 0)
             for j in range(BLOCKS):
-                top = jnp.max(tops[j * count:(j + 1) * count].T, axis=0, keepdims=True)
-                a_out[j:j + 1] = jnp.maximum(a_out[j:j + 1], top)
+                top = jnp.max(rows_best[j * count:(j + 1) * count].T, axis=0, keepdims=True)
+                best[a_out, j:j + 1] = jnp.maximum(best[a_out, j:j + 1], top)
+
+    def job(j, carry):
+        @pl.when(wanted(j))
+        def _():
+            first, second = jobs[5 * j], jobs[5 * j + 1]
+            fetched(first)
+            fetched(second)
+            tile(first, second, jobs[5 * j + 3], jobs[5 * j + 4])
+
+        return carry
+
+    lax.fori_loop(0, count_jobs, job, 0)
+    for k, out in enumerate(outs):
+        out[...] = best[k]
 
 
 def compare(flags, parts, jobs, begun):
@@ -229,13 +269,17 @@
     known = [item for item in items if item in begun]
     arrays = [part[0] for part in parts]
     many, width = len(arrays), arrays[0].shape[1]
+    listed = jnp.array(
+        [v for f, s, flag in jobs for v in (f, s, flag, items.index(parts[f][1]), items.index(parts[s][1]))], jnp.int32
+    )
     found = pl.pallas_call(
-        functools.partial(pairs_kernel, [part[1] for part in parts], jobs, items, known),
+        functools.partial(pairs_kernel, [part[1] for part in parts], len(jobs), items, known),
         out_shape=[jax.ShapeDtypeStruct((BLOCKS, COUNT), jnp.float32) for _ in items],
-        in_specs=[smem()] + [anywhere() for _ in arrays] + [vmem() for _ in known],
+        in_specs=[smem(), smem()] + [anywhere() for _ in arrays] + [vmem() for _ in known],
         out_specs=[vmem() for _ in items],
-        scratch_shapes=[pltpu.VMEM((BLOCKS * COUNT, width), jnp.bfloat16) for _ in arrays]
-        + [
+        scratch_shapes=[
+            pltpu.VMEM((many, BLOCKS * COUNT, width), jnp.bfloat16),
+            pltpu.VMEM((len(items), BLOCKS, COUNT), jnp.float32),
             pltpu.VMEM((many, TAIL, 128), jnp.bfloat16),
             pltpu.VMEM((8, 128), jnp.int32),
             pltpu.SMEM((8, 128), jnp.int32),
@@ -250,7 +294,7 @@
             flops=len(jobs) * 2 * (BLOCKS * COUNT) ** 2 * width,
             bytes_accessed=sum(2 * a.size for a in arrays), transcendentals=0,
         ),
-    )(flags, *arrays, *[begun[item] for item in known])
+    )(listed, flags, *arrays, *[begun[item] for item in known])
     return {**begun, **dict(zip(items, found))}
 
 
@@ -343,47 +387,34 @@
         flags, [(nxt, "next"), (units, "own"), (prv, "prev"), (up, "up")],
         [(0, 1, ONE), (0, 3, ONE), (0, 2, LEFT_HALF), (1, 3, ONE), (2, 3, ONE)], {},
     )
-    from_prev = shifted(found["next"], right)
     found = compare(
         flags, [(prv, "prev"), (down, "down"), (up_next_even, "up_next"), (up_next_odd, "up_next")],
         [(2, 0, EVEN), (2, 1, EVEN_LEFT), (3, 0, ODD), (3, 1, ODD_LEFT)], found,
     )
-    from_next = shifted(found["prev"], left)
     found = compare(
         flags,
         [
-            (up, "up"), (down, "down"), (up_next_even, "up_next"), (down_prev_even, "down_prev"),
+            (up, "corner"), (down, "down"), (up_next_even, "up_next"), (down_prev_even, "down_prev"),
             (up_next_odd, "up_next"), (down_prev_odd, "down_prev"), (corner_odd, "down_prev"),
         ],
         [(2, 3, EVEN_BETWEEN), (1, 3, EVEN_FIRST), (4, 5, ODD_BETWEEN), (0, 6, ODD_LAST)], found,
     )
-    from_below = shifted(found["up"], above)
-    from_above = shifted(found["down"], below)
-    rows = devices // ROW
-    sites = [(r, c) for r in range(rows) for c in range(ROW)]
-    from_below_prev = shifted(
-        found["up_next"], [(r * ROW + c, (r - 1) * ROW + (c + 1) % ROW) for r, c in sites if r > 0]
-    )
-    from_corner = shifted(
-        found["down_prev"],
-        [(r * ROW + c, (r + 1) * ROW + c - 1) for r, c in sites if r + 1 < rows and c in (1, 2)]
-        + [(r * ROW, r * ROW - 1) for r in range(1, rows) if even(r)],
-    )
-    from_last = shifted(
-        found["down_prev"], [(r * ROW + ROW - 1, (r + 1) * ROW) for r in range(rows - 1) if odd(r)]
-    )
-    has_below, has_above = row < last_row, row > 0
-    parity_below = ((row + 1) * ROW // minor) % 2
-    parity_above = (jnp.maximum(row - 1, 0) * ROW // minor) % 2
-    best = jnp.maximum(jnp.maximum(best, found["own"]), jnp.maximum(from_prev, from_next))
-    for there, value in (
-        (has_below, from_below),
-        (has_above, from_above),
-        (has_below, from_below_prev),
-        ((has_above & (x < 2)) | (has_below & (x == ROW - 1) & (parity_below == 0)), from_corner),
-        (has_above & (x == 0) & (parity_above == 1), from_last),
-    ):
-        best = jnp.maximum(best, jnp.where(there, value, LOW))
+    none = jnp.full((blocks, count), LOW, jnp.float32)
+    from_prev = shifted(
+        jnp.stack([found["next"], found["up_next"], jnp.where(late, found["down_prev"], none)]), right
+    )
+    from_next = shifted(
+        jnp.stack([
+            found["prev"], jnp.where(early, found["down_prev"], none),
+            jnp.where(early | late, none, found["down_prev"]),
+        ]), left
+    )
+    around = jnp.maximum(from_prev, from_next)
+    from_below = shifted(jnp.maximum(jnp.maximum(found["up"], found["corner"]), around[1]), above)
+    from_above = shifted(jnp.maximum(found["down"], around[2]), below)
+    best = jnp.maximum(jnp.maximum(best, found["own"]), around[0])
+    best = jnp.maximum(best, jnp.where(row < last_row, from_below, LOW))
+    best = jnp.maximum(best, jnp.where(row > 0, from_above, LOW))
     position = lax.broadcasted_iota(jnp.int32, (blocks, count), 1)
     return jnp.where(position < block_rows[:, None], jnp.maximum(1.0 + best, 0.0) - 1.0, 0.0)
 

time: 126 us -> 122 us (0.968)
  the two profiles are of different devices: /device:TPU:22 before, /device:TPU:23 now
where the time goes in v4:
time: 122 us; the launch traced here: 121 us
  waiting for transfers between devices  55.1 us (45%)
  starting transfers between devices  39.3 us (32%)
  Pallas kernels  23.2 us (19%)
  other arithmetic  3.22 us (3%)
    ppermute x13, waiting for transfers between devices, shifted(): return lax.ppermute(array, AXES, pairs)  55.1 us
    ppermute x13, starting transfers between devices, shifted(): return lax.ppermute(array, AXES, pairs)  39.3 us
    pallas_call x3, Pallas kernels, compare(): pl.pallas_call(functools.partial(pairs_kernel, [part[1] for part in parts...  11.8 us
    pallas_call x1, Pallas kernels, own_tile(): pl.pallas_call(own_kernel, out_shape=jax.ShapeDtypeStruct((blocks, count)...  5.88 us
    pallas_call x1, Pallas kernels, normalize(): pl.pallas_call(unit_kernel, out_shape=jax.ShapeDtypeStruct((blocks * coun...  3.02 us
    pallas_call x1, Pallas kernels, with_corner(): pl.pallas_call(corner_kernel, out_shape=jax.ShapeDtypeStruct(down.shape,...  2.44 us
  transfers between devices with their start and end apart: 13, of which 6 were waited for; matrix products, arithmetic and copies ran while one was open for 1% of the time, Pallas kernels for 14%

profile of v4, /device:TPU:23, one launch (start us, length us, event | category | flops | bytes accessed | tf_op | source)
XLA Modules:
  0.0 121.2 jit_solution(14865392442953527467)
XLA Ops:
  0.0 3.0 %shard_map.64.units.refs_1_ = bf16[1040,1024]{1,0:T(8,128)(2,1)} custom-call(s32[8]{0:T(128)} %cluster.1, s32[8]{0:T(128)} %live.1, bf16[8,128,1024]{2,1,0:T(8,128)(2,1)} %embeddings.1), custom_call_target="tpu_custom_call" | custom-call | flops 4194304 | bytes 4194304 | tf_op jit(solution)/shard_map/pallas_call | solution.py:74
  3.0 0.6 collective-permute-start.1
  3.6 3.5 %collective-permute-start = (bf16[1040,1024]{1,0:T(8,128)(2,1)}, bf16[1040,1024]{1,0:T(8,128)(2,1)S(1)}, u32[]{:S(2)}, u32[]{:S(2)}) collective-permute-start(bf16[1040,1024]{1,0:T(8,128)(2,1)} %shard_map.64.units.refs_1_), channel_id=1, source_target_pairs={{0,4},{1,5},{2,6},{3,7},{4,8},{5,9},{6,10},{7,11},{8,12},{9,13},{1... | collective-permute-start | bytes 6389768 | tf_op jit(solution)/shard_map/ppermute | solution.py:23
  7.2 2.2 %collective-permute-start.2 = (bf16[1040,1024]{1,0:T(8,128)(2,1)}, bf16[1040,1024]{1,0:T(8,128)(2,1)}, u32[]{:S(2)}, u32[]{:S(2)}) collective-permute-start(bf16[1040,1024]{1,0:T(8,128)(2,1)} %shard_map.64.units.refs_1_), channel_id=1, source_target_pairs={{0,1},{1,2},{2,3},{3,0},{4,5},{5,6},{6,7},{7,4},{8,9},{9,10},{10,1... | collective-permute-start | bytes 6389768 | tf_op jit(solution)/shard_map/ppermute | solution.py:23
  9.4 5.1 %collective-permute-start.3 = (bf16[1040,1024]{1,0:T(8,128)(2,1)}, bf16[1040,1024]{1,0:T(8,128)(2,1)}, u32[]{:S(2)}, u32[]{:S(2)}) collective-permute-start(bf16[1040,1024]{1,0:T(8,128)(2,1)} %shard_map.64.units.refs_1_), channel_id=1, source_target_pairs={{4,0},{5,1},{6,2},{7,3},{8,4},{9,5},{10,6},{11,7},{12,8},{13,9},{1... | collective-permute-start | bytes 6389768 | tf_op jit(solution)/shard_map/ppermute | solution.py:23
  14.5 5.9 %shard_map.65 = f32[8,128]{1,0:T(8,128)} custom-call(s32[8]{0:T(128)} %cluster.1, s32[8]{0:T(128)} %live.1, bf16[1040,1024]{1,0:T(8,128)(2,1)} %shard_map.64.units.refs_1_), custom_call_target="tpu_custom_call" | custom-call | flops 2147483648 | bytes 2097152 | tf_op jit(solution)/shard_map/pallas_call | solution.py:121
  20.4 31.4 %collective-permute-done.1.refs_0_ = bf16[1040,1024]{1,0:T(8,128)(2,1)} collective-permute-done((bf16[1040,1024]{1,0:T(8,128)(2,1)}, bf16[1040,1024]{1,0:T(8,128)(2,1)}, u32[]{:S(2)}, u32[]{:S(2)}) %collective-permute-start.1) | collective-permute-done | bytes 2129952 | tf_op jit(solution)/shard_map/ppermute | solution.py:23
  51.8 4.9 %collective-permute-done.refs_3_.up.refs_0_ = bf16[1040,1024]{1,0:T(8,128)(2,1)S(1)} collective-permute-done((bf16[1040,1024]{1,0:T(8,128)(2,1)}, bf16[1040,1024]{1,0:T(8,128)(2,1)S(1)}, u32[]{:S(2)}, u32[]{:S(2)}) %collective-permute-start) | collective-permute-done | bytes 2129952 | tf_op jit(solution)/shard_map/ppermute | solution.py:23
  56.7 1.9 %collective-permute-start.6 = (bf16[1040,1024]{1,0:T(8,128)(2,1)}, bf16[1040,1024]{1,0:T(8,128)(2,1)}, u32[]{:S(2)}, u32[]{:S(2)}) collective-permute-start(bf16[1040,1024]{1,0:T(8,128)(2,1)} %collective-permute-done.1.refs_0_), channel_id=1, source_target_pairs={{12,16},{13,17},{14,18},{15,19},{16,20},{17,21},{18,22},{19,23},{2... | collective-permute-start | bytes 6389768 | tf_op jit(solution)/shard_map/ppermute | solution.py:23
  58.7 2.0 %collective-permute-start.4 = (bf16[1040,1024]{1,0:T(8,128)(2,1)S(1)}, bf16[1040,1024]{1,0:T(8,128)(2,1)}, u32[]{:S(2)}, u32[]{:S(2)}) collective-permute-start(bf16[1040,1024]{1,0:T(8,128)(2,1)S(1)} %collective-permute-done.refs_3_.up.refs_0_), channel_id=1, source_target_pairs={{0,3},{1,0},{2,1},{3,2},{4,7},{5,4},{6,5},{7,6},{8,11},{9,8},{10,9... | collective-permute-start | bytes 6389768 | tf_op jit(solution)/shard_map/ppermute | solution.py:23
  60.7 1.3 %collective-permute-start.8 = (bf16[1040,1024]{1,0:T(8,128)(2,1)}, bf16[1040,1024]{1,0:T(8,128)(2,1)}, u32[]{:S(2)}, u32[]{:S(2)}) collective-permute-start(bf16[1040,1024]{1,0:T(8,128)(2,1)} %collective-permute-done.1.refs_0_), channel_id=1, source_target_pairs={{23,19},{27,23},{31,27},{35,31},{55,51},{59,55},{63,59},{67,63},{8... | collective-permute-start | bytes 6389768 | tf_op jit(solution)/shard_map/ppermute | solution.py:23
  61.9 0.0 collective-permute-done.2.refs_2_.refs_0_
  62.0 2.1 %collective-permute-start.7 = (bf16[1040,1024]{1,0:T(8,128)(2,1)}, bf16[1040,1024]{1,0:T(8,128)(2,1)}, u32[]{:S(2)}, u32[]{:S(2)}) collective-permute-start(bf16[1040,1024]{1,0:T(8,128)(2,1)} %collective-permute-done.2.refs_2_.refs_0_), channel_id=1, source_target_pairs={{21,17},{22,18},{25,21},{26,22},{29,25},{30,26},{33,29},{34,30},{5... | collective-permute-start | bytes 6389768 | tf_op jit(solution)/shard_map/ppermute | solution.py:23
  64.0 0.0 collective-permute-done.3.down
  64.0 0.0 copy-done
  64.0 2.4 %shard_map.67.refs_1_ = bf16[1040,1024]{1,0:T(8,128)(2,1)} custom-call(s32[1]{0:T(128)} %bitcast.11.flags, bf16[1040,1024]{1,0:T(8,128)(2,1)} %collective-permute-done.3.down, bf16[1040,1024]{1,0:T(8,128)(2,1)} %copy-done), custom_call_target="tpu_custom_call", output_to_operand_aliasing={{}: (1, {})} | custom-call | bytes 4259840 | tf_op jit(solution)/shard_map/pallas_call | solution.py:318
  66.5 2.0 %collective-permute-start.5 = (bf16[1040,1024]{1,0:T(8,128)(2,1)}, bf16[1040,1024]{1,0:T(8,128)(2,1)}, u32[]{:S(2)}, u32[]{:S(2)}) collective-permute-start(bf16[1040,1024]{1,0:T(8,128)(2,1)} %shard_map.67.refs_1_), channel_id=1, source_target_pairs={{0,1},{1,2},{3,0},{4,5},{5,6},{7,4},{8,9},{9,10},{11,8},{12,13},{1... | collective-permute-start | bytes 6389768 | tf_op jit(solution)/shard_map/ppermute | solution.py:23
  68.5 0.1 stack.67
  68.6 0.5 convert_element_type.4.flags
  69.1 6.0 %shard_map.66 = (f32[8,128]{1,0:T(8,128)}, f32[8,128]{1,0:T(8,128)}, f32[8,128]{1,0:T(8,128)}, f32[8,128]{1,0:T(8,128)}) custom-call(s32[25]{0:T(128)} %constant.66.clone.jobs, s32[10]{0:T(128)} %convert_element_type.4.flags, bf16[1040,1024]{1,0:T(8,128)(2,1)} %collective-permute-done.1.refs_0_, bf16[1040,1024]{1,0:T(8,128)(2,1)} %shard_map.64.units.refs_1_, ...), custom_call_target="tpu_custom_call" | custom-call | flops 10737418240 | bytes 8519680 | tf_op jit(solution)/shard_map/pallas_call | solution.py:275
  75.2 10.8 %collective-permute-done.6.refs_3_.refs_4_ = bf16[1040,1024]{1,0:T(8,128)(2,1)} collective-permute-done((bf16[1040,1024]{1,0:T(8,128)(2,1)}, bf16[1040,1024]{1,0:T(8,128)(2,1)}, u32[]{:S(2)}, u32[]{:S(2)}) %collective-permute-start.6) | collective-permute-done | bytes 2129952 | tf_op jit(solution)/shard_map/ppermute | solution.py:23
  86.0 0.0 collective-permute-done.4.refs_2_
  86.0 2.8 %shard_map.68 = (f32[8,128]{1,0:T(8,128)}, f32[8,128]{1,0:T(8,128)}, f32[8,128]{1,0:T(8,128)}) custom-call(s32[20]{0:T(128)} %constant.67.clone.jobs, s32[10]{0:T(128)} %convert_element_type.4.flags, bf16[1040,1024]{1,0:T(8,128)(2,1)} %collective-permute-done.2.refs_2_.refs_0_, bf16[1040,1024]{1,0:T(8,128)(2,1)} %shard_map.67.refs_1_, ...), custom_call_target="tpu_custom_call" | custom-call | flops 8589934592 | bytes 8519680 | tf_op jit(solution)/shard_map/pallas_call | solution.py:275
  88.8 0.0 collective-permute-done.7.refs_5_
  88.8 0.0 collective-permute-done.8.refs_6_
  88.8 0.0 collective-permute-done.5.refs_3_
  88.9 0.0 copy-start.4
  88.9 0.0 copy-start.5
  88.9 0.0 copy-start.3
  88.9 0.0 copy-start.1
  88.9 0.0 copy-start.2
  88.9 0.0 copy-start.6
  88.9 3.0 %shard_map.69 = (f32[8,128]{1,0:T(8,128)}, f32[8,128]{1,0:T(8,128)}, f32[8,128]{1,0:T(8,128)}, f32[8,128]{1,0:T(8,128)}) custom-call(s32[20]{0:T(128)} %constant.68.clone.jobs, s32[10]{0:T(128)} %convert_element_type.4.flags, bf16[1040,1024]{1,0:T(8,128)(2,1)} %copy-done, bf16[1040,1024]{1,0:T(8,128)(2,1)} %shard_map.67.refs_1_, ...), custom_call_target="tpu_custom_call" | custom-call | flops 8589934592 | bytes 14909440 | tf_op jit(solution)/shard_map/pallas_call | solution.py:275
  91.9 0.7 select_bitcast_fusion.1
  92.6 0.0 copy-done.4
  92.6 0.7 pad_maximum_fusion
  93.2 2.8 %collective-permute-start.9 = (f32[3,8,128]{2,1,0:T(8,128)S(1)}, f32[3,8,128]{2,1,0:T(8,128)S(1)}, u32[]{:S(2)}, u32[]{:S(2)}) collective-permute-start(f32[3,8,128]{2,1,0:T(8,128)S(1)} %pad_maximum_fusion), channel_id=1, source_target_pairs={{0,1},{1,2},{2,3},{3,0},{4,5},{5,6},{6,7},{7,4},{8,9},{9,10},{10,1... | collective-permute-start | bytes 36872 | tf_op jit(solution)/shard_map/ppermute | solution.py:23
  96.0 0.0 copy-done.5
  96.1 0.0 collective-permute-start.10
  96.1 0.8 collective-permute-done.9
  96.9 2.9 %collective-permute-done.10 = f32[3,8,128]{2,1,0:T(8,128)S(1)} collective-permute-done((f32[3,8,128]{2,1,0:T(8,128)S(1)}, f32[3,8,128]{2,1,0:T(8,128)S(1)}, u32[]{:S(2)}, u32[]{:S(2)}) %collective-permute-start.10) | collective-permute-done | bytes 12320 | tf_op jit(solution)/shard_map/ppermute | solution.py:23
  99.8 0.7 fusion.1
  100.5 13.8 %collective-permute-start.11 = (f32[8,128]{1,0:T(8,128)S(1)}, f32[8,128]{1,0:T(8,128)S(1)}, u32[]{:S(2)}, u32[]{:S(2)}) collective-permute-start(f32[8,128]{1,0:T(8,128)S(1)} %get-tuple-element.33), channel_id=1, source_target_pairs={{4,0},{5,1},{6,2},{7,3},{8,4},{9,5},{10,6},{11,7},{12,8},{13,9},{1... | collective-permute-start | bytes 12296 | tf_op jit(solution)/shard_map/ppermute | solution.py:23
  114.3 1.9 %collective-permute-start.12 = (f32[8,128]{1,0:T(8,128)S(1)}, f32[8,128]{1,0:T(8,128)S(1)}, u32[]{:S(2)}, u32[]{:S(2)}) collective-permute-start(f32[8,128]{1,0:T(8,128)S(1)} %get-tuple-element.34), channel_id=1, source_target_pairs={{0,4},{1,5},{2,6},{3,7},{4,8},{5,9},{6,10},{7,11},{8,12},{9,13},{1... | collective-permute-start | bytes 12296 | tf_op jit(solution)/shard_map/ppermute | solution.py:23
  116.3 0.0 collective-permute-done.11
  116.3 4.2 %collective-permute-done.12 = f32[8,128]{1,0:T(8,128)S(1)} collective-permute-done((f32[8,128]{1,0:T(8,128)S(1)}, f32[8,128]{1,0:T(8,128)S(1)}, u32[]{:S(2)}, u32[]{:S(2)}) %collective-permute-start.12) | collective-permute-done | bytes 4128 | tf_op jit(solution)/shard_map/ppermute | solution.py:23
  120.5 0.0 copy-done.2
  120.5 0.7 fusion.8
  (6 shorter events, 0.0 us)
Async XLA Ops:
  3.0 48.8 %collective-permute-start.1 = (bf16[1040,1024]{1,0:T(8,128)(2,1)}, bf16[1040,1024]{1,0:T(8,128)(2,1)}, u32[]{:S(2)}, u32[]{:S(2)}) collective-permute-start(bf16[1040,1024]{1,0:T(8,128)(2,1)} %shard_map.64.units.refs_1_), channel_id=1, source_target_pairs={{0,3},{1,0},{2,1},{3,2},{4,7},{5,4},{6,5},{7,6},{8,11},{9,8},{10,9... | collective-permute-start | bytes 6389768 | tf_op jit(solution)/shard_map/ppermute | solution.py:23
  3.6 53.1 %collective-permute-start = (bf16[1040,1024]{1,0:T(8,128)(2,1)}, bf16[1040,1024]{1,0:T(8,128)(2,1)S(1)}, u32[]{:S(2)}, u32[]{:S(2)}) collective-permute-start(bf16[1040,1024]{1,0:T(8,128)(2,1)} %shard_map.64.units.refs_1_), channel_id=1, source_target_pairs={{0,4},{1,5},{2,6},{3,7},{4,8},{5,9},{6,10},{7,11},{8,12},{9,13},{1... | collective-permute-start | bytes 6389768 | tf_op jit(solution)/shard_map/ppermute | solution.py:23
  7.2 54.8 %collective-permute-start.2 = (bf16[1040,1024]{1,0:T(8,128)(2,1)}, bf16[1040,1024]{1,0:T(8,128)(2,1)}, u32[]{:S(2)}, u32[]{:S(2)}) collective-permute-start(bf16[1040,1024]{1,0:T(8,128)(2,1)} %shard_map.64.units.refs_1_), channel_id=1, source_target_pairs={{0,1},{1,2},{2,3},{3,0},{4,5},{5,6},{6,7},{7,4},{8,9},{9,10},{10,1... | collective-permute-start | bytes 6389768 | tf_op jit(solution)/shard_map/ppermute | solution.py:23
  9.4 54.6 %collective-permute-start.3 = (bf16[1040,1024]{1,0:T(8,128)(2,1)}, bf16[1040,1024]{1,0:T(8,128)(2,1)}, u32[]{:S(2)}, u32[]{:S(2)}) collective-permute-start(bf16[1040,1024]{1,0:T(8,128)(2,1)} %shard_map.64.units.refs_1_), channel_id=1, source_target_pairs={{4,0},{5,1},{6,2},{7,3},{8,4},{9,5},{10,6},{11,7},{12,8},{13,9},{1... | collective-permute-start | bytes 6389768 | tf_op jit(solution)/shard_map/ppermute | solution.py:23
  56.7 7.3 %copy-start = (bf16[1040,1024]{1,0:T(8,128)(2,1)}, bf16[1040,1024]{1,0:T(8,128)(2,1)S(1)}, u32[]{:S(2)}) copy-start(bf16[1040,1024]{1,0:T(8,128)(2,1)S(1)} %collective-permute-done.refs_3_.up.refs_0_) | copy-start | bytes 6389764
  56.7 29.2 %collective-permute-start.6 = (bf16[1040,1024]{1,0:T(8,128)(2,1)}, bf16[1040,1024]{1,0:T(8,128)(2,1)}, u32[]{:S(2)}, u32[]{:S(2)}) collective-permute-start(bf16[1040,1024]{1,0:T(8,128)(2,1)} %collective-permute-done.1.refs_0_), channel_id=1, source_target_pairs={{12,16},{13,17},{14,18},{15,19},{16,20},{17,21},{18,22},{19,23},{2... | collective-permute-start | bytes 6389768 | tf_op jit(solution)/shard_map/ppermute | solution.py:23
  58.7 27.3 %collective-permute-start.4 = (bf16[1040,1024]{1,0:T(8,128)(2,1)S(1)}, bf16[1040,1024]{1,0:T(8,128)(2,1)}, u32[]{:S(2)}, u32[]{:S(2)}) collective-permute-start(bf16[1040,1024]{1,0:T(8,128)(2,1)S(1)} %collective-permute-done.refs_3_.up.refs_0_), channel_id=1, source_target_pairs={{0,3},{1,0},{2,1},{3,2},{4,7},{5,4},{6,5},{7,6},{8,11},{9,8},{10,9... | collective-permute-start | bytes 6389768 | tf_op jit(solution)/shard_map/ppermute | solution.py:23
  60.7 28.2 %collective-permute-start.8 = (bf16[1040,1024]{1,0:T(8,128)(2,1)}, bf16[1040,1024]{1,0:T(8,128)(2,1)}, u32[]{:S(2)}, u32[]{:S(2)}) collective-permute-start(bf16[1040,1024]{1,0:T(8,128)(2,1)} %collective-permute-done.1.refs_0_), channel_id=1, source_target_pairs={{23,19},{27,23},{31,27},{35,31},{55,51},{59,55},{63,59},{67,63},{8... | collective-permute-start | bytes 6389768 | tf_op jit(solution)/shard_map/ppermute | solution.py:23
  62.0 26.9 %collective-permute-start.7 = (bf16[1040,1024]{1,0:T(8,128)(2,1)}, bf16[1040,1024]{1,0:T(8,128)(2,1)}, u32[]{:S(2)}, u32[]{:S(2)}) collective-permute-start(bf16[1040,1024]{1,0:T(8,128)(2,1)} %collective-permute-done.2.refs_2_.refs_0_), channel_id=1, source_target_pairs={{21,17},{22,18},{25,21},{26,22},{29,25},{30,26},{33,29},{34,30},{5... | collective-permute-start | bytes 6389768 | tf_op jit(solution)/shard_map/ppermute | solution.py:23
  66.5 22.4 %collective-permute-start.5 = (bf16[1040,1024]{1,0:T(8,128)(2,1)}, bf16[1040,1024]{1,0:T(8,128)(2,1)}, u32[]{:S(2)}, u32[]{:S(2)}) collective-permute-start(bf16[1040,1024]{1,0:T(8,128)(2,1)} %shard_map.67.refs_1_), channel_id=1, source_target_pairs={{0,1},{1,2},{3,0},{4,5},{5,6},{7,4},{8,9},{9,10},{11,8},{12,13},{1... | collective-permute-start | bytes 6389768 | tf_op jit(solution)/shard_map/ppermute | solution.py:23
  88.9 3.7 %copy-start.4 = (f32[8,128]{1,0:T(8,128)S(1)}, f32[8,128]{1,0:T(8,128)}, u32[]{:S(2)}) copy-start(f32[8,128]{1,0:T(8,128)} %get-tuple-element.23) | copy-start | bytes 12292
  88.9 7.2 %copy-start.5 = (f32[8,128]{1,0:T(8,128)S(1)}, f32[8,128]{1,0:T(8,128)}, u32[]{:S(2)}) copy-start(f32[8,128]{1,0:T(8,128)} %get-tuple-element.29) | copy-start | bytes 12292
  88.9 10.9 %copy-start.3 = (f32[8,128]{1,0:T(8,128)S(1)}, f32[8,128]{1,0:T(8,128)}, u32[]{:S(2)}) copy-start(f32[8,128]{1,0:T(8,128)} %get-tuple-element.30) | copy-start | bytes 12292
  88.9 31.6 %copy-start.1 = (f32[8,128]{1,0:T(8,128)S(1)}, f32[8,128]{1,0:T(8,128)}, u32[]{:S(2)}) copy-start(f32[8,128]{1,0:T(8,128)} %shard_map.65) | copy-start | bytes 12292
  88.9 31.6 %copy-start.2 = (f32[8,128]{1,0:T(8,128)S(1)}, f32[8,128]{1,0:T(8,128)}, u32[]{:S(2)}) copy-start(f32[8,128]{1,0:T(8,128)} %get-tuple-element.22) | copy-start | bytes 12292
  88.9 31.6 %copy-start.6 = (s32[8]{0:T(128)S(1)}, s32[8]{0:T(128)}, u32[]{:S(2)}) copy-start(s32[8]{0:T(128)} %live.1) | copy-start | bytes 100
  93.2 3.6 %collective-permute-start.9 = (f32[3,8,128]{2,1,0:T(8,128)S(1)}, f32[3,8,128]{2,1,0:T(8,128)S(1)}, u32[]{:S(2)}, u32[]{:S(2)}) collective-permute-start(f32[3,8,128]{2,1,0:T(8,128)S(1)} %pad_maximum_fusion), channel_id=1, source_target_pairs={{0,1},{1,2},{2,3},{3,0},{4,5},{5,6},{6,7},{7,4},{8,9},{9,10},{10,1... | collective-permute-start | bytes 36872 | tf_op jit(solution)/shard_map/ppermute | solution.py:23
  96.1 3.8 %collective-permute-start.10 = (f32[3,8,128]{2,1,0:T(8,128)S(1)}, f32[3,8,128]{2,1,0:T(8,128)S(1)}, u32[]{:S(2)}, u32[]{:S(2)}) collective-permute-start(f32[3,8,128]{2,1,0:T(8,128)S(1)} %pad_maximum_fusion.1), channel_id=1, source_target_pairs={{0,3},{1,0},{2,1},{3,2},{4,7},{5,4},{6,5},{7,6},{8,11},{9,8},{10,9... | collective-permute-start | bytes 36872 | tf_op jit(solution)/shard_map/ppermute | solution.py:23
  100.5 15.8 %collective-permute-start.11 = (f32[8,128]{1,0:T(8,128)S(1)}, f32[8,128]{1,0:T(8,128)S(1)}, u32[]{:S(2)}, u32[]{:S(2)}) collective-permute-start(f32[8,128]{1,0:T(8,128)S(1)} %get-tuple-element.33), channel_id=1, source_target_pairs={{4,0},{5,1},{6,2},{7,3},{8,4},{9,5},{10,6},{11,7},{12,8},{13,9},{1... | collective-permute-start | bytes 12296 | tf_op jit(solution)/shard_map/ppermute | solution.py:23
  114.3 6.1 %collective-permute-start.12 = (f32[8,128]{1,0:T(8,128)S(1)}, f32[8,128]{1,0:T(8,128)S(1)}, u32[]{:S(2)}, u32[]{:S(2)}) collective-permute-start(f32[8,128]{1,0:T(8,128)S(1)} %get-tuple-element.34), channel_id=1, source_target_pairs={{0,4},{1,5},{2,6},{3,7},{4,8},{5,9},{6,10},{7,11},{8,12},{9,13},{1... | collective-permute-start | bytes 12296 | tf_op jit(solution)/shard_map/ppermute | solution.py:23

commit v5 on v4

--- a/solution.py
+++ b/solution.py
@@ -375,7 +375,9 @@
     up, nxt = shifted(units, below), shifted(units, left)
     down, prv = shifted(units, above), shifted(units, right)
     best = own_tile(units, block_cluster, block_rows)
-    up, nxt, best = lax.optimization_barrier((up, nxt, best))
+    up, first_best = lax.optimization_barrier((up, best))
+    nxt, second_best = lax.optimization_barrier((nxt, best))
+    best = jnp.maximum(first_best, second_best)
     up_next_even = shifted(up, ring(devices, -1, even))
     up_next_odd = shifted(nxt, column(devices, 1, odd))
     down = with_corner((x == ROW - 1).astype(jnp.int32)[None], down, up)

time: 122 us -> 119 us (0.975)
  the two profiles are of different devices: /device:TPU:23 before, /device:TPU:32 now
where the time goes in v5:
time: 119 us; the launch traced here: 117 us
  waiting for transfers between devices  46.9 us (39%)
  Pallas kernels  36.4 us (31%)
  starting transfers between devices  29.9 us (25%)
  other arithmetic  3.23 us (3%)
    ppermute x13, waiting for transfers between devices, shifted(): return lax.ppermute(array, AXES, pairs)  46.9 us
    ppermute x13, starting transfers between devices, shifted(): return lax.ppermute(array, AXES, pairs)  29.9 us
    pallas_call x3, Pallas kernels, compare(): pl.pallas_call(functools.partial(pairs_kernel, [part[1] for part in parts...  27.3 us
    pallas_call x1, Pallas kernels, own_tile(): pl.pallas_call(own_kernel, out_shape=jax.ShapeDtypeStruct((blocks, count)...  5.89 us
    pallas_call x1, Pallas kernels, normalize(): pl.pallas_call(unit_kernel, out_shape=jax.ShapeDtypeStruct((blocks * coun...  3.02 us
  transfers between devices with their start and end apart: 13, of which 5 were waited for; matrix products, arithmetic and copies ran while one was open for 1% of the time, Pallas kernels for 22%

profile of v5, /device:TPU:32, one launch (start us, length us, event | category | flops | bytes accessed | tf_op | source)
XLA Modules:
  0.0 116.8 jit_solution(10690777709581435761)
XLA Ops:
  0.0 3.0 %shard_map.64.units.refs_1_ = bf16[1040,1024]{1,0:T(8,128)(2,1)} custom-call(s32[8]{0:T(128)} %cluster.1, s32[8]{0:T(128)} %live.1, bf16[8,128,1024]{2,1,0:T(8,128)(2,1)} %embeddings.1), custom_call_target="tpu_custom_call" | custom-call | flops 4194304 | bytes 4194304 | tf_op jit(solution)/shard_map/pallas_call | solution.py:74
  3.0 2.8 %collective-permute-start.1 = (bf16[1040,1024]{1,0:T(8,128)(2,1)}, bf16[1040,1024]{1,0:T(8,128)(2,1)}, u32[]{:S(2)}, u32[]{:S(2)}) collective-permute-start(bf16[1040,1024]{1,0:T(8,128)(2,1)} %shard_map.64.units.refs_1_), channel_id=1, source_target_pairs={{0,3},{1,0},{2,1},{3,2},{4,7},{5,4},{6,5},{7,6},{8,11},{9,8},{10,9... | collective-permute-start | bytes 6389768 | tf_op jit(solution)/shard_map/ppermute | solution.py:23
  5.9 3.8 %collective-permute-start = (bf16[1040,1024]{1,0:T(8,128)(2,1)}, bf16[1040,1024]{1,0:T(8,128)(2,1)S(1)}, u32[]{:S(2)}, u32[]{:S(2)}) collective-permute-start(bf16[1040,1024]{1,0:T(8,128)(2,1)} %shard_map.64.units.refs_1_), channel_id=1, source_target_pairs={{0,4},{1,5},{2,6},{3,7},{4,8},{5,9},{6,10},{7,11},{8,12},{9,13},{1... | collective-permute-start | bytes 6389768 | tf_op jit(solution)/shard_map/ppermute | solution.py:23
  9.7 0.1 collective-permute-start.2
  9.8 2.1 %collective-permute-start.3 = (bf16[1040,1024]{1,0:T(8,128)(2,1)}, bf16[1040,1024]{1,0:T(8,128)(2,1)}, u32[]{:S(2)}, u32[]{:S(2)}) collective-permute-start(bf16[1040,1024]{1,0:T(8,128)(2,1)} %shard_map.64.units.refs_1_), channel_id=1, source_target_pairs={{4,0},{5,1},{6,2},{7,3},{8,4},{9,5},{10,6},{11,7},{12,8},{13,9},{1... | collective-permute-start | bytes 6389768 | tf_op jit(solution)/shard_map/ppermute | solution.py:23
  11.9 5.9 %shard_map.65 = f32[8,128]{1,0:T(8,128)} custom-call(s32[8]{0:T(128)} %cluster.1, s32[8]{0:T(128)} %live.1, bf16[1040,1024]{1,0:T(8,128)(2,1)} %shard_map.64.units.refs_1_), custom_call_target="tpu_custom_call" | custom-call | flops 2147483648 | bytes 2097152 | tf_op jit(solution)/shard_map/pallas_call | solution.py:121
  17.8 34.0 %collective-permute-done.1.refs_0_ = bf16[1040,1024]{1,0:T(8,128)(2,1)} collective-permute-done((bf16[1040,1024]{1,0:T(8,128)(2,1)}, bf16[1040,1024]{1,0:T(8,128)(2,1)}, u32[]{:S(2)}, u32[]{:S(2)}) %collective-permute-start.1) | collective-permute-done | bytes 2129952 | tf_op jit(solution)/shard_map/ppermute | solution.py:23
  51.8 2.0 %collective-permute-start.6 = (bf16[1040,1024]{1,0:T(8,128)(2,1)}, bf16[1040,1024]{1,0:T(8,128)(2,1)}, u32[]{:S(2)}, u32[]{:S(2)}) collective-permute-start(bf16[1040,1024]{1,0:T(8,128)(2,1)} %collective-permute-done.1.refs_0_), channel_id=1, source_target_pairs={{12,16},{13,17},{14,18},{15,19},{16,20},{17,21},{18,22},{19,23},{2... | collective-permute-start | bytes 6389768 | tf_op jit(solution)/shard_map/ppermute | solution.py:23
  53.8 2.2 %collective-permute-done.refs_3_.up.refs_0_ = bf16[1040,1024]{1,0:T(8,128)(2,1)S(1)} collective-permute-done((bf16[1040,1024]{1,0:T(8,128)(2,1)}, bf16[1040,1024]{1,0:T(8,128)(2,1)S(1)}, u32[]{:S(2)}, u32[]{:S(2)}) %collective-permute-start) | collective-permute-done | bytes 2129952 | tf_op jit(solution)/shard_map/ppermute | solution.py:23
  56.0 3.4 %collective-permute-start.4 = (bf16[1040,1024]{1,0:T(8,128)(2,1)S(1)}, bf16[1040,1024]{1,0:T(8,128)(2,1)}, u32[]{:S(2)}, u32[]{:S(2)}) collective-permute-start(bf16[1040,1024]{1,0:T(8,128)(2,1)S(1)} %collective-permute-done.refs_3_.up.refs_0_), channel_id=1, source_target_pairs={{0,3},{1,0},{2,1},{3,2},{4,7},{5,4},{6,5},{7,6},{8,11},{9,8},{10,9... | collective-permute-start | bytes 6389768 | tf_op jit(solution)/shard_map/ppermute | solution.py:23
  59.4 2.1 %collective-permute-start.8 = (bf16[1040,1024]{1,0:T(8,128)(2,1)}, bf16[1040,1024]{1,0:T(8,128)(2,1)}, u32[]{:S(2)}, u32[]{:S(2)}) collective-permute-start(bf16[1040,1024]{1,0:T(8,128)(2,1)} %collective-permute-done.1.refs_0_), channel_id=1, source_target_pairs={{23,19},{27,23},{31,27},{35,31},{55,51},{59,55},{63,59},{67,63},{8... | collective-permute-start | bytes 6389768 | tf_op jit(solution)/shard_map/ppermute | solution.py:23
  61.5 0.0 collective-permute-done.2.refs_2_.refs_0_
  61.5 2.1 %collective-permute-start.7 = (bf16[1040,1024]{1,0:T(8,128)(2,1)}, bf16[1040,1024]{1,0:T(8,128)(2,1)}, u32[]{:S(2)}, u32[]{:S(2)}) collective-permute-start(bf16[1040,1024]{1,0:T(8,128)(2,1)} %collective-permute-done.2.refs_2_.refs_0_), channel_id=1, source_target_pairs={{21,17},{22,18},{25,21},{26,22},{29,25},{30,26},{33,29},{34,30},{5... | collective-permute-start | bytes 6389768 | tf_op jit(solution)/shard_map/ppermute | solution.py:23
  63.5 0.0 collective-permute-done.3.down
  63.5 0.0 copy-done
  63.5 0.2 shard_map.67.refs_1_
  63.7 2.4 %collective-permute-start.5 = (bf16[1040,1024]{1,0:T(8,128)(2,1)}, bf16[1040,1024]{1,0:T(8,128)(2,1)}, u32[]{:S(2)}, u32[]{:S(2)}) collective-permute-start(bf16[1040,1024]{1,0:T(8,128)(2,1)} %shard_map.67.refs_1_), channel_id=1, source_target_pairs={{0,1},{1,2},{3,0},{4,5},{5,6},{7,4},{8,9},{9,10},{11,8},{12,13},{1... | collective-permute-start | bytes 6389768 | tf_op jit(solution)/shard_map/ppermute | solution.py:23
  66.2 0.1 stack.67
  66.3 0.5 convert_element_type.4.flags
  66.8 10.0 %shard_map.66 = (f32[8,128]{1,0:T(8,128)}, f32[8,128]{1,0:T(8,128)}, f32[8,128]{1,0:T(8,128)}, f32[8,128]{1,0:T(8,128)}) custom-call(s32[25]{0:T(128)} %constant.66.clone.jobs, s32[10]{0:T(128)} %convert_element_type.4.flags, bf16[1040,1024]{1,0:T(8,128)(2,1)} %collective-permute-done.1.refs_0_, bf16[1040,1024]{1,0:T(8,128)(2,1)} %shard_map.64.units.refs_1_, ...), custom_call_target="tpu_custom_call" | custom-call | flops 10737418240 | bytes 8519680 | tf_op jit(solution)/shard_map/pallas_call | solution.py:275
  76.9 0.0 collective-permute-done.6.refs_3_.refs_4_
  76.9 7.5 %collective-permute-done.4.refs_2_ = bf16[1040,1024]{1,0:T(8,128)(2,1)} collective-permute-done((bf16[1040,1024]{1,0:T(8,128)(2,1)S(1)}, bf16[1040,1024]{1,0:T(8,128)(2,1)}, u32[]{:S(2)}, u32[]{:S(2)}) %collective-permute-start.4) | collective-permute-done | bytes 2129952 | tf_op jit(solution)/shard_map/ppermute | solution.py:23
  84.4 9.7 %shard_map.68 = (f32[8,128]{1,0:T(8,128)}, f32[8,128]{1,0:T(8,128)}, f32[8,128]{1,0:T(8,128)}) custom-call(s32[20]{0:T(128)} %constant.67.clone.jobs, s32[10]{0:T(128)} %convert_element_type.4.flags, bf16[1040,1024]{1,0:T(8,128)(2,1)} %collective-permute-done.2.refs_2_.refs_0_, bf16[1040,1024]{1,0:T(8,128)(2,1)} %shard_map.67.refs_1_, ...), custom_call_target="tpu_custom_call" | custom-call | flops 8589934592 | bytes 8519680 | tf_op jit(solution)/shard_map/pallas_call | solution.py:275
  94.1 0.0 collective-permute-done.7.refs_5_
  94.1 0.0 collective-permute-done.8.refs_6_
  94.1 0.0 collective-permute-done.5.refs_3_
  94.1 0.0 copy-start.4
  94.1 0.0 copy-start.5
  94.1 0.0 copy-start.3
  94.1 0.0 copy-start.1
  94.1 0.0 copy-start.2
  94.2 0.0 copy-start.6
  94.2 7.6 %shard_map.69 = (f32[8,128]{1,0:T(8,128)}, f32[8,128]{1,0:T(8,128)}, f32[8,128]{1,0:T(8,128)}, f32[8,128]{1,0:T(8,128)}) custom-call(s32[20]{0:T(128)} %constant.68.clone.jobs, s32[10]{0:T(128)} %convert_element_type.4.flags, bf16[1040,1024]{1,0:T(8,128)(2,1)} %copy-done, bf16[1040,1024]{1,0:T(8,128)(2,1)} %shard_map.67.refs_1_, ...), custom_call_target="tpu_custom_call" | custom-call | flops 8589934592 | bytes 14909440 | tf_op jit(solution)/shard_map/pallas_call | solution.py:275
  101.8 0.7 select_bitcast_fusion.1
  102.4 0.0 copy-done.4
  102.4 0.7 pad_maximum_fusion
  103.1 0.0 collective-permute-start.9
  103.1 0.0 copy-done.5
  103.1 3.2 %collective-permute-start.10 = (f32[3,8,128]{2,1,0:T(8,128)S(1)}, f32[3,8,128]{2,1,0:T(8,128)S(1)}, u32[]{:S(2)}, u32[]{:S(2)}) collective-permute-start(f32[3,8,128]{2,1,0:T(8,128)S(1)} %pad_maximum_fusion.1), channel_id=1, source_target_pairs={{0,3},{1,0},{2,1},{3,2},{4,7},{5,4},{6,5},{7,6},{8,11},{9,8},{10,9... | collective-permute-start | bytes 36872 | tf_op jit(solution)/shard_map/ppermute | solution.py:23
  106.4 1.7 %collective-permute-done.9 = f32[3,8,128]{2,1,0:T(8,128)S(1)} collective-permute-done((f32[3,8,128]{2,1,0:T(8,128)S(1)}, f32[3,8,128]{2,1,0:T(8,128)S(1)}, u32[]{:S(2)}, u32[]{:S(2)}) %collective-permute-start.9) | collective-permute-done | bytes 12320 | tf_op jit(solution)/shard_map/ppermute | solution.py:23
  108.0 0.0 collective-permute-done.10
  108.0 0.7 fusion.1
  108.7 1.9 %collective-permute-start.11 = (f32[8,128]{1,0:T(8,128)S(1)}, f32[8,128]{1,0:T(8,128)S(1)}, u32[]{:S(2)}, u32[]{:S(2)}) collective-permute-start(f32[8,128]{1,0:T(8,128)S(1)} %get-tuple-element.35), channel_id=1, source_target_pairs={{4,0},{5,1},{6,2},{7,3},{8,4},{9,5},{10,6},{11,7},{12,8},{13,9},{1... | collective-permute-start | bytes 12296 | tf_op jit(solution)/shard_map/ppermute | solution.py:23
  110.6 3.9 %collective-permute-start.12 = (f32[8,128]{1,0:T(8,128)S(1)}, f32[8,128]{1,0:T(8,128)S(1)}, u32[]{:S(2)}, u32[]{:S(2)}) collective-permute-start(f32[8,128]{1,0:T(8,128)S(1)} %get-tuple-element.36), channel_id=1, source_target_pairs={{0,4},{1,5},{2,6},{3,7},{4,8},{5,9},{6,10},{7,11},{8,12},{9,13},{1... | collective-permute-start | bytes 12296 | tf_op jit(solution)/shard_map/ppermute | solution.py:23
  114.6 0.0 collective-permute-done.11
  114.6 1.5 %collective-permute-done.12 = f32[8,128]{1,0:T(8,128)S(1)} collective-permute-done((f32[8,128]{1,0:T(8,128)S(1)}, f32[8,128]{1,0:T(8,128)S(1)}, u32[]{:S(2)}, u32[]{:S(2)}) %collective-permute-start.12) | collective-permute-done | bytes 4128 | tf_op jit(solution)/shard_map/ppermute | solution.py:23
  116.1 0.0 copy-done.1
  116.1 0.7 fusion.8
  (6 shorter events, 0.0 us)
Async XLA Ops:
  3.0 48.7 %collective-permute-start.1 = (bf16[1040,1024]{1,0:T(8,128)(2,1)}, bf16[1040,1024]{1,0:T(8,128)(2,1)}, u32[]{:S(2)}, u32[]{:S(2)}) collective-permute-start(bf16[1040,1024]{1,0:T(8,128)(2,1)} %shard_map.64.units.refs_1_), channel_id=1, source_target_pairs={{0,3},{1,0},{2,1},{3,2},{4,7},{5,4},{6,5},{7,6},{8,11},{9,8},{10,9... | collective-permute-start | bytes 6389768 | tf_op jit(solution)/shard_map/ppermute | solution.py:23
  5.9 50.1 %collective-permute-start = (bf16[1040,1024]{1,0:T(8,128)(2,1)}, bf16[1040,1024]{1,0:T(8,128)(2,1)S(1)}, u32[]{:S(2)}, u32[]{:S(2)}) collective-permute-start(bf16[1040,1024]{1,0:T(8,128)(2,1)} %shard_map.64.units.refs_1_), channel_id=1, source_target_pairs={{0,4},{1,5},{2,6},{3,7},{4,8},{5,9},{6,10},{7,11},{8,12},{9,13},{1... | collective-permute-start | bytes 6389768 | tf_op jit(solution)/shard_map/ppermute | solution.py:23
  9.7 51.8 %collective-permute-start.2 = (bf16[1040,1024]{1,0:T(8,128)(2,1)}, bf16[1040,1024]{1,0:T(8,128)(2,1)}, u32[]{:S(2)}, u32[]{:S(2)}) collective-permute-start(bf16[1040,1024]{1,0:T(8,128)(2,1)} %shard_map.64.units.refs_1_), channel_id=1, source_target_pairs={{0,1},{1,2},{2,3},{3,0},{4,5},{5,6},{6,7},{7,4},{8,9},{9,10},{10,1... | collective-permute-start | bytes 6389768 | tf_op jit(solution)/shard_map/ppermute | solution.py:23
  9.8 53.8 %collective-permute-start.3 = (bf16[1040,1024]{1,0:T(8,128)(2,1)}, bf16[1040,1024]{1,0:T(8,128)(2,1)}, u32[]{:S(2)}, u32[]{:S(2)}) collective-permute-start(bf16[1040,1024]{1,0:T(8,128)(2,1)} %shard_map.64.units.refs_1_), channel_id=1, source_target_pairs={{4,0},{5,1},{6,2},{7,3},{8,4},{9,5},{10,6},{11,7},{12,8},{13,9},{1... | collective-permute-start | bytes 6389768 | tf_op jit(solution)/shard_map/ppermute | solution.py:23
  51.8 25.1 %collective-permute-start.6 = (bf16[1040,1024]{1,0:T(8,128)(2,1)}, bf16[1040,1024]{1,0:T(8,128)(2,1)}, u32[]{:S(2)}, u32[]{:S(2)}) collective-permute-start(bf16[1040,1024]{1,0:T(8,128)(2,1)} %collective-permute-done.1.refs_0_), channel_id=1, source_target_pairs={{12,16},{13,17},{14,18},{15,19},{16,20},{17,21},{18,22},{19,23},{2... | collective-permute-start | bytes 6389768 | tf_op jit(solution)/shard_map/ppermute | solution.py:23
  56.0 7.5 %copy-start = (bf16[1040,1024]{1,0:T(8,128)(2,1)}, bf16[1040,1024]{1,0:T(8,128)(2,1)S(1)}, u32[]{:S(2)}) copy-start(bf16[1040,1024]{1,0:T(8,128)(2,1)S(1)} %collective-permute-done.refs_3_.up.refs_0_) | copy-start | bytes 6389764
  56.0 28.4 %collective-permute-start.4 = (bf16[1040,1024]{1,0:T(8,128)(2,1)S(1)}, bf16[1040,1024]{1,0:T(8,128)(2,1)}, u32[]{:S(2)}, u32[]{:S(2)}) collective-permute-start(bf16[1040,1024]{1,0:T(8,128)(2,1)S(1)} %collective-permute-done.refs_3_.up.refs_0_), channel_id=1, source_target_pairs={{0,3},{1,0},{2,1},{3,2},{4,7},{5,4},{6,5},{7,6},{8,11},{9,8},{10,9... | collective-permute-start | bytes 6389768 | tf_op jit(solution)/shard_map/ppermute | solution.py:23
  59.4 34.7 %collective-permute-start.8 = (bf16[1040,1024]{1,0:T(8,128)(2,1)}, bf16[1040,1024]{1,0:T(8,128)(2,1)}, u32[]{:S(2)}, u32[]{:S(2)}) collective-permute-start(bf16[1040,1024]{1,0:T(8,128)(2,1)} %collective-permute-done.1.refs_0_), channel_id=1, source_target_pairs={{23,19},{27,23},{31,27},{35,31},{55,51},{59,55},{63,59},{67,63},{8... | collective-permute-start | bytes 6389768 | tf_op jit(solution)/shard_map/ppermute | solution.py:23
  61.5 32.6 %collective-permute-start.7 = (bf16[1040,1024]{1,0:T(8,128)(2,1)}, bf16[1040,1024]{1,0:T(8,128)(2,1)}, u32[]{:S(2)}, u32[]{:S(2)}) collective-permute-start(bf16[1040,1024]{1,0:T(8,128)(2,1)} %collective-permute-done.2.refs_2_.refs_0_), channel_id=1, source_target_pairs={{21,17},{22,18},{25,21},{26,22},{29,25},{30,26},{33,29},{34,30},{5... | collective-permute-start | bytes 6389768 | tf_op jit(solution)/shard_map/ppermute | solution.py:23
  63.7 30.4 %collective-permute-start.5 = (bf16[1040,1024]{1,0:T(8,128)(2,1)}, bf16[1040,1024]{1,0:T(8,128)(2,1)}, u32[]{:S(2)}, u32[]{:S(2)}) collective-permute-start(bf16[1040,1024]{1,0:T(8,128)(2,1)} %shard_map.67.refs_1_), channel_id=1, source_target_pairs={{0,1},{1,2},{3,0},{4,5},{5,6},{7,4},{8,9},{9,10},{11,8},{12,13},{1... | collective-permute-start | bytes 6389768 | tf_op jit(solution)/shard_map/ppermute | solution.py:23
  94.1 8.3 %copy-start.4 = (f32[8,128]{1,0:T(8,128)S(1)}, f32[8,128]{1,0:T(8,128)}, u32[]{:S(2)}) copy-start(f32[8,128]{1,0:T(8,128)} %get-tuple-element.25) | copy-start | bytes 12292
  94.1 9.0 %copy-start.5 = (f32[8,128]{1,0:T(8,128)S(1)}, f32[8,128]{1,0:T(8,128)}, u32[]{:S(2)}) copy-start(f32[8,128]{1,0:T(8,128)} %get-tuple-element.31) | copy-start | bytes 12292
  94.1 13.9 %copy-start.3 = (f32[8,128]{1,0:T(8,128)S(1)}, f32[8,128]{1,0:T(8,128)}, u32[]{:S(2)}) copy-start(f32[8,128]{1,0:T(8,128)} %get-tuple-element.32) | copy-start | bytes 12292
  94.1 22.0 %copy-start.1 = (f32[8,128]{1,0:T(8,128)S(1)}, f32[8,128]{1,0:T(8,128)}, u32[]{:S(2)}) copy-start(f32[8,128]{1,0:T(8,128)} %shard_map.65) | copy-start | bytes 12292
  94.1 22.0 %copy-start.2 = (f32[8,128]{1,0:T(8,128)S(1)}, f32[8,128]{1,0:T(8,128)}, u32[]{:S(2)}) copy-start(f32[8,128]{1,0:T(8,128)} %get-tuple-element.24) | copy-start | bytes 12292
  94.2 22.0 %copy-start.6 = (s32[8]{0:T(128)S(1)}, s32[8]{0:T(128)}, u32[]{:S(2)}) copy-start(s32[8]{0:T(128)} %live.1) | copy-start | bytes 100
  103.1 4.9 %collective-permute-start.9 = (f32[3,8,128]{2,1,0:T(8,128)S(1)}, f32[3,8,128]{2,1,0:T(8,128)S(1)}, u32[]{:S(2)}, u32[]{:S(2)}) collective-permute-start(f32[3,8,128]{2,1,0:T(8,128)S(1)} %pad_maximum_fusion), channel_id=1, source_target_pairs={{0,1},{1,2},{2,3},{3,0},{4,5},{5,6},{6,7},{7,4},{8,9},{9,10},{10,1... | collective-permute-start | bytes 36872 | tf_op jit(solution)/shard_map/ppermute | solution.py:23
  103.1 4.9 %collective-permute-start.10 = (f32[3,8,128]{2,1,0:T(8,128)S(1)}, f32[3,8,128]{2,1,0:T(8,128)S(1)}, u32[]{:S(2)}, u32[]{:S(2)}) collective-permute-start(f32[3,8,128]{2,1,0:T(8,128)S(1)} %pad_maximum_fusion.1), channel_id=1, source_target_pairs={{0,3},{1,0},{2,1},{3,2},{4,7},{5,4},{6,5},{7,6},{8,11},{9,8},{10,9... | collective-permute-start | bytes 36872 | tf_op jit(solution)/shard_map/ppermute | solution.py:23
  108.7 5.9 %collective-permute-start.11 = (f32[8,128]{1,0:T(8,128)S(1)}, f32[8,128]{1,0:T(8,128)S(1)}, u32[]{:S(2)}, u32[]{:S(2)}) collective-permute-start(f32[8,128]{1,0:T(8,128)S(1)} %get-tuple-element.35), channel_id=1, source_target_pairs={{4,0},{5,1},{6,2},{7,3},{8,4},{9,5},{10,6},{11,7},{12,8},{13,9},{1... | collective-permute-start | bytes 12296 | tf_op jit(solution)/shard_map/ppermute | solution.py:23
  110.6 5.5 %collective-permute-start.12 = (f32[8,128]{1,0:T(8,128)S(1)}, f32[8,128]{1,0:T(8,128)S(1)}, u32[]{:S(2)}, u32[]{:S(2)}) collective-permute-start(f32[8,128]{1,0:T(8,128)S(1)} %get-tuple-element.36), channel_id=1, source_target_pairs={{0,4},{1,5},{2,6},{3,7},{4,8},{5,9},{6,10},{7,11},{8,12},{9,13},{1... | collective-permute-start | bytes 12296 | tf_op jit(solution)/shard_map/ppermute | solution.py:23

commit v6 on v5

--- a/solution.py
+++ b/solution.py
@@ -397,20 +397,12 @@
         flags,
         [
             (up, "corner"), (down, "down"), (up_next_even, "up_next"), (down_prev_even, "down_prev"),
-            (up_next_odd, "up_next"), (down_prev_odd, "down_prev"), (corner_odd, "down_prev"),
+            (up_next_odd, "up_next"), (down_prev_odd, "down_prev"), (corner_odd, "late"), (down_prev_even, "early"),
         ],
-        [(2, 3, EVEN_BETWEEN), (1, 3, EVEN_FIRST), (4, 5, ODD_BETWEEN), (0, 6, ODD_LAST)], found,
+        [(2, 3, EVEN_BETWEEN), (1, 7, EVEN_FIRST), (4, 5, ODD_BETWEEN), (0, 6, ODD_LAST)], found,
     )
-    none = jnp.full((blocks, count), LOW, jnp.float32)
-    from_prev = shifted(
-        jnp.stack([found["next"], found["up_next"], jnp.where(late, found["down_prev"], none)]), right
-    )
-    from_next = shifted(
-        jnp.stack([
-            found["prev"], jnp.where(early, found["down_prev"], none),
-            jnp.where(early | late, none, found["down_prev"]),
-        ]), left
-    )
+    from_prev = shifted(jnp.stack([found["next"], found["up_next"], found["late"]]), right)
+    from_next = shifted(jnp.stack([found["prev"], found["early"], found["down_prev"]]), left)
     around = jnp.maximum(from_prev, from_next)
     from_below = shifted(jnp.maximum(jnp.maximum(found["up"], found["corner"]), around[1]), above)
     from_above = shifted(jnp.maximum(found["down"], around[2]), below)

time: 119 us -> 119 us (level)
  the two profiles are of different devices: /device:TPU:32 before, /device:TPU:1 now
where the time goes in v6:
time: 119 us; the launch traced here: 118 us
  waiting for transfers between devices  50.4 us (42%)
  starting transfers between devices  42 us (35%)
  Pallas kernels  22.1 us (19%)
  other arithmetic  3.29 us (3%)
    ppermute x13, waiting for transfers between devices, shifted(): return lax.ppermute(array, AXES, pairs)  50.4 us
    ppermute x13, starting transfers between devices, shifted(): return lax.ppermute(array, AXES, pairs)  42 us
    pallas_call x3, Pallas kernels, compare(): pl.pallas_call(functools.partial(pairs_kernel, [part[1] for part in parts...  13 us
    pallas_call x1, Pallas kernels, own_tile(): pl.pallas_call(own_kernel, out_shape=jax.ShapeDtypeStruct((blocks, count)...  5.91 us
    pallas_call x1, Pallas kernels, normalize(): pl.pallas_call(unit_kernel, out_shape=jax.ShapeDtypeStruct((blocks * coun...  3.03 us
  transfers between devices with their start and end apart: 13, of which 5 were waited for; matrix products, arithmetic and copies ran while one was open for 1% of the time, Pallas kernels for 14%

profile of v6, /device:TPU:1, one launch (start us, length us, event | category | flops | bytes accessed | tf_op | source)
XLA Modules:
  0.0 118.2 jit_solution(8025075113168418476)
XLA Ops:
  0.0 3.0 %shard_map.64.units.refs_1_ = bf16[1040,1024]{1,0:T(8,128)(2,1)} custom-call(s32[8]{0:T(128)} %cluster.1, s32[8]{0:T(128)} %live.1, bf16[8,128,1024]{2,1,0:T(8,128)(2,1)} %embeddings.1), custom_call_target="tpu_custom_call" | custom-call | flops 4194304 | bytes 4194304 | tf_op jit(solution)/shard_map/pallas_call | solution.py:74
  3.0 3.4 %collective-permute-start.1 = (bf16[1040,1024]{1,0:T(8,128)(2,1)}, bf16[1040,1024]{1,0:T(8,128)(2,1)}, u32[]{:S(2)}, u32[]{:S(2)}) collective-permute-start(bf16[1040,1024]{1,0:T(8,128)(2,1)} %shard_map.64.units.refs_1_), channel_id=1, source_target_pairs={{0,3},{1,0},{2,1},{3,2},{4,7},{5,4},{6,5},{7,6},{8,11},{9,8},{10,9... | collective-permute-start | bytes 6389768 | tf_op jit(solution)/shard_map/ppermute | solution.py:23
  6.4 3.5 %collective-permute-start = (bf16[1040,1024]{1,0:T(8,128)(2,1)}, bf16[1040,1024]{1,0:T(8,128)(2,1)S(1)}, u32[]{:S(2)}, u32[]{:S(2)}) collective-permute-start(bf16[1040,1024]{1,0:T(8,128)(2,1)} %shard_map.64.units.refs_1_), channel_id=1, source_target_pairs={{0,4},{1,5},{2,6},{3,7},{4,8},{5,9},{6,10},{7,11},{8,12},{9,13},{1... | collective-permute-start | bytes 6389768 | tf_op jit(solution)/shard_map/ppermute | solution.py:23
  10.0 0.1 collective-permute-start.2
  10.0 4.9 %collective-permute-start.3 = (bf16[1040,1024]{1,0:T(8,128)(2,1)}, bf16[1040,1024]{1,0:T(8,128)(2,1)}, u32[]{:S(2)}, u32[]{:S(2)}) collective-permute-start(bf16[1040,1024]{1,0:T(8,128)(2,1)} %shard_map.64.units.refs_1_), channel_id=1, source_target_pairs={{4,0},{5,1},{6,2},{7,3},{8,4},{9,5},{10,6},{11,7},{12,8},{13,9},{1... | collective-permute-start | bytes 6389768 | tf_op jit(solution)/shard_map/ppermute | solution.py:23
  14.9 5.9 %shard_map.65 = f32[8,128]{1,0:T(8,128)} custom-call(s32[8]{0:T(128)} %cluster.1, s32[8]{0:T(128)} %live.1, bf16[1040,1024]{1,0:T(8,128)(2,1)} %shard_map.64.units.refs_1_), custom_call_target="tpu_custom_call" | custom-call | flops 2147483648 | bytes 2097152 | tf_op jit(solution)/shard_map/pallas_call | solution.py:121
  20.8 30.9 %collective-permute-done.1.refs_0_ = bf16[1040,1024]{1,0:T(8,128)(2,1)} collective-permute-done((bf16[1040,1024]{1,0:T(8,128)(2,1)}, bf16[1040,1024]{1,0:T(8,128)(2,1)}, u32[]{:S(2)}, u32[]{:S(2)}) %collective-permute-start.1) | collective-permute-done | bytes 2129952 | tf_op jit(solution)/shard_map/ppermute | solution.py:23
  51.7 3.5 %collective-permute-start.6 = (bf16[1040,1024]{1,0:T(8,128)(2,1)}, bf16[1040,1024]{1,0:T(8,128)(2,1)}, u32[]{:S(2)}, u32[]{:S(2)}) collective-permute-start(bf16[1040,1024]{1,0:T(8,128)(2,1)} %collective-permute-done.1.refs_0_), channel_id=1, source_target_pairs={{12,16},{13,17},{14,18},{15,19},{16,20},{17,21},{18,22},{19,23},{2... | collective-permute-start | bytes 6389768 | tf_op jit(solution)/shard_map/ppermute | solution.py:23
  55.3 0.0 collective-permute-done.refs_3_.up.refs_0_
  55.3 0.0 copy-start
  55.3 2.0 %collective-permute-start.4 = (bf16[1040,1024]{1,0:T(8,128)(2,1)S(1)}, bf16[1040,1024]{1,0:T(8,128)(2,1)}, u32[]{:S(2)}, u32[]{:S(2)}) collective-permute-start(bf16[1040,1024]{1,0:T(8,128)(2,1)S(1)} %collective-permute-done.refs_3_.up.refs_0_), channel_id=1, source_target_pairs={{0,3},{1,0},{2,1},{3,2},{4,7},{5,4},{6,5},{7,6},{8,11},{9,8},{10,9... | collective-permute-start | bytes 6389768 | tf_op jit(solution)/shard_map/ppermute | solution.py:23
  57.3 2.0 %collective-permute-start.8 = (bf16[1040,1024]{1,0:T(8,128)(2,1)}, bf16[1040,1024]{1,0:T(8,128)(2,1)}, u32[]{:S(2)}, u32[]{:S(2)}) collective-permute-start(bf16[1040,1024]{1,0:T(8,128)(2,1)} %collective-permute-done.1.refs_0_), channel_id=1, source_target_pairs={{23,19},{27,23},{31,27},{35,31},{55,51},{59,55},{63,59},{67,63},{8... | collective-permute-start | bytes 6389768 | tf_op jit(solution)/shard_map/ppermute | solution.py:23
  59.3 0.0 collective-permute-done.2.refs_2_.refs_0_
  59.3 2.1 %collective-permute-start.7 = (bf16[1040,1024]{1,0:T(8,128)(2,1)}, bf16[1040,1024]{1,0:T(8,128)(2,1)}, u32[]{:S(2)}, u32[]{:S(2)}) collective-permute-start(bf16[1040,1024]{1,0:T(8,128)(2,1)} %collective-permute-done.2.refs_2_.refs_0_), channel_id=1, source_target_pairs={{21,17},{22,18},{25,21},{26,22},{29,25},{30,26},{33,29},{34,30},{5... | collective-permute-start | bytes 6389768 | tf_op jit(solution)/shard_map/ppermute | solution.py:23
  61.4 0.0 collective-permute-done.3.down
  61.4 0.0 copy-done
  61.4 0.2 shard_map.67.refs_1_
  61.5 2.0 %collective-permute-start.5 = (bf16[1040,1024]{1,0:T(8,128)(2,1)}, bf16[1040,1024]{1,0:T(8,128)(2,1)}, u32[]{:S(2)}, u32[]{:S(2)}) collective-permute-start(bf16[1040,1024]{1,0:T(8,128)(2,1)} %shard_map.67.refs_1_), channel_id=1, source_target_pairs={{0,1},{1,2},{3,0},{4,5},{5,6},{7,4},{8,9},{9,10},{11,8},{12,13},{1... | collective-permute-start | bytes 6389768 | tf_op jit(solution)/shard_map/ppermute | solution.py:23
  63.6 0.1 stack.67
  63.7 0.6 convert_element_type.4.flags
  64.3 7.1 %shard_map.66 = (f32[8,128]{1,0:T(8,128)}, f32[8,128]{1,0:T(8,128)}, f32[8,128]{1,0:T(8,128)}, f32[8,128]{1,0:T(8,128)}) custom-call(s32[25]{0:T(128)} %constant.65.clone.jobs, s32[10]{0:T(128)} %convert_element_type.4.flags, bf16[1040,1024]{1,0:T(8,128)(2,1)} %collective-permute-done.1.refs_0_, bf16[1040,1024]{1,0:T(8,128)(2,1)} %shard_map.64.units.refs_1_, ...), custom_call_target="tpu_custom_call" | custom-call | flops 10737418240 | bytes 8519680 | tf_op jit(solution)/shard_map/pallas_call | solution.py:275
  71.3 11.5 %collective-permute-done.6.refs_3_.refs_4_ = bf16[1040,1024]{1,0:T(8,128)(2,1)} collective-permute-done((bf16[1040,1024]{1,0:T(8,128)(2,1)}, bf16[1040,1024]{1,0:T(8,128)(2,1)}, u32[]{:S(2)}, u32[]{:S(2)}) %collective-permute-start.6) | collective-permute-done | bytes 2129952 | tf_op jit(solution)/shard_map/ppermute | solution.py:23
  82.9 0.0 collective-permute-done.4.refs_2_
  82.9 2.9 %shard_map.68 = (f32[8,128]{1,0:T(8,128)}, f32[8,128]{1,0:T(8,128)}, f32[8,128]{1,0:T(8,128)}) custom-call(s32[20]{0:T(128)} %constant.66.clone.jobs, s32[10]{0:T(128)} %convert_element_type.4.flags, bf16[1040,1024]{1,0:T(8,128)(2,1)} %collective-permute-done.2.refs_2_.refs_0_, bf16[1040,1024]{1,0:T(8,128)(2,1)} %shard_map.67.refs_1_, ...), custom_call_target="tpu_custom_call" | custom-call | flops 8589934592 | bytes 8519680 | tf_op jit(solution)/shard_map/pallas_call | solution.py:275
  85.7 0.0 collective-permute-done.7.refs_5_
  85.7 0.0 collective-permute-done.8.refs_6_
  85.7 0.0 collective-permute-done.5.refs_3_.refs_7_
  85.8 0.0 copy-start.5
  85.8 0.0 copy-start.4
  85.8 0.0 copy-start.3
  85.8 0.0 copy-start.1
  85.8 0.0 copy-start.2
  85.8 0.0 copy-start.6
  85.8 3.1 %shard_map.69 = (f32[8,128]{1,0:T(8,128)}, f32[8,128]{1,0:T(8,128)}, f32[8,128]{1,0:T(8,128)}, f32[8,128]{1,0:T(8,128)}, f32[8,128]{1,0:T(8,128)}, /*index=5*/f32[8,128]{1,0:T(8,128)}) custom-call(s32[20]{0:T(128)} %constant.67.clone.jobs, s32[10]{0:T(128)} %convert_element_type.4.flags, bf16[1040,1024]{1,0:T(8,128)(2,1)} %copy-done, ...), custom_call_target="tpu_custom_call" | custom-call | flops 8589934592 | bytes 17039360 | tf_op jit(solution)/shard_map/pallas_call | solution.py:275
  89.0 0.0 copy-done.5
  89.0 0.7 pad_maximum_fusion.1
  89.7 3.4 %collective-permute-start.10 = (f32[3,8,128]{2,1,0:T(8,128)S(1)}, f32[3,8,128]{2,1,0:T(8,128)S(1)}, u32[]{:S(2)}, u32[]{:S(2)}) collective-permute-start(f32[3,8,128]{2,1,0:T(8,128)S(1)} %pad_maximum_fusion.1), channel_id=1, source_target_pairs={{0,3},{1,0},{2,1},{3,2},{4,7},{5,4},{6,5},{7,6},{8,11},{9,8},{10,9... | collective-permute-start | bytes 36872 | tf_op jit(solution)/shard_map/ppermute | solution.py:23
  93.1 0.0 copy-done.4
  93.1 0.7 pad_maximum_fusion
  93.8 0.0 collective-permute-start.9
  93.8 0.1 collective-permute-done.10
  93.9 3.6 %collective-permute-done.9 = f32[3,8,128]{2,1,0:T(8,128)S(1)} collective-permute-done((f32[3,8,128]{2,1,0:T(8,128)S(1)}, f32[3,8,128]{2,1,0:T(8,128)S(1)}, u32[]{:S(2)}, u32[]{:S(2)}) %collective-permute-start.9) | collective-permute-done | bytes 12320 | tf_op jit(solution)/shard_map/ppermute | solution.py:23
  97.5 0.7 fusion.1
  98.2 13.1 %collective-permute-start.11 = (f32[8,128]{1,0:T(8,128)S(1)}, f32[8,128]{1,0:T(8,128)S(1)}, u32[]{:S(2)}, u32[]{:S(2)}) collective-permute-start(f32[8,128]{1,0:T(8,128)S(1)} %get-tuple-element.39), channel_id=1, source_target_pairs={{4,0},{5,1},{6,2},{7,3},{8,4},{9,5},{10,6},{11,7},{12,8},{13,9},{1... | collective-permute-start | bytes 12296 | tf_op jit(solution)/shard_map/ppermute | solution.py:23
  111.3 1.9 %collective-permute-start.12 = (f32[8,128]{1,0:T(8,128)S(1)}, f32[8,128]{1,0:T(8,128)S(1)}, u32[]{:S(2)}, u32[]{:S(2)}) collective-permute-start(f32[8,128]{1,0:T(8,128)S(1)} %get-tuple-element.40), channel_id=1, source_target_pairs={{0,4},{1,5},{2,6},{3,7},{4,8},{5,9},{6,10},{7,11},{8,12},{9,13},{1... | collective-permute-start | bytes 12296 | tf_op jit(solution)/shard_map/ppermute | solution.py:23
  113.3 0.0 collective-permute-done.11
  113.3 4.2 %collective-permute-done.12 = f32[8,128]{1,0:T(8,128)S(1)} collective-permute-done((f32[8,128]{1,0:T(8,128)S(1)}, f32[8,128]{1,0:T(8,128)S(1)}, u32[]{:S(2)}, u32[]{:S(2)}) %collective-permute-start.12) | collective-permute-done | bytes 4128 | tf_op jit(solution)/shard_map/ppermute | solution.py:23
  117.5 0.7 fusion.8
  (5 shorter events, 0.0 us)
Async XLA Ops:
  3.0 48.7 %collective-permute-start.1 = (bf16[1040,1024]{1,0:T(8,128)(2,1)}, bf16[1040,1024]{1,0:T(8,128)(2,1)}, u32[]{:S(2)}, u32[]{:S(2)}) collective-permute-start(bf16[1040,1024]{1,0:T(8,128)(2,1)} %shard_map.64.units.refs_1_), channel_id=1, source_target_pairs={{0,3},{1,0},{2,1},{3,2},{4,7},{5,4},{6,5},{7,6},{8,11},{9,8},{10,9... | collective-permute-start | bytes 6389768 | tf_op jit(solution)/shard_map/ppermute | solution.py:23
  6.4 48.9 %collective-permute-start = (bf16[1040,1024]{1,0:T(8,128)(2,1)}, bf16[1040,1024]{1,0:T(8,128)(2,1)S(1)}, u32[]{:S(2)}, u32[]{:S(2)}) collective-permute-start(bf16[1040,1024]{1,0:T(8,128)(2,1)} %shard_map.64.units.refs_1_), channel_id=1, source_target_pairs={{0,4},{1,5},{2,6},{3,7},{4,8},{5,9},{6,10},{7,11},{8,12},{9,13},{1... | collective-permute-start | bytes 6389768 | tf_op jit(solution)/shard_map/ppermute | solution.py:23
  10.0 49.3 %collective-permute-start.2 = (bf16[1040,1024]{1,0:T(8,128)(2,1)}, bf16[1040,1024]{1,0:T(8,128)(2,1)}, u32[]{:S(2)}, u32[]{:S(2)}) collective-permute-start(bf16[1040,1024]{1,0:T(8,128)(2,1)} %shard_map.64.units.refs_1_), channel_id=1, source_target_pairs={{0,1},{1,2},{2,3},{3,0},{4,5},{5,6},{6,7},{7,4},{8,9},{9,10},{10,1... | collective-permute-start | bytes 6389768 | tf_op jit(solution)/shard_map/ppermute | solution.py:23
  10.0 51.3 %collective-permute-start.3 = (bf16[1040,1024]{1,0:T(8,128)(2,1)}, bf16[1040,1024]{1,0:T(8,128)(2,1)}, u32[]{:S(2)}, u32[]{:S(2)}) collective-permute-start(bf16[1040,1024]{1,0:T(8,128)(2,1)} %shard_map.64.units.refs_1_), channel_id=1, source_target_pairs={{4,0},{5,1},{6,2},{7,3},{8,4},{9,5},{10,6},{11,7},{12,8},{13,9},{1... | collective-permute-start | bytes 6389768 | tf_op jit(solution)/shard_map/ppermute | solution.py:23
  51.7 31.1 %collective-permute-start.6 = (bf16[1040,1024]{1,0:T(8,128)(2,1)}, bf16[1040,1024]{1,0:T(8,128)(2,1)}, u32[]{:S(2)}, u32[]{:S(2)}) collective-permute-start(bf16[1040,1024]{1,0:T(8,128)(2,1)} %collective-permute-done.1.refs_0_), channel_id=1, source_target_pairs={{12,16},{13,17},{14,18},{15,19},{16,20},{17,21},{18,22},{19,23},{2... | collective-permute-start | bytes 6389768 | tf_op jit(solution)/shard_map/ppermute | solution.py:23
  55.3 6.1 %copy-start = (bf16[1040,1024]{1,0:T(8,128)(2,1)}, bf16[1040,1024]{1,0:T(8,128)(2,1)S(1)}, u32[]{:S(2)}) copy-start(bf16[1040,1024]{1,0:T(8,128)(2,1)S(1)} %collective-permute-done.refs_3_.up.refs_0_) | copy-start | bytes 6389764
  55.3 27.6 %collective-permute-start.4 = (bf16[1040,1024]{1,0:T(8,128)(2,1)S(1)}, bf16[1040,1024]{1,0:T(8,128)(2,1)}, u32[]{:S(2)}, u32[]{:S(2)}) collective-permute-start(bf16[1040,1024]{1,0:T(8,128)(2,1)S(1)} %collective-permute-done.refs_3_.up.refs_0_), channel_id=1, source_target_pairs={{0,3},{1,0},{2,1},{3,2},{4,7},{5,4},{6,5},{7,6},{8,11},{9,8},{10,9... | collective-permute-start | bytes 6389768 | tf_op jit(solution)/shard_map/ppermute | solution.py:23
  57.3 28.5 %collective-permute-start.8 = (bf16[1040,1024]{1,0:T(8,128)(2,1)}, bf16[1040,1024]{1,0:T(8,128)(2,1)}, u32[]{:S(2)}, u32[]{:S(2)}) collective-permute-start(bf16[1040,1024]{1,0:T(8,128)(2,1)} %collective-permute-done.1.refs_0_), channel_id=1, source_target_pairs={{23,19},{27,23},{31,27},{35,31},{55,51},{59,55},{63,59},{67,63},{8... | collective-permute-start | bytes 6389768 | tf_op jit(solution)/shard_map/ppermute | solution.py:23
  59.3 26.4 %collective-permute-start.7 = (bf16[1040,1024]{1,0:T(8,128)(2,1)}, bf16[1040,1024]{1,0:T(8,128)(2,1)}, u32[]{:S(2)}, u32[]{:S(2)}) collective-permute-start(bf16[1040,1024]{1,0:T(8,128)(2,1)} %collective-permute-done.2.refs_2_.refs_0_), channel_id=1, source_target_pairs={{21,17},{22,18},{25,21},{26,22},{29,25},{30,26},{33,29},{34,30},{5... | collective-permute-start | bytes 6389768 | tf_op jit(solution)/shard_map/ppermute | solution.py:23
  61.5 24.2 %collective-permute-start.5 = (bf16[1040,1024]{1,0:T(8,128)(2,1)}, bf16[1040,1024]{1,0:T(8,128)(2,1)}, u32[]{:S(2)}, u32[]{:S(2)}) collective-permute-start(bf16[1040,1024]{1,0:T(8,128)(2,1)} %shard_map.67.refs_1_), channel_id=1, source_target_pairs={{0,1},{1,2},{3,0},{4,5},{5,6},{7,4},{8,9},{9,10},{11,8},{12,13},{1... | collective-permute-start | bytes 6389768 | tf_op jit(solution)/shard_map/ppermute | solution.py:23
  85.8 3.2 %copy-start.5 = (f32[8,128]{1,0:T(8,128)S(1)}, f32[8,128]{1,0:T(8,128)}, u32[]{:S(2)}) copy-start(f32[8,128]{1,0:T(8,128)} %get-tuple-element.33) | copy-start | bytes 12292
  85.8 7.3 %copy-start.4 = (f32[8,128]{1,0:T(8,128)S(1)}, f32[8,128]{1,0:T(8,128)}, u32[]{:S(2)}) copy-start(f32[8,128]{1,0:T(8,128)} %get-tuple-element.27) | copy-start | bytes 12292
  85.8 11.7 %copy-start.3 = (f32[8,128]{1,0:T(8,128)S(1)}, f32[8,128]{1,0:T(8,128)}, u32[]{:S(2)}) copy-start(f32[8,128]{1,0:T(8,128)} %get-tuple-element.36) | copy-start | bytes 12292
  85.8 31.7 %copy-start.1 = (f32[8,128]{1,0:T(8,128)S(1)}, f32[8,128]{1,0:T(8,128)}, u32[]{:S(2)}) copy-start(f32[8,128]{1,0:T(8,128)} %shard_map.65) | copy-start | bytes 12292
  85.8 31.7 %copy-start.2 = (f32[8,128]{1,0:T(8,128)S(1)}, f32[8,128]{1,0:T(8,128)}, u32[]{:S(2)}) copy-start(f32[8,128]{1,0:T(8,128)} %get-tuple-element.26) | copy-start | bytes 12292
  85.8 31.7 %copy-start.6 = (s32[8]{0:T(128)S(1)}, s32[8]{0:T(128)}, u32[]{:S(2)}) copy-start(s32[8]{0:T(128)} %live.1) | copy-start | bytes 100
  89.7 4.2 %collective-permute-start.10 = (f32[3,8,128]{2,1,0:T(8,128)S(1)}, f32[3,8,128]{2,1,0:T(8,128)S(1)}, u32[]{:S(2)}, u32[]{:S(2)}) collective-permute-start(f32[3,8,128]{2,1,0:T(8,128)S(1)} %pad_maximum_fusion.1), channel_id=1, source_target_pairs={{0,3},{1,0},{2,1},{3,2},{4,7},{5,4},{6,5},{7,6},{8,11},{9,8},{10,9... | collective-permute-start | bytes 36872 | tf_op jit(solution)/shard_map/ppermute | solution.py:23
  93.8 3.8 %collective-permute-start.9 = (f32[3,8,128]{2,1,0:T(8,128)S(1)}, f32[3,8,128]{2,1,0:T(8,128)S(1)}, u32[]{:S(2)}, u32[]{:S(2)}) collective-permute-start(f32[3,8,128]{2,1,0:T(8,128)S(1)} %pad_maximum_fusion), channel_id=1, source_target_pairs={{0,1},{1,2},{2,3},{3,0},{4,5},{5,6},{6,7},{7,4},{8,9},{9,10},{10,1... | collective-permute-start | bytes 36872 | tf_op jit(solution)/shard_map/ppermute | solution.py:23
  98.2 15.1 %collective-permute-start.11 = (f32[8,128]{1,0:T(8,128)S(1)}, f32[8,128]{1,0:T(8,128)S(1)}, u32[]{:S(2)}, u32[]{:S(2)}) collective-permute-start(f32[8,128]{1,0:T(8,128)S(1)} %get-tuple-element.39), channel_id=1, source_target_pairs={{4,0},{5,1},{6,2},{7,3},{8,4},{9,5},{10,6},{11,7},{12,8},{13,9},{1... | collective-permute-start | bytes 12296 | tf_op jit(solution)/shard_map/ppermute | solution.py:23
  111.3 6.1 %collective-permute-start.12 = (f32[8,128]{1,0:T(8,128)S(1)}, f32[8,128]{1,0:T(8,128)S(1)}, u32[]{:S(2)}, u32[]{:S(2)}) collective-permute-start(f32[8,128]{1,0:T(8,128)S(1)} %get-tuple-element.40), channel_id=1, source_target_pairs={{0,4},{1,5},{2,6},{3,7},{4,8},{5,9},{6,10},{7,11},{8,12},{9,13},{1... | collective-permute-start | bytes 12296 | tf_op jit(solution)/shard_map/ppermute | solution.py:23
